TPU v7x, 32 devices: a whole 2x2x4 slice. The times are simulated.
32 devices in a mesh: lat: 4 (over x, core), lev: 4 (over z), lon: 2 (over y).
Axes of the slice: x: 2, y: 2, z: 4, core: 2. Of those that a mesh axis runs over, the one named last changes fastest.
Arguments:
- adjoint: float32 [4, 136, 16, 512], P(None, 'lev', 'lat', 'lon'), may hold values from -6 to 6
- wind_east: float32 [136, 16, 512], P('lev', 'lat', 'lon'), may hold values from -0.48 to 0.48
- wind_north: float32 [136, 16, 512], P('lev', 'lat', 'lon'), may hold values from -0.48 to 0.48
- kz_inverse: float32 [4, 136, 136], replicated, may hold values from 0 to 1.2
- kz_regime: int32 [2, 16, 512], P(None, 'lat', 'lon'), may hold values from 0 to 3
- fp_cell: int32 [16, 2, 512], P(('lat', 'lev'), 'lon'), may hold values from 0 to 2047
- fp_owner: int32 [16, 2, 512, 1], P(('lat', 'lev'), 'lon'), may hold values from 0 to 15; in each aligned block of 512 rows (0 to 511, 512 to 1023, ..., all dimensions but the last counted through in order) at most 64 rows name the same one
- fp_station: int32 [16, 2, 512], P(('lat', 'lev'), 'lon'), may hold values from 0 to 3
- fp_weight: float32 [16, 2, 512], P(('lat', 'lev'), 'lon'), may hold values from 0.02 to 0.2
Outputs:
- final_adjoint: float32 [4, 136, 16, 512], P(None, 'lev', 'lat', 'lon')
- station_sens: float32 [2, 4, 2, 64], P(None, None, 'lon', ('lat', 'lev'))
Inputs may be any that keep to these rules, and one draw needn't show every extreme that they name: `fp_owner`: among the rows of one device no region is named by more than 64 entries, a bound that some block reaches.
All inputs are finite; a program needn't handle non-finite values.
Results may differ from a plain program's by a relative error of at most 0.00014.
Values sent between devices are 32-bit elements; how exact they have to be, the bound alone decides.
No kernel may reach another device: no remote copies, remote signals or barrier semaphores. Data moves between devices by JAX's collectives and lax.ppermute only.
A program may use at most 64 MiB of HBM per device.

v0:
```python
import functools
import jax
import jax.numpy as jnp
from jax import lax
from jax.experimental import pallas as pl
from jax.experimental.pallas import tpu as pltpu
from jax.sharding import PartitionSpec as P

NSUB = 4
HOURS = 2
REGIMES = 4
FOOT_LEVELS = 8
SPO = 4
LANES = 128
GRAIN = 16
F32 = jnp.float32
BF16 = jnp.bfloat16
AXES = ("lat", "lev")
RING = ("lat", "lev", "lon")


def chunk_owner(n_lat, n_lev):
    place = [0] * (n_lat * n_lev)
    for a in range(n_lat):
        for z in range(n_lev):
            chip, core = divmod(a, 2)
            step = z if chip % 2 == 0 else n_lev - 1 - z
            place[(chip * n_lev + step) * 2 + core] = a * n_lev + z
    return place


def ring_perm(n_lat, n_lev, n_lon, shift):
    place = chunk_owner(n_lat, n_lev)
    ring = [place[d] * n_lon + o for o in range(n_lon) for d in range(len(place))]
    count = len(ring)
    return [(ring[i], ring[(i + shift) % count]) for i in range(count)]


def lane_ids(rows):
    return lax.broadcasted_iota(jnp.int32, (rows, LANES), 1)


def swap_grains(blocks):
    blocks = list(blocks)
    grain = lane_ids(blocks[0].shape[0]) // GRAIN
    bit = len(blocks) // 2
    while bit:
        low = (grain & bit) == 0
        for i in range(len(blocks)):
            if i & bit == 0:
                a, b = blocks[i], blocks[i | bit]
                blocks[i] = jnp.where(low, a, pltpu.roll(b, bit * GRAIN, 1))
                blocks[i | bit] = jnp.where(low, pltpu.roll(a, LANES - bit * GRAIN, 1), b)
        bit //= 2
    return blocks


def swap_halves(a, b):
    low = lane_ids(a.shape[0]) < LANES // 2
    return (
        jnp.where(low, a, pltpu.roll(b, LANES // 2, 1)),
        jnp.where(low, pltpu.roll(a, LANES // 2, 1), b),
    )


def transpose_matrix():
    i = lax.broadcasted_iota(jnp.int32, (256, 256), 0)
    j = lax.broadcasted_iota(jnp.int32, (256, 256), 1)
    return ((i // 16 == j % 16) & (i % 16 == j // 16)).astype(F32).astype(BF16)


def split_two(x):
    high = x.astype(BF16)
    return high, (x - high.astype(F32)).astype(BF16)


def split_three(x):
    high, _ = split_two(x)
    rest = x - high.astype(F32)
    middle = rest.astype(BF16)
    return high, middle, (rest - middle.astype(F32)).astype(BF16)


def mm(a, b):
    return jnp.dot(a, b, preferred_element_type=F32)


def move_lanes(x, matrix):
    high, middle, low = split_three(x)
    return (mm(high, matrix) + mm(middle, matrix)) + mm(low, matrix)


def pack_kernel(place, adj, east, north, regime, cell, owner, station, weight, out):
    levels = adj.shape[1]
    rows = adj.shape[2]
    for pair in range(3):
        if pair < 2:
            srcs = [adj[2 * pair + k, :, r, :] for k in range(2) for r in range(rows)]
        else:
            srcs = [w[:, r, :] for w in (east, north) for r in range(rows)]
        for half in range(2):
            lanes = slice(half * LANES, (half + 1) * LANES)
            for j, piece in enumerate(swap_grains([s[:, lanes] for s in srcs])):
                out[place[half * 8 + j], pair * levels : (pair + 1) * levels, :] = piece
    first = 3 * levels
    srcs = [regime[h, r : r + 1, :].astype(F32) for h in range(HOURS) for r in range(rows)]
    cells = cell[0]
    level, lon = cells // 256, cells % 256
    stations = (owner[...] * SPO + station[0]).astype(F32)
    weights = weight[0]
    for half in range(2):
        lanes = slice(half * LANES, (half + 1) * LANES)
        for j, piece in enumerate(swap_grains([s[:, lanes] for s in srcs])):
            d = half * 8 + j
            g = place[d]
            out[g, first : first + 1, :] = piece
            here = lon - d * GRAIN
            code = jnp.where((here >= 0) & (here < GRAIN), here * FOOT_LEVELS + level, -1).astype(F32)
            for k in range(4):
                part = slice(k * LANES, (k + 1) * LANES)
                out[g, first + 2 + k : first + 3 + k, :] = code[:, part]
                out[g, first + 6 + k : first + 7 + k, :] = stations[:, part]
                out[g, first + 10 + k : first + 11 + k, :] = weights[:, part]


def solve_columns(high, low, kz_high, kz_low, regime, levels):
    product = mm(kz_high, high) + (mm(kz_low, high) + mm(kz_high, low))
    result = product[:levels]
    for k in range(1, REGIMES):
        result = jnp.where(regime == float(k), product[k * levels : (k + 1) * levels], result)
    return result


def mixing(kz):
    stacked = jnp.concatenate([kz[k].T for k in range(REGIMES)], axis=0)
    return split_two(stacked)


def rim_messages(top, bottom, first, last, rows):
    half = LANES // 2
    low = lane_ids(top.shape[0]) < half
    first[rows, :] = jnp.where(low, top[:, :LANES], pltpu.roll(bottom[:, :LANES], half, 1))
    last[rows, :] = jnp.where(low, pltpu.roll(top[:, LANES:], half, 1), bottom[:, LANES:])


def unpack_solve_kernel(n_lev, recv, kz, solved, winds, regimes, first, last, field):
    per = recv.shape[0] // n_lev
    total = kz.shape[1]
    levels = total // n_lev
    for pair in range(3):
        for z in range(n_lev):
            for half in range(2):
                lanes = slice(half * LANES, (half + 1) * LANES)
                a, b = [
                    recv[(2 * half + k) * n_lev + z, pair * levels : (pair + 1) * levels, :]
                    for k in range(2)
                ]
                for k, value in enumerate(swap_halves(a, b)):
                    base = (2 * pair + k) * total + z * levels
                    field[base : base + levels, lanes] = value
    base = 6 * total
    field[base : base + 8, :] = jnp.zeros((8, 256), F32)
    for half in range(2):
        lanes = slice(half * LANES, (half + 1) * LANES)
        a, b = [
            recv[(2 * half + k) * n_lev, 3 * levels : 3 * levels + 1, :] for k in range(2)
        ]
        for k, value in enumerate(swap_halves(a, b)):
            field[base + k : base + k + 1, lanes] = value
    matrix = transpose_matrix()
    regime = mm(field[base : base + 8, :].astype(BF16), matrix)
    regimes[...] = regime
    kz_high, kz_low = mixing(kz)
    for k in range(2):
        winds[k * total : (k + 1) * total, :] = move_lanes(
            field[(4 + k) * total : (5 + k) * total, :], matrix
        )
    for t in range(4):
        high, low = split_two(field[t * total : (t + 1) * total, :])
        high = mm(high, matrix).astype(BF16)
        low = mm(low, matrix).astype(BF16)
        solved[t * total : (t + 1) * total, :] = solve_columns(
            high, low, kz_high, kz_low, regime[0:1], total
        )
    rim_messages(
        solved[0 : 2 * total, :], solved[2 * total :, :], first, last, slice(0, 2 * total)
    )
    rim_messages(
        winds[0:total, :], winds[total:, :], first, last, slice(2 * total, 3 * total)
    )


def with_rims(main, from_east, from_west, upper):
    half = LANES // 2
    low = lane_ids(main.shape[0]) < half
    if upper:
        rim = jnp.where(low, pltpu.roll(from_east, half, 1), from_west)
    else:
        rim = jnp.where(low, from_east, pltpu.roll(from_west, half, 1))
    return jnp.concatenate([main, rim], axis=1)


def face_weights(lat_count, winds, from_east, from_west, total, faces):
    width = 384
    rims = slice(2 * total, 3 * total)
    east = with_rims(winds[0:total, :], from_east[rims, :], from_west[rims, :], False)
    north = with_rims(winds[total:, :], from_east[rims, :], from_west[rims, :], True)
    lat = lax.broadcasted_iota(jnp.int32, (total, width), 1) % lat_count
    north = jnp.where(lat == lat_count - 1, 0.0, north)
    south = pltpu.roll(north, 1, 1)
    west = pltpu.roll(east, lat_count, 1)
    faces[0] = jnp.maximum(north, 0.0)
    faces[1] = -jnp.minimum(south, 0.0)
    faces[2] = jnp.maximum(east, 0.0)
    faces[3] = -jnp.minimum(west, 0.0)


def transport(lat_count, field, east_rows, west_rows, faces, total, result):
    width = 384
    block = 8

    @pl.loop(0, total // block)
    def _(step):
        rows = pl.ds(pl.multiple_of(step * block, block), block)
        up, down, right, left = [faces[k, rows, :] for k in range(4)]
        for t in range(4):
            own = pl.ds(pl.multiple_of(t * total + step * block, block), block)
            rim = pl.ds(pl.multiple_of((t % 2) * total + step * block, block), block)
            f = with_rims(field[own, :], east_rows[rim, :], west_rows[rim, :], t >= 2)
            for _ in range(NSUB):
                f = (
                    f
                    + up * (pltpu.roll(f, width - 1, 1) - f)
                    + down * (pltpu.roll(f, 1, 1) - f)
                )
                f = (
                    f
                    + right * (pltpu.roll(f, width - lat_count, 1) - f)
                    + left * (pltpu.roll(f, lat_count, 1) - f)
                )
            result[own, :] = f[:, :256]


def transport_solve_kernel(
    lat_count, field, winds, regimes, kz, from_east, from_west, solved, first, last, faces, moved
):
    total = kz.shape[1]
    face_weights(lat_count, winds, from_east, from_west, total, faces)
    transport(lat_count, field, from_east, from_west, faces, total, moved)
    kz_high, kz_low = mixing(kz)
    for t in range(4):
        high, low = split_two(moved[t * total : (t + 1) * total, :])
        solved[t * total : (t + 1) * total, :] = solve_columns(
            high, low, kz_high, kz_low, regimes[1:2, :], total
        )
    rim_messages(
        solved[0 : 2 * total, :], solved[2 * total :, :], first, last, slice(0, 2 * total)
    )


def footprint_kernel(entry_row, recv, hour_0, hour_1, sums):
    total = hour_0.shape[0] // 4
    matrix = transpose_matrix()
    low = jnp.concatenate(
        [h[t * total : t * total + FOOT_LEVELS, :] for h in (hour_0, hour_1) for t in range(4)],
        axis=0,
    )
    parts = mm(jnp.concatenate(split_three(low), axis=0), matrix).astype(BF16)
    count = low.shape[0]
    acc = jnp.zeros((count, 64), F32)
    cell_ids = lax.broadcasted_iota(jnp.int32, (GRAIN, 512), 0)
    level_ids = lax.broadcasted_iota(jnp.int32, (FOOT_LEVELS, 512), 0)
    station_ids = lax.broadcasted_iota(jnp.int32, (64, 512), 0)
    for row in range(recv.shape[0]):
        def entries(at):
            return jnp.concatenate(
                [recv[row, at + k : at + k + 1, :] for k in range(4)], axis=1
            )

        code = entries(entry_row).astype(jnp.int32)
        station = entries(entry_row + 4).astype(jnp.int32)
        weight = entries(entry_row + 8)
        cells = ((code >> 3) == cell_ids).astype(F32).astype(BF16)
        picked = mm(parts[:, row * GRAIN : (row + 1) * GRAIN], cells)
        picked = (picked[:count] + picked[count : 2 * count]) + picked[2 * count :]
        level = jnp.where((code & 7) == level_ids, weight, 0.0)
        picked = picked * jnp.concatenate([level] * (count // FOOT_LEVELS), axis=0)
        named = (station == station_ids).astype(F32).astype(BF16)
        high, rest = split_two(picked)
        both = jnp.concatenate([high, rest], axis=0)
        both = lax.dot_general(both, named, (((1,), (1,)), ((), ())), preferred_element_type=F32)
        acc = acc + (both[:count] + both[count:])
    sums[...] = jnp.sum(acc.reshape(count // FOOT_LEVELS, FOOT_LEVELS, 64), axis=1)


def transport_pack_kernel(
    lat_count, n_lev, field, winds, from_east_0, from_west_0, from_east, from_west, sums, out,
    faces, moved,
):
    total = winds.shape[0] // 2
    levels = total // n_lev
    face_weights(lat_count, winds, from_east_0, from_west_0, total, faces)
    transport(lat_count, field, from_east, from_west, faces, total, moved)
    matrix = transpose_matrix()
    for pair in range(2):
        for k in range(2):
            rows = slice((2 * pair + k) * total, (2 * pair + k + 1) * total)
            moved[rows, :] = move_lanes(moved[rows, :], matrix)
        for z in range(n_lev):
            for half in range(2):
                lanes = slice(half * LANES, (half + 1) * LANES)
                a, b = [
                    moved[
                        (2 * pair + k) * total + z * levels : (2 * pair + k) * total
                        + (z + 1) * levels,
                        lanes,
                    ]
                    for k in range(2)
                ]
                for k, value in enumerate(swap_halves(a, b)):
                    out[
                        (2 * half + k) * n_lev + z, pair * levels : (pair + 1) * levels, :
                    ] = value
    wide = jnp.concatenate([sums[...], jnp.zeros((8, 64), F32)], axis=1)
    line = lax.broadcasted_iota(jnp.int32, (8, LANES), 0)
    spread = jnp.zeros((8, LANES), F32)
    for k in range(8):
        spread = jnp.where(line == k, pltpu.roll(wide, 4 * k, 1) if k else wide, spread)
    keep = lax.broadcasted_iota(jnp.int32, (8, LANES), 1) // 4 == line
    for g in range(out.shape[0]):
        value = pltpu.roll(spread, LANES - 4 * g, 1) if g else spread
        value = jnp.sum(jnp.where(keep, value, 0.0), axis=0, keepdims=True)
        out[g, 2 * levels : 2 * levels + 1, :] = value


def unpack_kernel(place, recv, final, stations):
    levels = final.shape[1]
    for pair in range(2):
        for half in range(2):
            lanes = slice(half * LANES, (half + 1) * LANES)
            blocks = [
                recv[place[half * 8 + j], pair * levels : (pair + 1) * levels, :]
                for j in range(8)
            ]
            for i, value in enumerate(swap_grains(blocks)):
                k, r = divmod(i, 4)
                final[2 * pair + k, :, r, lanes] = value
    line = recv[0, 2 * levels : 2 * levels + 1, :]
    for g in range(1, recv.shape[0]):
        line = line + recv[g, 2 * levels : 2 * levels + 1, :]
    for h in range(HOURS):
        for t in range(4):
            at = (h * 4 + t) * 4
            stations[h, t, :, :] = line[:, at : at + 4]


def call(kernel, outs, scratch=()):
    return pl.pallas_call(
        kernel,
        out_shape=[jax.ShapeDtypeStruct(s, F32) for s in outs],
        scratch_shapes=[pltpu.VMEM(s, F32) for s in scratch],
        compiler_params=pltpu.CompilerParams(vmem_limit_bytes=48 * 1024 * 1024),
    )


def regrouped(sizes, adjoint, wind_east, wind_north, kz_inverse, kz_regime, fp_cell, fp_owner, fp_station, fp_weight):
    n_lat, n_lev, n_lon = sizes
    levels = adjoint.shape[1]
    total = levels * n_lev
    group = n_lat * n_lev
    lat_count = n_lat * adjoint.shape[2]
    place = chunk_owner(n_lat, n_lev)
    to_west = ring_perm(n_lat, n_lev, n_lon, -1)
    to_east = ring_perm(n_lat, n_lev, n_lon, 1)

    def exchange(x):
        return lax.all_to_all(x, AXES, split_axis=0, concat_axis=0, tiled=True)

    def rims(first, last):
        return lax.ppermute(first, RING, to_west), lax.ppermute(last, RING, to_east)

    in_rows = 3 * levels + 14
    in_rows += -in_rows % 8
    out_rows = 2 * levels + 1
    out_rows += -out_rows % 8
    (sent,) = call(functools.partial(pack_kernel, place), [(group, in_rows, LANES)])(
        adjoint, wind_east, wind_north, kz_regime, fp_cell, fp_owner.reshape(1, -1), fp_station, fp_weight
    )
    recv = exchange(sent)
    solved_0, winds, regimes, first, last = call(
        functools.partial(unpack_solve_kernel, n_lev),
        [(4 * total, 256), (2 * total, 256), (8, 256), (3 * total, LANES), (3 * total, LANES)],
        [(6 * total + 8, 256)],
    )(recv, kz_inverse)
    east_0, west_0 = rims(first, last)
    solved_1, first, last = call(
        functools.partial(transport_solve_kernel, lat_count),
        [(4 * total, 256), (2 * total, LANES), (2 * total, LANES)],
        [(4, total, 384), (4 * total, 256)],
    )(solved_0, winds, regimes, kz_inverse, east_0, west_0)
    east_1, west_1 = rims(first, last)
    (sums,) = call(functools.partial(footprint_kernel, 3 * levels + 2), [(8, 64)])(
        recv, solved_0, solved_1
    )
    (back,) = call(
        functools.partial(transport_pack_kernel, lat_count, n_lev),
        [(group, out_rows, LANES)],
        [(4, total, 384), (4 * total, 256)],
    )(solved_1, winds, east_0, west_0, east_1, west_1, sums)
    final, stations = call(
        functools.partial(unpack_kernel, place), [adjoint.shape, (HOURS, 4, 1, SPO)]
    )(exchange(back))
    return final, stations


def padded_2(x, sides, width, wrap):
    for axis, dim in sides:
        peers, length = (lax.axis_size(axis), x.shape[dim])
        up = [(i, (i + 1) % peers) for i in range(peers if wrap else peers - 1)]
        down = [(j, i) for i, j in up]
        last = lax.slice_in_dim(x, length - width, length, axis=dim)
        initial = lax.slice_in_dim(x, 0, width, axis=dim)
        before = lax.ppermute(last, axis, up)
        after = lax.ppermute(initial, axis, down)
        x = jnp.concatenate([before, x, after], axis=dim)
    return x


def lat_rim(values, rim_width):
    return padded_2(values, (("lat", 2),), rim_width, False)


def lon_rim(values, rim_width):
    return padded_2(values, (("lon", 3),), rim_width, True)


def lat_sweep(padded, north_face, south_face):
    middle = padded[:, :, 1:-1]
    return (
        middle
        + jnp.maximum(north_face, 0.0) * (padded[:, :, 2:] - middle)
        - jnp.minimum(south_face, 0.0) * (padded[:, :, :-2] - middle)
    )


def lon_sweep(padded, east_face, west_face):
    middle = padded[:, :, :, 1:-1]
    return (
        middle
        + jnp.maximum(east_face, 0.0) * (padded[:, :, :, 2:] - middle)
        - jnp.minimum(west_face, 0.0) * (padded[:, :, :, :-2] - middle)
    )


def shards(
    adjoint, wind_east, wind_north, kz_inverse, kz_regime, fp_cell, fp_owner, fp_station, fp_weight
):
    tracers, levels_dev, lat_rows, lon_cells = adjoint.shape
    row_index = lax.axis_index("lat") * lat_rows + lax.broadcasted_iota(
        jnp.int32, (1, lat_rows, 1), 1
    )
    last_row = lat_rows * lax.axis_size("lat") - 1
    north_face = jnp.where(row_index == last_row, jnp.zeros_like(wind_north), wind_north)
    south_face = lat_rim(north_face[None], 1)[0][:, :-2]
    west_face = lon_rim(wind_east[None], 1)[0][:, :, :-2]
    groups = lax.axis_size("lat") * lax.axis_size("lev")
    column_count = lat_rows * lon_cells // lax.axis_size("lev")
    first_column = lax.axis_index("lev") * column_count
    regime_rows = kz_regime.reshape(HOURS, lat_rows * lon_cells)
    cell_ids = fp_cell.reshape(-1)
    owners = fp_owner.reshape(-1)
    stations = fp_station.reshape(-1)
    weights = fp_weight.reshape(-1)
    entries = cell_ids.shape[0]
    adjoint_field = adjoint
    outputs = []
    for hour_step in range(HOURS):
        chosen = lax.dynamic_slice_in_dim(regime_rows[hour_step], first_column, column_count, 0)

        def column_solve(columns, chosen=chosen):
            result = jnp.zeros_like(columns)
            for regime in range(REGIMES):
                product = jnp.einsum(
                    "ji,tjp->tip", kz_inverse[regime], columns, precision=lax.Precision.HIGHEST
                )
                result = jnp.where(chosen[None, None, :] == regime, product, result)
            returned = lax.all_to_all(result, "lev", split_axis=1, concat_axis=2, tiled=True)
            return (returned, result)

        flat_field = adjoint_field.reshape(tracers, levels_dev, lat_rows * lon_cells)
        returned, solved = column_solve(
            lax.all_to_all(flat_field, "lev", split_axis=2, concat_axis=1, tiled=True)
        )
        lowest = solved[:, :FOOT_LEVELS, :].reshape(tracers, -1)
        picked = jnp.take(lowest, cell_ids, axis=1) * weights[None, :]
        capacity = 2 * entries // groups
        owner_hits = (owners[:, None] == jnp.arange(groups, dtype=jnp.int32)[None, :]).astype(
            jnp.int32
        )
        bucket_rank = jnp.sum(jnp.cumsum(owner_hits, axis=0) * owner_hits, axis=1) - 1
        slot_pos = owners * capacity + bucket_rank
        send_values = (
            jnp.zeros((tracers, groups * capacity), jnp.float32).at[:, slot_pos].set(picked)
        )
        send_ids = jnp.full((groups * capacity,), -1, jnp.int32).at[slot_pos].set(stations)
        arrived_values, arrived_ids = (
            lax.all_to_all(
                send_values.reshape(tracers, groups, capacity),
                ("lat", "lev"),
                split_axis=1,
                concat_axis=1,
                tiled=True,
            ),
            lax.all_to_all(
                send_ids.reshape(1, groups, capacity),
                ("lat", "lev"),
                split_axis=1,
                concat_axis=1,
                tiled=True,
            ),
        )
        matches = (
            arrived_ids[0][:, :, None] == jnp.arange(SPO, dtype=jnp.int32)[None, None, :]
        ).astype(jnp.float32)
        station_sums = jnp.einsum(
            "tgc,gcs->ts", arrived_values, matches, precision=lax.Precision.HIGHEST
        )
        outputs.append(station_sums)
        adjoint_field = returned.reshape(tracers, levels_dev, lat_rows, lon_cells)
        for substep in range(NSUB):
            adjoint_field = lat_sweep(lat_rim(adjoint_field, 1), north_face, south_face)
            adjoint_field = lon_sweep(lon_rim(adjoint_field, 1), wind_east, west_face)
    return (adjoint_field, jnp.stack(outputs)[:, :, None, :])


def fits(mesh_sizes, shape, kz_shape, entries):
    n_lat, n_lev, n_lon = mesh_sizes
    tracers, levels, rows, cells = shape
    return (
        tracers == 4
        and rows == 4
        and cells == 256
        and n_lat == 4
        and n_lat * n_lev == 16
        and levels * n_lev == kz_shape[1]
        and kz_shape[1] % 8 == 0
        and entries == 512
    )


def device_part(sizes, *arrays):
    if fits(sizes, arrays[0].shape, arrays[3].shape, arrays[5].shape[-1]):
        return regrouped(sizes, *arrays)
    return shards(*arrays)


def solution(mesh):
    sizes = tuple(mesh.shape[name] for name in RING)
    in_specs = (
        P(None, "lev", "lat", "lon"),
        P("lev", "lat", "lon"),
        P("lev", "lat", "lon"),
        P(),
        P(None, "lat", "lon"),
        P(AXES, "lon", None),
        P(AXES, "lon", None, None),
        P(AXES, "lon", None),
        P(AXES, "lon", None),
    )
    out_specs = (P(None, "lev", "lat", "lon"), P(None, None, "lon", AXES))
    return jax.shard_map(
        functools.partial(device_part, sizes),
        mesh=mesh,
        in_specs=in_specs,
        out_specs=out_specs,
        check_vma=False,
    )
```

profile of v0, /device:TPU:0, one launch (start us, length us, event | category | flops | bytes accessed | tf_op | source)
XLA Modules:
  0.0 105.0 jit_solution(15715688568175043278)
XLA Ops:
  0.6 1.0 copy-done.1
  1.7 0.9 copy-done.2
  2.6 0.9 copy-done.3
  3.5 0.7 copy-done.4
  4.2 0.7 copy-done.5
  4.9 0.7 copy-done.6
  5.6 0.7 copy-done.7
  6.2 0.7 copy-done.8
  6.9 1.5 %shard_map.104 = f32[16,120,128]{2,1,0:T(8,128)S(1)} custom-call(f32[4,34,4,256]{3,2,1,0:T(4,128)S(1)} %copy-done.1, f32[34,4,256]{2,1,0:T(4,128)S(1)} %copy-done.2, f32[34,4,256]{2,1,0:T(4,128)S(1)} %copy-done.3, s32[2,4,256]{2,1,0:T(4,128)S(1)} %copy-done.4, s32[1,1,512]{2,1,0:T(1,128)S(1)} %copy-done.5, s32[1,512]{1,0:T(1,128)S(1)} %bitcast.1, ...), custom_call_target="tpu_custom_call" | custom-call | tf_op jit(solution)/shard_map/pallas_call | solution.py:386
  8.4 0.0 copy-start
  8.5 32.9 %all_to_all.10.recv = f32[16,120,128]{2,1,0:T(8,128)S(1)} all-to-all(f32[16,120,128]{2,1,0:T(8,128)S(1)} %shard_map.104), channel_id=1, replica_groups=mesh['lat'=4,'lev'=4,'lon'=2] {'lat','lev'}, dimensions={0} | all-to-all | bytes 1966080 | tf_op jit(solution)/shard_map/all_to_all | solution.py:377
  41.3 1.7 %shard_map.105 = (f32[544,256]{1,0:T(8,128)S(1)}, f32[272,256]{1,0:T(8,128)S(1)}, f32[8,256]{1,0:T(8,128)S(1)}, f32[408,128]{1,0:T(8,128)S(1)}, f32[408,128]{1,0:T(8,128)S(1)}) custom-call(f32[16,120,128]{2,1,0:T(8,128)S(1)} %all_to_all.10.recv, f32[4,136,136]{2,1,0:T(8,128)S(1)} %copy-done), custom_call_target="tpu_custom_call" | custom-call | tf_op jit(solution)/shard_map/pallas_call | solution.py:390
  43.1 1.5 %collective-permute-start = (f32[408,128]{1,0:T(8,128)S(1)}, f32[408,128]{1,0:T(8,128)S(1)}, u32[]{:S(2)}, u32[]{:S(2)}) collective-permute-start(f32[408,128]{1,0:T(8,128)S(1)} %get-tuple-element.13), channel_id=1, source_target_pairs={{0,25},{8,0},{2,8},{10,2},{4,10},{12,4},{6,12},{14,6},{22,14},{30,... | collective-permute-start | bytes 626696 | tf_op jit(solution)/shard_map/ppermute | solution.py:380
  44.5 0.0 collective-permute-start.1
  44.5 3.3 %collective-permute-done.from_east.from_east_0 = f32[408,128]{1,0:T(8,128)S(1)} collective-permute-done((f32[408,128]{1,0:T(8,128)S(1)}, f32[408,128]{1,0:T(8,128)S(1)}, u32[]{:S(2)}, u32[]{:S(2)}) %collective-permute-start) | collective-permute-done | bytes 208928 | tf_op jit(solution)/shard_map/ppermute | solution.py:380
  47.8 2.8 %collective-permute-done.1.from_west.from_west_0 = f32[408,128]{1,0:T(8,128)S(1)} collective-permute-done((f32[408,128]{1,0:T(8,128)S(1)}, f32[408,128]{1,0:T(8,128)S(1)}, u32[]{:S(2)}, u32[]{:S(2)}) %collective-permute-start.1) | collective-permute-done | bytes 208928 | tf_op jit(solution)/shard_map/ppermute | solution.py:380
  50.7 13.9 %shard_map.106 = (f32[544,256]{1,0:T(8,128)S(1)}, f32[272,128]{1,0:T(8,128)S(1)}, f32[272,128]{1,0:T(8,128)S(1)}) custom-call(f32[544,256]{1,0:T(8,128)S(1)} %get-tuple-element.10.field.hour_0, f32[272,256]{1,0:T(8,128)S(1)} %get-tuple-element.11.winds, f32[8,256]{1,0:T(8,128)S(1)} %get-tuple-element.12.regimes, f32[4,136,136]{2,1,0:T(8,128)S(1)} %copy-done, ...), custom_call_target="tpu_custom_call" | custom-call | tf_op jit(solution)/shard_map/pallas_call | solution.py:396
  64.6 0.1 collective-permute-start.2
  64.6 0.5 collective-permute-start.3
  65.1 2.2 %shard_map.107.sums = f32[8,64]{1,0:T(8,128)S(1)} custom-call(f32[16,120,128]{2,1,0:T(8,128)S(1)} %all_to_all.10.recv, f32[544,256]{1,0:T(8,128)S(1)} %get-tuple-element.10.field.hour_0, f32[544,256]{1,0:T(8,128)S(1)} %get-tuple-element.15.hour_1.field), custom_call_target="tpu_custom_call" | custom-call | tf_op jit(solution)/shard_map/pallas_call | solution.py:402
  67.4 2.7 %collective-permute-done.3.from_west = f32[272,128]{1,0:T(8,128)S(1)} collective-permute-done((f32[272,128]{1,0:T(8,128)S(1)}, f32[272,128]{1,0:T(8,128)S(1)}, u32[]{:S(2)}, u32[]{:S(2)}) %collective-permute-start.3) | collective-permute-done | bytes 139296 | tf_op jit(solution)/shard_map/ppermute | solution.py:380
  70.1 13.2 %shard_map.108 = f32[16,72,128]{2,1,0:T(8,128)S(1)} custom-call(f32[544,256]{1,0:T(8,128)S(1)} %get-tuple-element.15.hour_1.field, f32[272,256]{1,0:T(8,128)S(1)} %get-tuple-element.11.winds, f32[408,128]{1,0:T(8,128)S(1)} %collective-permute-done.from_east.from_east_0, f32[408,128]{1,0:T(8,128)S(1)} %collective-permute-done.1.from_west.from_west_0, ...), custom_call_target="tpu_custom_call" | custom-call | tf_op jit(solution)/shard_map/pallas_call | solution.py:405
  83.3 19.9 %all_to_all.11.recv = f32[16,72,128]{2,1,0:T(8,128)S(1)} all-to-all(f32[16,72,128]{2,1,0:T(8,128)S(1)} %shard_map.108), channel_id=1, replica_groups=mesh['lat'=4,'lev'=4,'lon'=2] {'lat','lev'}, dimensions={0} | all-to-all | bytes 1179648 | tf_op jit(solution)/shard_map/all_to_all | solution.py:377
  103.2 1.8 %shard_map.109 = (f32[4,34,4,256]{3,2,1,0:T(4,128)}, f32[2,4,1,4]{3,2,1,0:T(1,128)}) custom-call(f32[16,72,128]{2,1,0:T(8,128)S(1)} %all_to_all.11.recv), custom_call_target="tpu_custom_call" | custom-call | tf_op jit(solution)/shard_map/pallas_call | solution.py:410
  (10 shorter events, 0.0 us)
Async XLA Ops:
  0.6 1.1 %copy-start.1 = (f32[4,34,4,256]{3,2,1,0:T(4,128)S(1)}, f32[4,34,4,256]{3,2,1,0:T(4,128)}, u32[]{:S(2)}) copy-start(f32[4,34,4,256]{3,2,1,0:T(4,128)} %adj.1) | copy-start | bytes 1671172
  1.7 0.9 copy-start.2
  2.6 0.9 copy-start.3
  3.5 0.7 copy-start.4
  4.2 0.7 copy-start.5
  4.9 0.7 copy-start.6
  5.6 0.7 copy-start.7
  6.2 0.7 copy-start.8
  8.4 32.9 %copy-start = (f32[4,136,136]{2,1,0:T(8,128)S(1)}, f32[4,136,136]{2,1,0:T(8,128)}, u32[]{:S(2)}) copy-start(f32[4,136,136]{2,1,0:T(8,128)} %kz.3) | copy-start | bytes 887812
  43.1 4.8 %collective-permute-start = (f32[408,128]{1,0:T(8,128)S(1)}, f32[408,128]{1,0:T(8,128)S(1)}, u32[]{:S(2)}, u32[]{:S(2)}) collective-permute-start(f32[408,128]{1,0:T(8,128)S(1)} %get-tuple-element.13), channel_id=1, source_target_pairs={{0,25},{8,0},{2,8},{10,2},{4,10},{12,4},{6,12},{14,6},{22,14},{30,... | collective-permute-start | bytes 626696 | tf_op jit(solution)/shard_map/ppermute | solution.py:380
  44.5 6.1 %collective-permute-start.1 = (f32[408,128]{1,0:T(8,128)S(1)}, f32[408,128]{1,0:T(8,128)S(1)}, u32[]{:S(2)}, u32[]{:S(2)}) collective-permute-start(f32[408,128]{1,0:T(8,128)S(1)} %get-tuple-element.14), channel_id=1, source_target_pairs={{0,8},{8,2},{2,10},{10,4},{4,12},{12,6},{6,14},{14,22},{22,30},{30... | collective-permute-start | bytes 626696 | tf_op jit(solution)/shard_map/ppermute | solution.py:380
  64.6 2.8 %collective-permute-start.2 = (f32[272,128]{1,0:T(8,128)S(1)}, f32[272,128]{1,0:T(8,128)S(1)}, u32[]{:S(2)}, u32[]{:S(2)}) collective-permute-start(f32[272,128]{1,0:T(8,128)S(1)} %get-tuple-element.16), channel_id=1, source_target_pairs={{0,25},{8,0},{2,8},{10,2},{4,10},{12,4},{6,12},{14,6},{22,14},{30,... | collective-permute-start | bytes 417800 | tf_op jit(solution)/shard_map/ppermute | solution.py:380
  64.6 5.4 %collective-permute-start.3 = (f32[272,128]{1,0:T(8,128)S(1)}, f32[272,128]{1,0:T(8,128)S(1)}, u32[]{:S(2)}, u32[]{:S(2)}) collective-permute-start(f32[272,128]{1,0:T(8,128)S(1)} %get-tuple-element.17), channel_id=1, source_target_pairs={{0,8},{8,2},{2,10},{10,4},{4,12},{12,6},{6,14},{14,22},{22,30},{30... | collective-permute-start | bytes 417800 | tf_op jit(solution)/shard_map/ppermute | solution.py:380
where the time goes:
time: 105 us
  blocking collectives  52.7 us (50%)
  Pallas kernels  34.4 us (33%)
  waiting for transfers between devices  8.82 us (8%)
  local copies, waits for them, and re-layouts  6.29 us (6%)
  starting transfers between devices  2.03 us (2%)
    all_to_all x2, blocking collectives, exchange(): return lax.all_to_all(x, AXES, split_axis=0, concat_axis=0, tiled=True)  52.7 us
    pallas_call x1, Pallas kernels, regrouped(): call(functools.partial(transport_solve_kernel, lat_count), [(4 * total, 2...  13.9 us
    pallas_call x1, Pallas kernels, regrouped(): call(functools.partial(transport_pack_kernel, lat_count, n_lev), [(group,...  13.2 us
    unnamed x18, local copies, waits for them, and re-layouts  6.29 us
    ppermute x2, waiting for transfers between devices, rims(): lax.ppermute(last, RING, to_east)  5.5 us
    ppermute x2, waiting for transfers between devices, rims(): lax.ppermute(first, RING, to_west)  3.32 us
    pallas_call x1, Pallas kernels, regrouped(): call(functools.partial(footprint_kernel, 3 * levels + 2), [(8, 64)])  2.22 us
  transfers between devices with their start and end apart: 4, of which 3 were waited for; matrix products, arithmetic and copies ran while one was open for 0% of the time, Pallas kernels for 2%

commit v1 on v0

--- a/solution.py
+++ b/solution.py
@@ -90,7 +90,20 @@
     return (mm(high, matrix) + mm(middle, matrix)) + mm(low, matrix)
 
 
-def pack_kernel(place, adj, east, north, regime, cell, owner, station, weight, out):
+def pack_kernel(place, *refs):
+    count = (len(refs) - 2) // 2
+    given, out, held, sems = refs[:count], refs[count], refs[count + 1 : -1], refs[-1]
+    copies = [
+        pltpu.make_async_copy(a, b, sems.at[i]) for i, (a, b) in enumerate(zip(given, held))
+    ]
+    for copy in copies:
+        copy.start()
+    for copy in copies:
+        copy.wait()
+    pack(place, *held, out)
+
+
+def pack(place, adj, east, north, regime, cell, owner, station, weight, out):
     levels = adj.shape[1]
     rows = adj.shape[2]
     for pair in range(3):
@@ -190,63 +203,98 @@
     )
 
 
-def with_rims(main, from_east, from_west, upper):
+def rim_lanes(from_east, from_west, rows, upper):
     half = LANES // 2
-    low = lane_ids(main.shape[0]) < half
+    east, west = from_east[rows, :], from_west[rows, :]
+    low = lane_ids(east.shape[0]) < half
     if upper:
-        rim = jnp.where(low, pltpu.roll(from_east, half, 1), from_west)
-    else:
-        rim = jnp.where(low, from_east, pltpu.roll(from_west, half, 1))
-    return jnp.concatenate([main, rim], axis=1)
+        return jnp.where(low, pltpu.roll(east, half, 1), west)
+    return jnp.where(low, east, pltpu.roll(west, half, 1))
+
+
+def columns(ref, rows):
+    return [ref[rows, i * LANES : (i + 1) * LANES] for i in range(3)]
+
+
+def pair_columns(ref, rows):
+    return [ref[rows, i * LANES : (i + 1) * LANES] for i in range(2)]
+
+
+def turned(x, shift):
+    return pltpu.roll(x, shift % LANES, 1)
+
+
+def stepped(blocks, shift):
+    count = len(blocks)
+    lane = lane_ids(blocks[0].shape[0])
+    moved = [turned(x, shift) for x in blocks]
+    if shift > 0:
+        return [jnp.where(lane < shift, moved[i - 1], moved[i]) for i in range(count)]
+    return [
+        jnp.where(lane >= LANES + shift, moved[(i + 1) % count], moved[i]) for i in range(count)
+    ]
 
 
 def face_weights(lat_count, winds, from_east, from_west, total, faces):
-    width = 384
     rims = slice(2 * total, 3 * total)
-    east = with_rims(winds[0:total, :], from_east[rims, :], from_west[rims, :], False)
-    north = with_rims(winds[total:, :], from_east[rims, :], from_west[rims, :], True)
-    lat = lax.broadcasted_iota(jnp.int32, (total, width), 1) % lat_count
-    north = jnp.where(lat == lat_count - 1, 0.0, north)
-    south = pltpu.roll(north, 1, 1)
-    west = pltpu.roll(east, lat_count, 1)
-    faces[0] = jnp.maximum(north, 0.0)
-    faces[1] = -jnp.minimum(south, 0.0)
-    faces[2] = jnp.maximum(east, 0.0)
-    faces[3] = -jnp.minimum(west, 0.0)
-
-
-def transport(lat_count, field, east_rows, west_rows, faces, total, result):
-    width = 384
-    block = 8
-
-    @pl.loop(0, total // block)
-    def _(step):
-        rows = pl.ds(pl.multiple_of(step * block, block), block)
-        up, down, right, left = [faces[k, rows, :] for k in range(4)]
+    east = pair_columns(winds, slice(0, total)) + [rim_lanes(from_east, from_west, rims, False)]
+    north = pair_columns(winds, slice(total, 2 * total)) + [
+        rim_lanes(from_east, from_west, rims, True)
+    ]
+    lat = lane_ids(total) % lat_count
+    north = [jnp.where(lat == lat_count - 1, 0.0, x) for x in north]
+    west = stepped(east, lat_count)
+    for i in range(3):
+        lanes = slice(i * LANES, (i + 1) * LANES)
+        after = jnp.maximum(north[i], 0.0)
+        before = -jnp.minimum(jnp.where(lat == 0, 0.0, turned(north[i], 1)), 0.0)
+        faces[0, :, lanes] = 1.0 - after - before
+        faces[1, :, lanes] = after
+        faces[2, :, lanes] = before
+        after = jnp.maximum(east[i], 0.0)
+        before = -jnp.minimum(west[i], 0.0)
+        faces[3, :, lanes] = 1.0 - after - before
+        faces[4, :, lanes] = after
+        faces[5, :, lanes] = before
+
+
+def transport(lat_count, field, east_rows, west_rows, faces, total, buffers, result):
+    for t in range(4):
+        own = slice(t * total, (t + 1) * total)
+        rim = slice((t % 2) * total, (t % 2 + 1) * total)
+        buffers[0, own, 0:256] = field[own, :]
+        buffers[0, own, 256:384] = rim_lanes(east_rows, west_rows, rim, t >= 2)
+    for step in range(2 * NSUB):
+        last = step == 2 * NSUB - 1
         for t in range(4):
-            own = pl.ds(pl.multiple_of(t * total + step * block, block), block)
-            rim = pl.ds(pl.multiple_of((t % 2) * total + step * block, block), block)
-            f = with_rims(field[own, :], east_rows[rim, :], west_rows[rim, :], t >= 2)
-            for _ in range(NSUB):
-                f = (
-                    f
-                    + up * (pltpu.roll(f, width - 1, 1) - f)
-                    + down * (pltpu.roll(f, 1, 1) - f)
+            own = slice(t * total, (t + 1) * total)
+            f = columns(buffers.at[step % 2], own)
+            if step % 2 == 0:
+                after = [turned(x, -1) for x in f]
+                before = [turned(x, 1) for x in f]
+            else:
+                after = stepped(f, -lat_count)
+                before = stepped(f, lat_count)
+            base = 3 * (step % 2)
+            for i in range(2 if last else 3):
+                lanes = slice(i * LANES, (i + 1) * LANES)
+                value = (
+                    faces[base, :, lanes] * f[i]
+                    + faces[base + 1, :, lanes] * after[i]
+                    + faces[base + 2, :, lanes] * before[i]
                 )
-                f = (
-                    f
-                    + right * (pltpu.roll(f, width - lat_count, 1) - f)
-                    + left * (pltpu.roll(f, lat_count, 1) - f)
-                )
-            result[own, :] = f[:, :256]
+                if last:
+                    result[own, lanes] = value
+                else:
+                    buffers[(step + 1) % 2, own, lanes] = value
 
 
 def transport_solve_kernel(
-    lat_count, field, winds, regimes, kz, from_east, from_west, solved, first, last, faces, moved
+    lat_count, field, winds, regimes, kz, from_east, from_west, solved, first, last, faces, buffers, moved
 ):
     total = kz.shape[1]
     face_weights(lat_count, winds, from_east, from_west, total, faces)
-    transport(lat_count, field, from_east, from_west, faces, total, moved)
+    transport(lat_count, field, from_east, from_west, faces, total, buffers, moved)
     kz_high, kz_low = mixing(kz)
     for t in range(4):
         high, low = split_two(moved[t * total : (t + 1) * total, :])
@@ -295,12 +343,12 @@
 
 def transport_pack_kernel(
     lat_count, n_lev, field, winds, from_east_0, from_west_0, from_east, from_west, sums, out,
-    faces, moved,
+    faces, buffers, moved,
 ):
     total = winds.shape[0] // 2
     levels = total // n_lev
     face_weights(lat_count, winds, from_east_0, from_west_0, total, faces)
-    transport(lat_count, field, from_east, from_west, faces, total, moved)
+    transport(lat_count, field, from_east, from_west, faces, total, buffers, moved)
     matrix = transpose_matrix()
     for pair in range(2):
         for k in range(2):
@@ -383,9 +431,16 @@
     in_rows += -in_rows % 8
     out_rows = 2 * levels + 1
     out_rows += -out_rows % 8
-    (sent,) = call(functools.partial(pack_kernel, place), [(group, in_rows, LANES)])(
+    given = (
         adjoint, wind_east, wind_north, kz_regime, fp_cell, fp_owner.reshape(1, -1), fp_station, fp_weight
     )
+    sent = pl.pallas_call(
+        functools.partial(pack_kernel, place),
+        in_specs=[pl.BlockSpec(memory_space=pltpu.HBM)] * len(given),
+        out_shape=jax.ShapeDtypeStruct((group, in_rows, LANES), F32),
+        scratch_shapes=[pltpu.VMEM(x.shape, x.dtype) for x in given]
+        + [pltpu.SemaphoreType.DMA((len(given),))],
+    )(*given)
     recv = exchange(sent)
     solved_0, winds, regimes, first, last = call(
         functools.partial(unpack_solve_kernel, n_lev),
@@ -396,7 +451,7 @@
     solved_1, first, last = call(
         functools.partial(transport_solve_kernel, lat_count),
         [(4 * total, 256), (2 * total, LANES), (2 * total, LANES)],
-        [(4, total, 384), (4 * total, 256)],
+        [(6, total, 384), (2, 4 * total, 384), (4 * total, 256)],
     )(solved_0, winds, regimes, kz_inverse, east_0, west_0)
     east_1, west_1 = rims(first, last)
     (sums,) = call(functools.partial(footprint_kernel, 3 * levels + 2), [(8, 64)])(
@@ -405,7 +460,7 @@
     (back,) = call(
         functools.partial(transport_pack_kernel, lat_count, n_lev),
         [(group, out_rows, LANES)],
-        [(4, total, 384), (4 * total, 256)],
+        [(6, total, 384), (2, 4 * total, 384), (4 * total, 256)],
     )(solved_1, winds, east_0, west_0, east_1, west_1, sums)
     final, stations = call(
         functools.partial(unpack_kernel, place), [adjoint.shape, (HOURS, 4, 1, SPO)]

time: 105 us -> 83.5 us (0.80)
  Pallas kernels: 34.4 us -> 18.6 us
  local copies, waits for them, and re-layouts: 6.29 us -> 0.01 us
    pallas_call x1, Pallas kernels: 13.9 us -> 4.79 us  [regrouped(): call(functools.partial(transport_solve_kernel, lat_count), [(4 * total, 2...]
    pallas_call x1, Pallas kernels: 13.2 us -> 4.36 us  [regrouped(): call(functools.partial(transport_pack_kernel, lat_count, n_lev), [(group,...]
    unnamed x18 -> x2, local copies, waits for them, and re-layouts: 6.29 us -> 0.01 us
    pallas_call x1, Pallas kernels: 1.51 us -> 3.66 us  [regrouped(): pl.pallas_call(functools.partial(pack_kernel, place), in_specs=[pl.BlockS...]
  transfers between devices with their start and end apart: 4 -> 4, of which waited for: 3 -> 3; matrix products, arithmetic and copies ran while one was open for 0% -> 0% of each run, Pallas kernels for 2% -> 3%
where the time goes in v1:
time: 83.5 us; the launch traced here: 83.3 us
  blocking collectives  52.9 us (63%)
  Pallas kernels  18.6 us (22%)
  waiting for transfers between devices  9 us (11%)
  starting transfers between devices  2.04 us (2%)
    all_to_all x2, blocking collectives, exchange(): return lax.all_to_all(x, AXES, split_axis=0, concat_axis=0, tiled=True)  52.9 us
    ppermute x2, waiting for transfers between devices, rims(): lax.ppermute(last, RING, to_east)  5.68 us
    pallas_call x1, Pallas kernels, regrouped(): call(functools.partial(transport_solve_kernel, lat_count), [(4 * total, 2...  4.79 us
    pallas_call x1, Pallas kernels, regrouped(): call(functools.partial(transport_pack_kernel, lat_count, n_lev), [(group,...  4.36 us
    pallas_call x1, Pallas kernels, regrouped(): pl.pallas_call(functools.partial(pack_kernel, place), in_specs=[pl.BlockS...  3.66 us
    ppermute x2, waiting for transfers between devices, rims(): lax.ppermute(first, RING, to_west)  3.32 us
    pallas_call x1, Pallas kernels, regrouped(): call(functools.partial(footprint_kernel, 3 * levels + 2), [(8, 64)])  2.22 us
    pallas_call x1, Pallas kernels, regrouped(): call(functools.partial(unpack_kernel, place), [adjoint.shape, (HOURS, 4,...  1.8 us
  transfers between devices with their start and end apart: 4, of which 3 were waited for; matrix products, arithmetic and copies ran while one was open for 0% of the time, Pallas kernels for 3%

profile of v1, /device:TPU:0, one launch (start us, length us, event | category | flops | bytes accessed | tf_op | source)
XLA Modules:
  0.0 83.3 jit_solution(3833618545122190265)
XLA Ops:
  0.6 3.7 %shard_map.104 = f32[16,120,128]{2,1,0:T(8,128)} custom-call(f32[4,34,4,256]{3,2,1,0:T(4,128)} %refs_0_.1, f32[34,4,256]{2,1,0:T(4,128)} %refs_1_.1, f32[34,4,256]{2,1,0:T(4,128)} %refs_2_.1, s32[2,4,256]{2,1,0:T(4,128)} %refs_3_.1, s32[1,1,512]{2,1,0:T(1,128)} %refs_4_.1, s32[1,512]{1,0:T(1,128)} %bitcast.1, s32[1,1,512]{2,1,0:T(1,128)} %refs_6_.1, ...), custom_call_target="tpu_custom_call" | custom-call | tf_op jit(solution)/shard_map/pallas_call | solution.py:437
  4.3 0.0 copy-start
  4.3 33.1 %all_to_all.10.recv = f32[16,120,128]{2,1,0:T(8,128)S(1)} all-to-all(f32[16,120,128]{2,1,0:T(8,128)} %shard_map.104), channel_id=1, replica_groups=mesh['lat'=4,'lev'=4,'lon'=2] {'lat','lev'}, dimensions={0} | all-to-all | bytes 1966080 | tf_op jit(solution)/shard_map/all_to_all | solution.py:425
  37.4 0.0 copy-done
  37.4 1.7 %shard_map.105 = (f32[544,256]{1,0:T(8,128)S(1)}, f32[272,256]{1,0:T(8,128)S(1)}, f32[8,256]{1,0:T(8,128)S(1)}, f32[408,128]{1,0:T(8,128)S(1)}, f32[408,128]{1,0:T(8,128)S(1)}) custom-call(f32[16,120,128]{2,1,0:T(8,128)S(1)} %all_to_all.10.recv, f32[4,136,136]{2,1,0:T(8,128)S(1)} %copy-done), custom_call_target="tpu_custom_call" | custom-call | tf_op jit(solution)/shard_map/pallas_call | solution.py:445
  39.1 1.5 %collective-permute-start = (f32[408,128]{1,0:T(8,128)S(1)}, f32[408,128]{1,0:T(8,128)S(1)}, u32[]{:S(2)}, u32[]{:S(2)}) collective-permute-start(f32[408,128]{1,0:T(8,128)S(1)} %get-tuple-element.13), channel_id=1, source_target_pairs={{0,25},{8,0},{2,8},{10,2},{4,10},{12,4},{6,12},{14,6},{22,14},{30,... | collective-permute-start | bytes 626696 | tf_op jit(solution)/shard_map/ppermute | solution.py:428
  40.6 0.0 collective-permute-start.1
  40.6 3.3 %collective-permute-done.from_east.from_east_0 = f32[408,128]{1,0:T(8,128)S(1)} collective-permute-done((f32[408,128]{1,0:T(8,128)S(1)}, f32[408,128]{1,0:T(8,128)S(1)}, u32[]{:S(2)}, u32[]{:S(2)}) %collective-permute-start) | collective-permute-done | bytes 208928 | tf_op jit(solution)/shard_map/ppermute | solution.py:428
  43.9 2.8 %collective-permute-done.1.from_west.from_west_0 = f32[408,128]{1,0:T(8,128)S(1)} collective-permute-done((f32[408,128]{1,0:T(8,128)S(1)}, f32[408,128]{1,0:T(8,128)S(1)}, u32[]{:S(2)}, u32[]{:S(2)}) %collective-permute-start.1) | collective-permute-done | bytes 208928 | tf_op jit(solution)/shard_map/ppermute | solution.py:428
  46.7 4.8 %shard_map.106 = (f32[544,256]{1,0:T(8,128)S(1)}, f32[272,128]{1,0:T(8,128)S(1)}, f32[272,128]{1,0:T(8,128)S(1)}) custom-call(f32[544,256]{1,0:T(8,128)S(1)} %get-tuple-element.10.field.hour_0, f32[272,256]{1,0:T(8,128)S(1)} %get-tuple-element.11.winds, f32[8,256]{1,0:T(8,128)S(1)} %get-tuple-element.12.regimes, f32[4,136,136]{2,1,0:T(8,128)S(1)} %copy-done, ...), custom_call_target="tpu_custom_call" | custom-call | tf_op jit(solution)/shard_map/pallas_call | solution.py:451
  51.5 0.1 collective-permute-start.2
  51.6 0.5 collective-permute-start.3
  52.1 2.2 %shard_map.107.sums = f32[8,64]{1,0:T(8,128)S(1)} custom-call(f32[16,120,128]{2,1,0:T(8,128)S(1)} %all_to_all.10.recv, f32[544,256]{1,0:T(8,128)S(1)} %get-tuple-element.10.field.hour_0, f32[544,256]{1,0:T(8,128)S(1)} %get-tuple-element.15.hour_1.field), custom_call_target="tpu_custom_call" | custom-call | tf_op jit(solution)/shard_map/pallas_call | solution.py:457
  54.3 0.0 collective-permute-done.2.from_east
  54.3 2.9 %collective-permute-done.3.from_west = f32[272,128]{1,0:T(8,128)S(1)} collective-permute-done((f32[272,128]{1,0:T(8,128)S(1)}, f32[272,128]{1,0:T(8,128)S(1)}, u32[]{:S(2)}, u32[]{:S(2)}) %collective-permute-start.3) | collective-permute-done | bytes 139296 | tf_op jit(solution)/shard_map/ppermute | solution.py:428
  57.2 4.4 %shard_map.108 = f32[16,72,128]{2,1,0:T(8,128)S(1)} custom-call(f32[544,256]{1,0:T(8,128)S(1)} %get-tuple-element.15.hour_1.field, f32[272,256]{1,0:T(8,128)S(1)} %get-tuple-element.11.winds, f32[408,128]{1,0:T(8,128)S(1)} %collective-permute-done.from_east.from_east_0, f32[408,128]{1,0:T(8,128)S(1)} %collective-permute-done.1.from_west.from_west_0, ...), custom_call_target="tpu_custom_call" | custom-call | tf_op jit(solution)/shard_map/pallas_call | solution.py:460
  61.6 19.9 %all_to_all.11.recv = f32[16,72,128]{2,1,0:T(8,128)S(1)} all-to-all(f32[16,72,128]{2,1,0:T(8,128)S(1)} %shard_map.108), channel_id=1, replica_groups=mesh['lat'=4,'lev'=4,'lon'=2] {'lat','lev'}, dimensions={0} | all-to-all | bytes 1179648 | tf_op jit(solution)/shard_map/all_to_all | solution.py:425
  81.5 1.8 %shard_map.109 = (f32[4,34,4,256]{3,2,1,0:T(4,128)}, f32[2,4,1,4]{3,2,1,0:T(1,128)}) custom-call(f32[16,72,128]{2,1,0:T(8,128)S(1)} %all_to_all.11.recv), custom_call_target="tpu_custom_call" | custom-call | tf_op jit(solution)/shard_map/pallas_call | solution.py:465
Async XLA Ops:
  4.3 33.1 %copy-start = (f32[4,136,136]{2,1,0:T(8,128)S(1)}, f32[4,136,136]{2,1,0:T(8,128)}, u32[]{:S(2)}) copy-start(f32[4,136,136]{2,1,0:T(8,128)} %kz.3) | copy-start | bytes 887812
  39.1 4.8 %collective-permute-start = (f32[408,128]{1,0:T(8,128)S(1)}, f32[408,128]{1,0:T(8,128)S(1)}, u32[]{:S(2)}, u32[]{:S(2)}) collective-permute-start(f32[408,128]{1,0:T(8,128)S(1)} %get-tuple-element.13), channel_id=1, source_target_pairs={{0,25},{8,0},{2,8},{10,2},{4,10},{12,4},{6,12},{14,6},{22,14},{30,... | collective-permute-start | bytes 626696 | tf_op jit(solution)/shard_map/ppermute | solution.py:428
  40.6 6.1 %collective-permute-start.1 = (f32[408,128]{1,0:T(8,128)S(1)}, f32[408,128]{1,0:T(8,128)S(1)}, u32[]{:S(2)}, u32[]{:S(2)}) collective-permute-start(f32[408,128]{1,0:T(8,128)S(1)} %get-tuple-element.14), channel_id=1, source_target_pairs={{0,8},{8,2},{2,10},{10,4},{4,12},{12,6},{6,14},{14,22},{22,30},{30... | collective-permute-start | bytes 626696 | tf_op jit(solution)/shard_map/ppermute | solution.py:428
  51.5 2.8 %collective-permute-start.2 = (f32[272,128]{1,0:T(8,128)S(1)}, f32[272,128]{1,0:T(8,128)S(1)}, u32[]{:S(2)}, u32[]{:S(2)}) collective-permute-start(f32[272,128]{1,0:T(8,128)S(1)} %get-tuple-element.16), channel_id=1, source_target_pairs={{0,25},{8,0},{2,8},{10,2},{4,10},{12,4},{6,12},{14,6},{22,14},{30,... | collective-permute-start | bytes 417800 | tf_op jit(solution)/shard_map/ppermute | solution.py:428
  51.6 5.6 %collective-permute-start.3 = (f32[272,128]{1,0:T(8,128)S(1)}, f32[272,128]{1,0:T(8,128)S(1)}, u32[]{:S(2)}, u32[]{:S(2)}) collective-permute-start(f32[272,128]{1,0:T(8,128)S(1)} %get-tuple-element.17), channel_id=1, source_target_pairs={{0,8},{8,2},{2,10},{10,4},{4,12},{12,6},{6,14},{14,22},{22,30},{30... | collective-permute-start | bytes 417800 | tf_op jit(solution)/shard_map/ppermute | solution.py:428

commit v2 on v1

--- a/solution.py
+++ b/solution.py
@@ -13,6 +13,7 @@
 SPO = 4
 LANES = 128
 GRAIN = 16
+ENTRY_ROWS = 16
 F32 = jnp.float32
 BF16 = jnp.bfloat16
 AXES = ("lat", "lev")
@@ -31,9 +32,18 @@
 
 def ring_perm(n_lat, n_lev, n_lon, shift):
     place = chunk_owner(n_lat, n_lev)
-    ring = [place[d] * n_lon + o for o in range(n_lon) for d in range(len(place))]
+    ring = [
+        (place[::-1] if o % 2 else place)[d] * n_lon + o
+        for o in range(n_lon)
+        for d in range(len(place))
+    ]
     count = len(ring)
     return [(ring[i], ring[(i + shift) % count]) for i in range(count)]
+
+
+def owners(place):
+    odd = lax.axis_index("lon") % 2 == 1
+    return [jnp.where(odd, there, here) for here, there in zip(place, place[::-1])]
 
 
 def lane_ids(rows):
@@ -91,49 +101,43 @@
 
 
 def pack_kernel(place, *refs):
-    count = (len(refs) - 2) // 2
-    given, out, held, sems = refs[:count], refs[count], refs[count + 1 : -1], refs[-1]
+    count = (len(refs) - 4) // 2
+    given, outs = refs[:count], refs[count : count + 3]
+    held, sems = refs[count + 3 : -1], refs[-1]
+    place = owners(place)
     copies = [
         pltpu.make_async_copy(a, b, sems.at[i]) for i, (a, b) in enumerate(zip(given, held))
     ]
     for copy in copies:
         copy.start()
-    for copy in copies:
-        copy.wait()
-    pack(place, *held, out)
-
-
-def pack(place, adj, east, north, regime, cell, owner, station, weight, out):
+    adj, east, north, regime, cell, owner, station, weight = held
+    fields, winds, entries = outs
     levels = adj.shape[1]
     rows = adj.shape[2]
-    for pair in range(3):
-        if pair < 2:
-            srcs = [adj[2 * pair + k, :, r, :] for k in range(2) for r in range(rows)]
-        else:
-            srcs = [w[:, r, :] for w in (east, north) for r in range(rows)]
+
+    def place_pieces(srcs, out, first, count):
         for half in range(2):
             lanes = slice(half * LANES, (half + 1) * LANES)
             for j, piece in enumerate(swap_grains([s[:, lanes] for s in srcs])):
-                out[place[half * 8 + j], pair * levels : (pair + 1) * levels, :] = piece
-    first = 3 * levels
+                out[place[half * 8 + j], first : first + count, :] = piece
+
+    copies[0].wait()
+    for pair in range(2):
+        srcs = [adj[2 * pair + k, :, r, :] for k in range(2) for r in range(rows)]
+        place_pieces(srcs, fields, pair * levels, levels)
+    for copy in copies[1:]:
+        copy.wait()
+    srcs = [w[:, r, :] for w in (east, north) for r in range(rows)]
+    place_pieces(srcs, winds, 0, levels)
     srcs = [regime[h, r : r + 1, :].astype(F32) for h in range(HOURS) for r in range(rows)]
-    cells = cell[0]
-    level, lon = cells // 256, cells % 256
+    place_pieces(srcs, fields, 2 * levels, 1)
+    cells = cell[0].astype(F32)
     stations = (owner[...] * SPO + station[0]).astype(F32)
-    weights = weight[0]
-    for half in range(2):
-        lanes = slice(half * LANES, (half + 1) * LANES)
-        for j, piece in enumerate(swap_grains([s[:, lanes] for s in srcs])):
-            d = half * 8 + j
-            g = place[d]
-            out[g, first : first + 1, :] = piece
-            here = lon - d * GRAIN
-            code = jnp.where((here >= 0) & (here < GRAIN), here * FOOT_LEVELS + level, -1).astype(F32)
-            for k in range(4):
-                part = slice(k * LANES, (k + 1) * LANES)
-                out[g, first + 2 + k : first + 3 + k, :] = code[:, part]
-                out[g, first + 6 + k : first + 7 + k, :] = stations[:, part]
-                out[g, first + 10 + k : first + 11 + k, :] = weights[:, part]
+    for k in range(4):
+        part = slice(k * LANES, (k + 1) * LANES)
+        entries[k : k + 1, :] = cells[:, part]
+        entries[4 + k : 5 + k, :] = stations[:, part]
+        entries[8 + k : 9 + k, :] = weight[0][:, part]
 
 
 def solve_columns(high, low, kz_high, kz_low, regime, levels):
@@ -156,11 +160,10 @@
     last[rows, :] = jnp.where(low, pltpu.roll(top[:, LANES:], half, 1), bottom[:, LANES:])
 
 
-def unpack_solve_kernel(n_lev, recv, kz, solved, winds, regimes, first, last, field):
-    per = recv.shape[0] // n_lev
+def unpack_solve_kernel(n_lev, recv, kz, solved, regimes, first, last, field):
     total = kz.shape[1]
     levels = total // n_lev
-    for pair in range(3):
+    for pair in range(2):
         for z in range(n_lev):
             for half in range(2):
                 lanes = slice(half * LANES, (half + 1) * LANES)
@@ -171,12 +174,12 @@
                 for k, value in enumerate(swap_halves(a, b)):
                     base = (2 * pair + k) * total + z * levels
                     field[base : base + levels, lanes] = value
-    base = 6 * total
+    base = 4 * total
     field[base : base + 8, :] = jnp.zeros((8, 256), F32)
     for half in range(2):
         lanes = slice(half * LANES, (half + 1) * LANES)
         a, b = [
-            recv[(2 * half + k) * n_lev, 3 * levels : 3 * levels + 1, :] for k in range(2)
+            recv[(2 * half + k) * n_lev, 2 * levels : 2 * levels + 1, :] for k in range(2)
         ]
         for k, value in enumerate(swap_halves(a, b)):
             field[base + k : base + k + 1, lanes] = value
@@ -184,10 +187,6 @@
     regime = mm(field[base : base + 8, :].astype(BF16), matrix)
     regimes[...] = regime
     kz_high, kz_low = mixing(kz)
-    for k in range(2):
-        winds[k * total : (k + 1) * total, :] = move_lanes(
-            field[(4 + k) * total : (5 + k) * total, :], matrix
-        )
     for t in range(4):
         high, low = split_two(field[t * total : (t + 1) * total, :])
         high = mm(high, matrix).astype(BF16)
@@ -198,9 +197,23 @@
     rim_messages(
         solved[0 : 2 * total, :], solved[2 * total :, :], first, last, slice(0, 2 * total)
     )
-    rim_messages(
-        winds[0:total, :], winds[total:, :], first, last, slice(2 * total, 3 * total)
-    )
+
+
+def unpack_winds_kernel(n_lev, others, winds, first, last, field):
+    total = winds.shape[0] // 2
+    levels = total // n_lev
+    own_lat, own_lev = lax.axis_index("lat"), lax.axis_index("lev")
+    for z in range(n_lev):
+        for half in range(2):
+            lanes = slice(half * LANES, (half + 1) * LANES)
+            a, b = [
+                others[z ^ own_lev, (2 * half + k) ^ own_lat, 0:levels, :] for k in range(2)
+            ]
+            for k, value in enumerate(swap_halves(a, b)):
+                base = k * total + z * levels
+                field[base : base + levels, lanes] = value
+    winds[...] = move_lanes(field[...], transpose_matrix())
+    rim_messages(winds[0:total, :], winds[total:, :], first, last, slice(0, total))
 
 
 def rim_lanes(from_east, from_west, rows, upper):
@@ -236,7 +249,7 @@
 
 
 def face_weights(lat_count, winds, from_east, from_west, total, faces):
-    rims = slice(2 * total, 3 * total)
+    rims = slice(0, total)
     east = pair_columns(winds, slice(0, total)) + [rim_lanes(from_east, from_west, rims, False)]
     north = pair_columns(winds, slice(total, 2 * total)) + [
         rim_lanes(from_east, from_west, rims, True)
@@ -290,10 +303,10 @@
 
 
 def transport_solve_kernel(
-    lat_count, field, winds, regimes, kz, from_east, from_west, solved, first, last, faces, buffers, moved
+    lat_count, field, winds, regimes, kz, wind_east, wind_west, from_east, from_west, solved, first, last, faces, buffers, moved
 ):
     total = kz.shape[1]
-    face_weights(lat_count, winds, from_east, from_west, total, faces)
+    face_weights(lat_count, winds, wind_east, wind_west, total, faces)
     transport(lat_count, field, from_east, from_west, faces, total, buffers, moved)
     kz_high, kz_low = mixing(kz)
     for t in range(4):
@@ -306,7 +319,13 @@
     )
 
 
-def footprint_kernel(entry_row, recv, hour_0, hour_1, sums):
+def footprint_kernel(n_lev, entry_row, others, hour_0, hour_1, sums):
+    own_lat, own_lev = lax.axis_index("lat"), lax.axis_index("lev")
+    chip, core = own_lat // 2, own_lat % 2
+    step = jnp.where(chip % 2 == 0, own_lev, n_lev - 1 - own_lev)
+    chunk = (chip * n_lev + step) * 2 + core
+    odd = lax.axis_index("lon") % 2 == 1
+    first_lon = jnp.where(odd, others.shape[0] * others.shape[1] - 1 - chunk, chunk) * GRAIN
     total = hour_0.shape[0] // 4
     matrix = transpose_matrix()
     low = jnp.concatenate(
@@ -319,19 +338,21 @@
     cell_ids = lax.broadcasted_iota(jnp.int32, (GRAIN, 512), 0)
     level_ids = lax.broadcasted_iota(jnp.int32, (FOOT_LEVELS, 512), 0)
     station_ids = lax.broadcasted_iota(jnp.int32, (64, 512), 0)
-    for row in range(recv.shape[0]):
+    for row in range(others.shape[0] * others.shape[1]):
+        z, a = (row % n_lev) ^ own_lev, (row // n_lev) ^ own_lat
+
         def entries(at):
             return jnp.concatenate(
-                [recv[row, at + k : at + k + 1, :] for k in range(4)], axis=1
+                [others[z, a, at + k : at + k + 1, :] for k in range(4)], axis=1
             )
 
         code = entries(entry_row).astype(jnp.int32)
         station = entries(entry_row + 4).astype(jnp.int32)
         weight = entries(entry_row + 8)
-        cells = ((code >> 3) == cell_ids).astype(F32).astype(BF16)
+        cells = ((code & 255) - first_lon == cell_ids).astype(F32).astype(BF16)
         picked = mm(parts[:, row * GRAIN : (row + 1) * GRAIN], cells)
         picked = (picked[:count] + picked[count : 2 * count]) + picked[2 * count :]
-        level = jnp.where((code & 7) == level_ids, weight, 0.0)
+        level = jnp.where((code >> 8) == level_ids, weight, 0.0)
         picked = picked * jnp.concatenate([level] * (count // FOOT_LEVELS), axis=0)
         named = (station == station_ids).astype(F32).astype(BF16)
         high, rest = split_two(picked)
@@ -382,6 +403,7 @@
 
 
 def unpack_kernel(place, recv, final, stations):
+    place = owners(place)
     levels = final.shape[1]
     for pair in range(2):
         for half in range(2):
@@ -402,6 +424,31 @@
             stations[h, t, :, :] = line[:, at : at + 4]
 
 
+def gather_others(sizes, winds, entries):
+    n_lat, n_lev, n_lon = sizes
+    own_lat, own_lev = lax.axis_index("lat"), lax.axis_index("lev")
+    pieces = winds.reshape(n_lat, n_lev, *winds.shape[1:])
+
+    def swap(x, axis, count, k):
+        return lax.ppermute(x, axis, [(i, i ^ k) for i in range(count)])
+
+    def for_lat(k):
+        piece = lax.dynamic_index_in_dim(pieces, own_lat ^ k, 0, keepdims=False)
+        return jnp.concatenate([piece.reshape(-1, LANES), entries], axis=0)
+
+    here = jnp.stack([for_lat(0)] + [swap(for_lat(k), "lat", n_lat, k) for k in range(1, n_lat)])
+    split = n_lev * winds.shape[1]
+    pieces = here[:, :split].reshape(n_lat, n_lev, *winds.shape[1:])
+
+    def for_lev(k):
+        piece = lax.dynamic_index_in_dim(pieces, own_lev ^ k, 1, keepdims=False)
+        return jnp.concatenate([piece, here[:, split:]], axis=1)
+
+    return jnp.stack(
+        [for_lev(0)] + [swap(for_lev(k), "lev", n_lev, k) for k in range(1, n_lev)]
+    )
+
+
 def call(kernel, outs, scratch=()):
     return pl.pallas_call(
         kernel,
@@ -427,41 +474,52 @@
     def rims(first, last):
         return lax.ppermute(first, RING, to_west), lax.ppermute(last, RING, to_east)
 
-    in_rows = 3 * levels + 14
-    in_rows += -in_rows % 8
     out_rows = 2 * levels + 1
     out_rows += -out_rows % 8
+    wind_rows = levels + -levels % 8
     given = (
         adjoint, wind_east, wind_north, kz_regime, fp_cell, fp_owner.reshape(1, -1), fp_station, fp_weight
     )
-    sent = pl.pallas_call(
+    fields, winds, entries = pl.pallas_call(
         functools.partial(pack_kernel, place),
         in_specs=[pl.BlockSpec(memory_space=pltpu.HBM)] * len(given),
-        out_shape=jax.ShapeDtypeStruct((group, in_rows, LANES), F32),
+        out_shape=[
+            jax.ShapeDtypeStruct(shape, F32)
+            for shape in (
+                (group, out_rows, LANES), (group, wind_rows, LANES), (ENTRY_ROWS, LANES)
+            )
+        ],
         scratch_shapes=[pltpu.VMEM(x.shape, x.dtype) for x in given]
         + [pltpu.SemaphoreType.DMA((len(given),))],
     )(*given)
-    recv = exchange(sent)
-    solved_0, winds, regimes, first, last = call(
+    recv = exchange(fields)
+    others = gather_others(sizes, winds, entries)
+    solved_0, regimes, first, last = call(
         functools.partial(unpack_solve_kernel, n_lev),
-        [(4 * total, 256), (2 * total, 256), (8, 256), (3 * total, LANES), (3 * total, LANES)],
-        [(6 * total + 8, 256)],
+        [(4 * total, 256), (8, 256), (2 * total, LANES), (2 * total, LANES)],
+        [(4 * total + 8, 256)],
     )(recv, kz_inverse)
     east_0, west_0 = rims(first, last)
+    winds, first, last = call(
+        functools.partial(unpack_winds_kernel, n_lev),
+        [(2 * total, 256), (total, LANES), (total, LANES)],
+        [(2 * total, 256)],
+    )(others)
+    wind_rims = rims(first, last)
     solved_1, first, last = call(
         functools.partial(transport_solve_kernel, lat_count),
         [(4 * total, 256), (2 * total, LANES), (2 * total, LANES)],
         [(6, total, 384), (2, 4 * total, 384), (4 * total, 256)],
-    )(solved_0, winds, regimes, kz_inverse, east_0, west_0)
+    )(solved_0, winds, regimes, kz_inverse, *wind_rims, east_0, west_0)
     east_1, west_1 = rims(first, last)
-    (sums,) = call(functools.partial(footprint_kernel, 3 * levels + 2), [(8, 64)])(
-        recv, solved_0, solved_1
+    (sums,) = call(functools.partial(footprint_kernel, n_lev, wind_rows), [(8, 64)])(
+        others, solved_0, solved_1
     )
     (back,) = call(
         functools.partial(transport_pack_kernel, lat_count, n_lev),
         [(group, out_rows, LANES)],
         [(6, total, 384), (2, 4 * total, 384), (4 * total, 256)],
-    )(solved_1, winds, east_0, west_0, east_1, west_1, sums)
+    )(solved_1, winds, *wind_rims, east_1, west_1, sums)
     final, stations = call(
         functools.partial(unpack_kernel, place), [adjoint.shape, (HOURS, 4, 1, SPO)]
     )(exchange(back))

time: 83.5 us -> 80.6 us (0.965)
  blocking collectives: 52.9 us -> 19.9 us
  starting transfers between devices: 2.04 us -> 17.9 us
  waiting for transfers between devices: 9 us -> 21.9 us
    all_to_all x2 -> x1, blocking collectives: 52.9 us -> 19.9 us  [exchange(): return lax.all_to_all(x, AXES, split_axis=0, concat_axis=0, tiled=True)]
    ppermute x0 -> x6, waiting for transfers between devices: none -> 14.9 us  [swap(): return lax.ppermute(x, axis, [(i, i ^ k) for i in range(count)])]
    all_to_all x0 -> x1, starting transfers between devices: none -> 7.5 us  [exchange(): return lax.all_to_all(x, AXES, split_axis=0, concat_axis=0, tiled=True)]
    ppermute x0 -> x6, starting transfers between devices: none -> 6.71 us  [swap(): return lax.ppermute(x, axis, [(i, i ^ k) for i in range(count)])]
    ppermute x2 -> x3, starting transfers between devices: 1.54 us -> 3.23 us  [rims(): lax.ppermute(first, RING, to_west)]
    ppermute x2 -> x3, waiting for transfers between devices: 3.32 us -> 1.95 us  [rims(): lax.ppermute(first, RING, to_west)]
    ppermute x2 -> x3, waiting for transfers between devices: 5.68 us -> 4.92 us  [rims(): lax.ppermute(last, RING, to_east)]
    pallas_call x2 -> x3, Pallas kernels: 3.97 us -> 4.25 us  [the longest x1 2.22 us: regrouped(): call(functools.partial(footprint_kernel, n_lev, wind_rows), [(8, 64)])]
  transfers between devices with their start and end apart: 4 -> 13, of which waited for: 3 -> 8; matrix products, arithmetic and copies ran while one was open for 0% -> 0% of each run, Pallas kernels for 3% -> 5%
where the time goes in v2:
time: 80.6 us; the launch traced here: 80.3 us
  waiting for transfers between devices  21.9 us (27%)
  blocking collectives  19.9 us (25%)
  Pallas kernels  18.9 us (23%)
  starting transfers between devices  17.9 us (22%)
    all_to_all x1, blocking collectives, exchange(): return lax.all_to_all(x, AXES, split_axis=0, concat_axis=0, tiled=True)  19.9 us
    ppermute x6, waiting for transfers between devices, swap(): return lax.ppermute(x, axis, [(i, i ^ k) for i in range(count)])  14.9 us
    all_to_all x1, starting transfers between devices, exchange(): return lax.all_to_all(x, AXES, split_axis=0, concat_axis=0, tiled=True)  7.5 us
    ppermute x6, starting transfers between devices, swap(): return lax.ppermute(x, axis, [(i, i ^ k) for i in range(count)])  6.71 us
    ppermute x3, waiting for transfers between devices, rims(): lax.ppermute(last, RING, to_east)  4.92 us
    pallas_call x1, Pallas kernels, regrouped(): call(functools.partial(transport_solve_kernel, lat_count), [(4 * total, 2...  4.76 us
    pallas_call x1, Pallas kernels, regrouped(): call(functools.partial(transport_pack_kernel, lat_count, n_lev), [(group,...  4.36 us
    pallas_call x1, Pallas kernels, regrouped(): pl.pallas_call(functools.partial(pack_kernel, place), in_specs=[pl.BlockS...  3.67 us
  transfers between devices with their start and end apart: 13, of which 8 were waited for; matrix products, arithmetic and copies ran while one was open for 0% of the time, Pallas kernels for 5%

profile of v2, /device:TPU:0, one launch (start us, length us, event | category | flops | bytes accessed | tf_op | source)
XLA Modules:
  0.0 80.3 jit_solution(16169391823293739912)
XLA Ops:
  0.6 3.7 %shard_map.104 = (f32[16,72,128]{2,1,0:T(8,128)}, f32[16,40,128]{2,1,0:T(8,128)}, f32[16,128]{1,0:T(8,128)}) custom-call(f32[4,34,4,256]{3,2,1,0:T(4,128)} %refs_0_.1, f32[34,4,256]{2,1,0:T(4,128)} %refs_1_.1, f32[34,4,256]{2,1,0:T(4,128)} %refs_2_.1, s32[2,4,256]{2,1,0:T(4,128)} %refs_3_.1, s32[1,1,512]{2,1,0:T(1,128)} %refs_4_.1, s32[1,512]{1,0:T(1,128)} %bitcast.40, ...), custom_call_target="tpu_custom_call" | custom-call | tf_op jit(solution)/shard_map/pallas_call | solution.py:483
  4.3 7.5 %all-to-all-start = ((f32[16,72,128]{2,1,0:T(8,128)}), f32[16,72,128]{2,1,0:T(8,128)S(1)}, u32[]{:S(2)}, u32[]{:S(2)}) async-start(f32[16,72,128]{2,1,0:T(8,128)} %get-tuple-element.15), calls=%async_computation | async-start | bytes 1179648 | tf_op jit(solution)/shard_map/all_to_all | solution.py:472
  11.9 0.7 copy-done.2
  12.6 0.5 collective-permute-start
  13.1 1.7 %collective-permute-start.1 = (f32[176,128]{1,0:T(8,128)S(1)}, f32[176,128]{1,0:T(8,128)S(1)}, u32[]{:S(2)}, u32[]{:S(2)}) collective-permute-start(f32[176,128]{1,0:T(8,128)S(1)} %get-tuple-element.43), channel_id=1, source_target_pairs={{0,16},{8,24},{16,0},{24,8},{1,17},{9,25},{17,1},{25,9},{2,18},{10... | collective-permute-start | bytes 270344 | tf_op jit(solution)/shard_map/ppermute | solution.py:433
  14.8 8.1 %collective-permute-done.1 = f32[176,128]{1,0:T(8,128)S(1)} collective-permute-done((f32[176,128]{1,0:T(8,128)S(1)}, f32[176,128]{1,0:T(8,128)S(1)}, u32[]{:S(2)}, u32[]{:S(2)}) %collective-permute-start.1) | collective-permute-done | bytes 90144 | tf_op jit(solution)/shard_map/ppermute | solution.py:433
  22.9 1.2 %collective-permute-done.2 = f32[176,128]{1,0:T(8,128)S(1)} collective-permute-done((f32[176,128]{1,0:T(8,128)S(1)}, f32[176,128]{1,0:T(8,128)S(1)}, u32[]{:S(2)}, u32[]{:S(2)}) %collective-permute-start.2) | collective-permute-done | bytes 90144 | tf_op jit(solution)/shard_map/ppermute | solution.py:433
  24.2 0.6 collective-permute-start.3
  24.8 4.0 %collective-permute-start.4 = (f32[4,56,128]{2,1,0:T(8,128)S(1)}, f32[4,56,128]{2,1,0:T(8,128)S(1)}, u32[]{:S(2)}, u32[]{:S(2)}) collective-permute-start(f32[4,56,128]{2,1,0:T(8,128)S(1)} %get-tuple-element.39), channel_id=1, source_target_pairs={{0,4},{2,6},{4,0},{6,2},{1,5},{3,7},{5,1},{7,3},{8,12},{10,14},{12... | collective-permute-start | bytes 344072 | tf_op jit(solution)/shard_map/ppermute | solution.py:433
  28.9 1.6 %shard_map.105 = (f32[544,256]{1,0:T(8,128)S(1)}, f32[8,256]{1,0:T(8,128)S(1)}, f32[272,128]{1,0:T(8,128)S(1)}, f32[272,128]{1,0:T(8,128)S(1)}) custom-call(f32[16,72,128]{2,1,0:T(8,128)S(1)} %all-to-all-done.recv, f32[4,136,136]{2,1,0:T(8,128)S(1)} %copy-done), custom_call_target="tpu_custom_call" | custom-call | tf_op jit(solution)/shard_map/pallas_call | solution.py:497
  30.5 1.6 %collective-permute-start.8 = (f32[272,128]{1,0:T(8,128)S(1)}, f32[272,128]{1,0:T(8,128)S(1)}, u32[]{:S(2)}, u32[]{:S(2)}) collective-permute-start(f32[272,128]{1,0:T(8,128)S(1)} %get-tuple-element.23), channel_id=1, source_target_pairs={{0,1},{8,0},{2,8},{10,2},{4,10},{12,4},{6,12},{14,6},{22,14},{30,2... | collective-permute-start | bytes 417800 | tf_op jit(solution)/shard_map/ppermute | solution.py:475
  32.1 0.6 collective-permute-done.3
  32.7 5.0 %collective-permute-done.4 = f32[4,56,128]{2,1,0:T(8,128)S(1)} collective-permute-done((f32[4,56,128]{2,1,0:T(8,128)S(1)}, f32[4,56,128]{2,1,0:T(8,128)S(1)}, u32[]{:S(2)}, u32[]{:S(2)}) %collective-permute-start.4) | collective-permute-done | bytes 114720 | tf_op jit(solution)/shard_map/ppermute | solution.py:433
  37.8 0.4 shard_map.106
  38.2 1.6 %collective-permute-start.6 = (f32[136,128]{1,0:T(8,128)S(1)}, f32[136,128]{1,0:T(8,128)S(1)}, u32[]{:S(2)}, u32[]{:S(2)}) collective-permute-start(f32[136,128]{1,0:T(8,128)S(1)} %get-tuple-element.21), channel_id=1, source_target_pairs={{0,1},{8,0},{2,8},{10,2},{4,10},{12,4},{6,12},{14,6},{22,14},{30,2... | collective-permute-start | bytes 208904 | tf_op jit(solution)/shard_map/ppermute | solution.py:475
  39.8 1.9 %collective-permute-done.6.wind_east.from_east_0 = f32[136,128]{1,0:T(8,128)S(1)} collective-permute-done((f32[136,128]{1,0:T(8,128)S(1)}, f32[136,128]{1,0:T(8,128)S(1)}, u32[]{:S(2)}, u32[]{:S(2)}) %collective-permute-start.6) | collective-permute-done | bytes 69664 | tf_op jit(solution)/shard_map/ppermute | solution.py:475
  41.7 2.4 %collective-permute-done.7.wind_west.from_west_0 = f32[136,128]{1,0:T(8,128)S(1)} collective-permute-done((f32[136,128]{1,0:T(8,128)S(1)}, f32[136,128]{1,0:T(8,128)S(1)}, u32[]{:S(2)}, u32[]{:S(2)}) %collective-permute-start.7) | collective-permute-done | bytes 69664 | tf_op jit(solution)/shard_map/ppermute | solution.py:475
  44.1 4.8 %shard_map.107 = (f32[544,256]{1,0:T(8,128)S(1)}, f32[272,128]{1,0:T(8,128)S(1)}, f32[272,128]{1,0:T(8,128)S(1)}) custom-call(f32[544,256]{1,0:T(8,128)S(1)} %get-tuple-element.16.field.hour_0, f32[272,256]{1,0:T(8,128)S(1)} %get-tuple-element.19.winds, f32[8,256]{1,0:T(8,128)S(1)} %get-tuple-element.20.regimes, f32[4,136,136]{2,1,0:T(8,128)S(1)} %copy-done, ...), custom_call_target="tpu_custom_call" | custom-call | tf_op jit(solution)/shard_map/pallas_call | solution.py:509
  48.9 0.5 collective-permute-start.11
  49.4 2.2 %shard_map.108.sums = f32[8,64]{1,0:T(8,128)S(1)} custom-call(f32[4,4,56,128]{3,2,1,0:T(8,128)S(1)} %pad_maximum_fusion.others, f32[544,256]{1,0:T(8,128)S(1)} %get-tuple-element.16.field.hour_0, f32[544,256]{1,0:T(8,128)S(1)} %get-tuple-element.25.hour_1.field), custom_call_target="tpu_custom_call" | custom-call | tf_op jit(solution)/shard_map/pallas_call | solution.py:515
  51.7 2.6 %collective-permute-done.11.from_west = f32[272,128]{1,0:T(8,128)S(1)} collective-permute-done((f32[272,128]{1,0:T(8,128)S(1)}, f32[272,128]{1,0:T(8,128)S(1)}, u32[]{:S(2)}, u32[]{:S(2)}) %collective-permute-start.11) | collective-permute-done | bytes 139296 | tf_op jit(solution)/shard_map/ppermute | solution.py:475
  54.2 4.4 %shard_map.109 = f32[16,72,128]{2,1,0:T(8,128)S(1)} custom-call(f32[544,256]{1,0:T(8,128)S(1)} %get-tuple-element.25.hour_1.field, f32[272,256]{1,0:T(8,128)S(1)} %get-tuple-element.19.winds, f32[136,128]{1,0:T(8,128)S(1)} %collective-permute-done.6.wind_east.from_east_0, f32[136,128]{1,0:T(8,128)S(1)} %collective-permute-done.7.wind_west.from_west_0, ...), custom_call_target="tpu_custom_call" | custom-call | tf_op jit(solution)/shard_map/pallas_call | solution.py:518
  58.6 19.9 %all_to_all.10.recv = f32[16,72,128]{2,1,0:T(8,128)S(1)} all-to-all(f32[16,72,128]{2,1,0:T(8,128)S(1)} %shard_map.109), channel_id=1, replica_groups=mesh['lat'=4,'lev'=4,'lon'=2] {'lat','lev'}, dimensions={0} | all-to-all | bytes 1179648 | tf_op jit(solution)/shard_map/all_to_all | solution.py:472
  78.5 1.8 %shard_map.110 = (f32[4,34,4,256]{3,2,1,0:T(4,128)}, f32[2,4,1,4]{3,2,1,0:T(1,128)}) custom-call(f32[16,72,128]{2,1,0:T(8,128)S(1)} %all_to_all.10.recv), custom_call_target="tpu_custom_call" | custom-call | tf_op jit(solution)/shard_map/pallas_call | solution.py:523
  (24 shorter events, 0.5 us)
Async XLA Ops:
  4.3 7.5 %copy-start.1 = (f32[16,40,128]{2,1,0:T(8,128)S(1)}, f32[16,40,128]{2,1,0:T(8,128)}, u32[]{:S(2)}) copy-start(f32[16,40,128]{2,1,0:T(8,128)} %get-tuple-element.17) | copy-start | bytes 983044
  4.3 24.6 %all-to-all-start = ((f32[16,72,128]{2,1,0:T(8,128)}), f32[16,72,128]{2,1,0:T(8,128)S(1)}, u32[]{:S(2)}, u32[]{:S(2)}) async-start(f32[16,72,128]{2,1,0:T(8,128)} %get-tuple-element.15), calls=%async_computation | async-start | bytes 1179648 | tf_op jit(solution)/shard_map/all_to_all | solution.py:472
  11.9 0.7 copy-start.2
  12.6 2.1 %collective-permute-start = (f32[176,128]{1,0:T(8,128)S(1)}, f32[176,128]{1,0:T(8,128)S(1)}, u32[]{:S(2)}, u32[]{:S(2)}) collective-permute-start(f32[176,128]{1,0:T(8,128)S(1)} %get-tuple-element.42), channel_id=1, source_target_pairs={{0,8},{8,0},{16,24},{24,16},{1,9},{9,1},{17,25},{25,17},{2,10},{10... | collective-permute-start | bytes 270344 | tf_op jit(solution)/shard_map/ppermute | solution.py:433
  13.1 9.8 %collective-permute-start.1 = (f32[176,128]{1,0:T(8,128)S(1)}, f32[176,128]{1,0:T(8,128)S(1)}, u32[]{:S(2)}, u32[]{:S(2)}) collective-permute-start(f32[176,128]{1,0:T(8,128)S(1)} %get-tuple-element.43), channel_id=1, source_target_pairs={{0,16},{8,24},{16,0},{24,8},{1,17},{9,25},{17,1},{25,9},{2,18},{10... | collective-permute-start | bytes 270344 | tf_op jit(solution)/shard_map/ppermute | solution.py:433
  14.8 9.3 %collective-permute-start.2 = (f32[176,128]{1,0:T(8,128)S(1)}, f32[176,128]{1,0:T(8,128)S(1)}, u32[]{:S(2)}, u32[]{:S(2)}) collective-permute-start(f32[176,128]{1,0:T(8,128)S(1)} %get-tuple-element.44), channel_id=1, source_target_pairs={{0,24},{8,16},{16,8},{24,0},{1,25},{9,17},{17,9},{25,1},{2,26},{10... | collective-permute-start | bytes 270344 | tf_op jit(solution)/shard_map/ppermute | solution.py:433
  24.1 4.8 %copy-start = (f32[4,136,136]{2,1,0:T(8,128)S(1)}, f32[4,136,136]{2,1,0:T(8,128)}, u32[]{:S(2)}) copy-start(f32[4,136,136]{2,1,0:T(8,128)} %kz.3) | copy-start | bytes 887812
  24.2 8.5 %collective-permute-start.3 = (f32[4,56,128]{2,1,0:T(8,128)S(1)}, f32[4,56,128]{2,1,0:T(8,128)S(1)}, u32[]{:S(2)}, u32[]{:S(2)}) collective-permute-start(f32[4,56,128]{2,1,0:T(8,128)S(1)} %get-tuple-element.38), channel_id=1, source_target_pairs={{0,2},{2,0},{4,6},{6,4},{1,3},{3,1},{5,7},{7,5},{8,10},{10,8},{12,... | collective-permute-start | bytes 344072 | tf_op jit(solution)/shard_map/ppermute | solution.py:433
  24.8 12.9 %collective-permute-start.4 = (f32[4,56,128]{2,1,0:T(8,128)S(1)}, f32[4,56,128]{2,1,0:T(8,128)S(1)}, u32[]{:S(2)}, u32[]{:S(2)}) collective-permute-start(f32[4,56,128]{2,1,0:T(8,128)S(1)} %get-tuple-element.39), channel_id=1, source_target_pairs={{0,4},{2,6},{4,0},{6,2},{1,5},{3,7},{5,1},{7,3},{8,12},{10,14},{12... | collective-permute-start | bytes 344072 | tf_op jit(solution)/shard_map/ppermute | solution.py:433
  28.8 9.0 %collective-permute-start.5 = (f32[4,56,128]{2,1,0:T(8,128)S(1)}, f32[4,56,128]{2,1,0:T(8,128)S(1)}, u32[]{:S(2)}, u32[]{:S(2)}) collective-permute-start(f32[4,56,128]{2,1,0:T(8,128)S(1)} %get-tuple-element.40), channel_id=1, source_target_pairs={{0,6},{2,4},{4,2},{6,0},{1,7},{3,5},{5,3},{7,1},{8,14},{10,12},{12... | collective-permute-start | bytes 344072 | tf_op jit(solution)/shard_map/ppermute | solution.py:433
  30.5 13.6 %collective-permute-start.8 = (f32[272,128]{1,0:T(8,128)S(1)}, f32[272,128]{1,0:T(8,128)S(1)}, u32[]{:S(2)}, u32[]{:S(2)}) collective-permute-start(f32[272,128]{1,0:T(8,128)S(1)} %get-tuple-element.23), channel_id=1, source_target_pairs={{0,1},{8,0},{2,8},{10,2},{4,10},{12,4},{6,12},{14,6},{22,14},{30,2... | collective-permute-start | bytes 417800 | tf_op jit(solution)/shard_map/ppermute | solution.py:475
  32.1 12.0 %collective-permute-start.9 = (f32[272,128]{1,0:T(8,128)S(1)}, f32[272,128]{1,0:T(8,128)S(1)}, u32[]{:S(2)}, u32[]{:S(2)}) collective-permute-start(f32[272,128]{1,0:T(8,128)S(1)} %get-tuple-element.24), channel_id=1, source_target_pairs={{0,8},{8,2},{2,10},{10,4},{4,12},{12,6},{6,14},{14,22},{22,30},{30... | collective-permute-start | bytes 417800 | tf_op jit(solution)/shard_map/ppermute | solution.py:475
  38.2 3.5 %collective-permute-start.6 = (f32[136,128]{1,0:T(8,128)S(1)}, f32[136,128]{1,0:T(8,128)S(1)}, u32[]{:S(2)}, u32[]{:S(2)}) collective-permute-start(f32[136,128]{1,0:T(8,128)S(1)} %get-tuple-element.21), channel_id=1, source_target_pairs={{0,1},{8,0},{2,8},{10,2},{4,10},{12,4},{6,12},{14,6},{22,14},{30,2... | collective-permute-start | bytes 208904 | tf_op jit(solution)/shard_map/ppermute | solution.py:475
  39.8 4.3 %collective-permute-start.7 = (f32[136,128]{1,0:T(8,128)S(1)}, f32[136,128]{1,0:T(8,128)S(1)}, u32[]{:S(2)}, u32[]{:S(2)}) collective-permute-start(f32[136,128]{1,0:T(8,128)S(1)} %get-tuple-element.22), channel_id=1, source_target_pairs={{0,8},{8,2},{2,10},{10,4},{4,12},{12,6},{6,14},{14,22},{22,30},{30... | collective-permute-start | bytes 208904 | tf_op jit(solution)/shard_map/ppermute | solution.py:475
  48.9 2.8 %collective-permute-start.10 = (f32[272,128]{1,0:T(8,128)S(1)}, f32[272,128]{1,0:T(8,128)S(1)}, u32[]{:S(2)}, u32[]{:S(2)}) collective-permute-start(f32[272,128]{1,0:T(8,128)S(1)} %get-tuple-element.26), channel_id=1, source_target_pairs={{0,1},{8,0},{2,8},{10,2},{4,10},{12,4},{6,12},{14,6},{22,14},{30,2... | collective-permute-start | bytes 417800 | tf_op jit(solution)/shard_map/ppermute | solution.py:475
  48.9 5.3 %collective-permute-start.11 = (f32[272,128]{1,0:T(8,128)S(1)}, f32[272,128]{1,0:T(8,128)S(1)}, u32[]{:S(2)}, u32[]{:S(2)}) collective-permute-start(f32[272,128]{1,0:T(8,128)S(1)} %get-tuple-element.27), channel_id=1, source_target_pairs={{0,8},{8,2},{2,10},{10,4},{4,12},{12,6},{6,14},{14,22},{22,30},{30... | collective-permute-start | bytes 417800 | tf_op jit(solution)/shard_map/ppermute | solution.py:475

commit v3 on v2

--- a/solution.py
+++ b/solution.py
@@ -13,7 +13,7 @@
 SPO = 4
 LANES = 128
 GRAIN = 16
-ENTRY_ROWS = 16
+ENTRY_ROWS = 12
 F32 = jnp.float32
 BF16 = jnp.bfloat16
 AXES = ("lat", "lev")
@@ -425,27 +425,31 @@
 
 
 def gather_others(sizes, winds, entries):
-    n_lat, n_lev, n_lon = sizes
+    n_lat, n_lev, _ = sizes
     own_lat, own_lev = lax.axis_index("lat"), lax.axis_index("lev")
-    pieces = winds.reshape(n_lat, n_lev, *winds.shape[1:])
+    levels = winds.shape[1]
+    pieces = winds.reshape(n_lat, n_lev * levels, LANES)
 
     def swap(x, axis, count, k):
         return lax.ppermute(x, axis, [(i, i ^ k) for i in range(count)])
 
     def for_lat(k):
         piece = lax.dynamic_index_in_dim(pieces, own_lat ^ k, 0, keepdims=False)
-        return jnp.concatenate([piece.reshape(-1, LANES), entries], axis=0)
+        return jnp.concatenate([piece, entries], axis=0)
 
     here = jnp.stack([for_lat(0)] + [swap(for_lat(k), "lat", n_lat, k) for k in range(1, n_lat)])
-    split = n_lev * winds.shape[1]
-    pieces = here[:, :split].reshape(n_lat, n_lev, *winds.shape[1:])
+    pieces = here[:, : n_lev * levels].reshape(n_lat, n_lev, levels, LANES)
+    entries = here[:, n_lev * levels :].reshape(-1, LANES)
 
     def for_lev(k):
         piece = lax.dynamic_index_in_dim(pieces, own_lev ^ k, 1, keepdims=False)
-        return jnp.concatenate([piece, here[:, split:]], axis=1)
-
-    return jnp.stack(
-        [for_lev(0)] + [swap(for_lev(k), "lev", n_lev, k) for k in range(1, n_lev)]
+        return jnp.concatenate([piece.reshape(-1, LANES), entries], axis=0)
+
+    both = jnp.stack([for_lev(0)] + [swap(for_lev(k), "lev", n_lev, k) for k in range(1, n_lev)])
+    split = n_lat * levels
+    return (
+        both[:, :split].reshape(n_lev, n_lat, levels, LANES),
+        both[:, split:].reshape(n_lev, n_lat, -1, LANES),
     )
 
 
@@ -493,7 +497,7 @@
         + [pltpu.SemaphoreType.DMA((len(given),))],
     )(*given)
     recv = exchange(fields)
-    others = gather_others(sizes, winds, entries)
+    winds, entries = gather_others(sizes, winds[:, :levels], entries)
     solved_0, regimes, first, last = call(
         functools.partial(unpack_solve_kernel, n_lev),
         [(4 * total, 256), (8, 256), (2 * total, LANES), (2 * total, LANES)],
@@ -504,7 +508,7 @@
         functools.partial(unpack_winds_kernel, n_lev),
         [(2 * total, 256), (total, LANES), (total, LANES)],
         [(2 * total, 256)],
-    )(others)
+    )(winds)
     wind_rims = rims(first, last)
     solved_1, first, last = call(
         functools.partial(transport_solve_kernel, lat_count),
@@ -512,8 +516,8 @@
         [(6, total, 384), (2, 4 * total, 384), (4 * total, 256)],
     )(solved_0, winds, regimes, kz_inverse, *wind_rims, east_0, west_0)
     east_1, west_1 = rims(first, last)
-    (sums,) = call(functools.partial(footprint_kernel, n_lev, wind_rows), [(8, 64)])(
-        others, solved_0, solved_1
+    (sums,) = call(functools.partial(footprint_kernel, n_lev, 0), [(8, 64)])(
+        entries, solved_0, solved_1
     )
     (back,) = call(
         functools.partial(transport_pack_kernel, lat_count, n_lev),

time: 80.6 us -> 79.1 us (0.981)
  waiting for transfers between devices: 21.9 us -> 19.8 us
    ppermute x6, waiting for transfers between devices: 14.9 us -> 12.5 us  [swap(): return lax.ppermute(x, axis, [(i, i ^ k) for i in range(count)])]
  transfers between devices with their start and end apart: 13 -> 13, of which waited for: 8 -> 7; matrix products, arithmetic and copies ran while one was open for 0% -> 1% of each run, Pallas kernels for 5% -> 5%
where the time goes in v3:
time: 79.1 us; the launch traced here: 78.7 us
  blocking collectives  19.9 us (25%)
  waiting for transfers between devices  19.8 us (25%)
  Pallas kernels  18.9 us (24%)
  starting transfers between devices  18.1 us (23%)
  local copies, waits for them, and re-layouts  1.13 us (1%)
  between operations  0.92 us (1%)
    all_to_all x1, blocking collectives, exchange(): return lax.all_to_all(x, AXES, split_axis=0, concat_axis=0, tiled=True)  19.9 us
    ppermute x6, waiting for transfers between devices, swap(): return lax.ppermute(x, axis, [(i, i ^ k) for i in range(count)])  12.5 us
    all_to_all x1, starting transfers between devices, exchange(): return lax.all_to_all(x, AXES, split_axis=0, concat_axis=0, tiled=True)  7.5 us
    ppermute x6, starting transfers between devices, swap(): return lax.ppermute(x, axis, [(i, i ^ k) for i in range(count)])  6.88 us
    ppermute x3, waiting for transfers between devices, rims(): lax.ppermute(last, RING, to_east)  4.85 us
    pallas_call x1, Pallas kernels, regrouped(): call(functools.partial(transport_solve_kernel, lat_count), [(4 * total, 2...  4.78 us
    pallas_call x1, Pallas kernels, regrouped(): call(functools.partial(transport_pack_kernel, lat_count, n_lev), [(group,...  4.36 us
    pallas_call x1, Pallas kernels, regrouped(): pl.pallas_call(functools.partial(pack_kernel, place), in_specs=[pl.BlockS...  3.66 us
  transfers between devices with their start and end apart: 13, of which 7 were waited for; matrix products, arithmetic and copies ran while one was open for 1% of the time, Pallas kernels for 5%

profile of v3, /device:TPU:0, one launch (start us, length us, event | category | flops | bytes accessed | tf_op | source)
XLA Modules:
  0.0 78.7 jit_solution(10825819662634920744)
XLA Ops:
  0.6 3.7 %shard_map.104 = (f32[16,72,128]{2,1,0:T(8,128)}, f32[16,40,128]{2,1,0:T(8,128)}, f32[12,128]{1,0:T(8,128)}) custom-call(f32[4,34,4,256]{3,2,1,0:T(4,128)} %refs_0_.1, f32[34,4,256]{2,1,0:T(4,128)} %refs_1_.1, f32[34,4,256]{2,1,0:T(4,128)} %refs_2_.1, s32[2,4,256]{2,1,0:T(4,128)} %refs_3_.1, s32[1,1,512]{2,1,0:T(1,128)} %refs_4_.1, s32[1,512]{1,0:T(1,128)} %bitcast.47, ...), custom_call_target="tpu_custom_call" | custom-call | tf_op jit(solution)/shard_map/pallas_call | solution.py:487
  4.3 7.5 %all-to-all-start = ((f32[16,72,128]{2,1,0:T(8,128)}), f32[16,72,128]{2,1,0:T(8,128)S(1)}, u32[]{:S(2)}, u32[]{:S(2)}) async-start(f32[16,72,128]{2,1,0:T(8,128)} %get-tuple-element.15), calls=%async_computation | async-start | bytes 1179648 | tf_op jit(solution)/shard_map/all_to_all | solution.py:476
  11.9 0.7 copy-done.2
  12.7 0.5 collective-permute-start
  13.1 1.7 %collective-permute-start.1 = (f32[148,128]{1,0:T(8,128)S(1)}, f32[148,128]{1,0:T(8,128)S(1)}, u32[]{:S(2)}, u32[]{:S(2)}) collective-permute-start(f32[148,128]{1,0:T(8,128)S(1)} %get-tuple-element.42), channel_id=1, source_target_pairs={{0,16},{8,24},{16,0},{24,8},{1,17},{9,25},{17,1},{25,9},{2,18},{10... | collective-permute-start | bytes 227336 | tf_op jit(solution)/shard_map/ppermute | solution.py:434
  14.8 7.3 %collective-permute-done.1 = f32[148,128]{1,0:T(8,128)S(1)} collective-permute-done((f32[148,128]{1,0:T(8,128)S(1)}, f32[148,128]{1,0:T(8,128)S(1)}, u32[]{:S(2)}, u32[]{:S(2)}) %collective-permute-start.1) | collective-permute-done | bytes 75808 | tf_op jit(solution)/shard_map/ppermute | solution.py:434
  22.1 1.3 %collective-permute-done.2 = f32[148,128]{1,0:T(8,128)S(1)} collective-permute-done((f32[148,128]{1,0:T(8,128)S(1)}, f32[148,128]{1,0:T(8,128)S(1)}, u32[]{:S(2)}, u32[]{:S(2)}) %collective-permute-start.2) | collective-permute-done | bytes 75808 | tf_op jit(solution)/shard_map/ppermute | solution.py:434
  23.7 0.2 collective-permute-start.3
  23.9 4.5 %collective-permute-start.4 = (f32[184,128]{1,0:T(8,128)S(1)}, f32[184,128]{1,0:T(8,128)S(1)}, u32[]{:S(2)}, u32[]{:S(2)}) collective-permute-start(f32[184,128]{1,0:T(8,128)S(1)} %get-tuple-element.38), channel_id=1, source_target_pairs={{0,4},{2,6},{4,0},{6,2},{1,5},{3,7},{5,1},{7,3},{8,12},{10,14},{12... | collective-permute-start | bytes 282632 | tf_op jit(solution)/shard_map/ppermute | solution.py:434
  28.4 0.5 all-to-all-done.recv
  28.9 1.6 %shard_map.105 = (f32[544,256]{1,0:T(8,128)S(1)}, f32[8,256]{1,0:T(8,128)S(1)}, f32[272,128]{1,0:T(8,128)S(1)}, f32[272,128]{1,0:T(8,128)S(1)}) custom-call(f32[16,72,128]{2,1,0:T(8,128)S(1)} %all-to-all-done.recv, f32[4,136,136]{2,1,0:T(8,128)S(1)} %copy-done), custom_call_target="tpu_custom_call" | custom-call | tf_op jit(solution)/shard_map/pallas_call | solution.py:501
  30.5 1.6 %collective-permute-start.8 = (f32[272,128]{1,0:T(8,128)S(1)}, f32[272,128]{1,0:T(8,128)S(1)}, u32[]{:S(2)}, u32[]{:S(2)}) collective-permute-start(f32[272,128]{1,0:T(8,128)S(1)} %get-tuple-element.23), channel_id=1, source_target_pairs={{0,1},{8,0},{2,8},{10,2},{4,10},{12,4},{6,12},{14,6},{22,14},{30,2... | collective-permute-start | bytes 417800 | tf_op jit(solution)/shard_map/ppermute | solution.py:479
  32.1 4.0 %collective-permute-done.4 = f32[184,128]{1,0:T(8,128)S(1)} collective-permute-done((f32[184,128]{1,0:T(8,128)S(1)}, f32[184,128]{1,0:T(8,128)S(1)}, u32[]{:S(2)}, u32[]{:S(2)}) %collective-permute-start.4) | collective-permute-done | bytes 94240 | tf_op jit(solution)/shard_map/ppermute | solution.py:434
  36.3 0.4 shard_map.106
  36.7 1.5 %collective-permute-start.6 = (f32[136,128]{1,0:T(8,128)S(1)}, f32[136,128]{1,0:T(8,128)S(1)}, u32[]{:S(2)}, u32[]{:S(2)}) collective-permute-start(f32[136,128]{1,0:T(8,128)S(1)} %get-tuple-element.21), channel_id=1, source_target_pairs={{0,1},{8,0},{2,8},{10,2},{4,10},{12,4},{6,12},{14,6},{22,14},{30,2... | collective-permute-start | bytes 208904 | tf_op jit(solution)/shard_map/ppermute | solution.py:479
  38.2 1.9 %collective-permute-done.6.wind_east.from_east_0 = f32[136,128]{1,0:T(8,128)S(1)} collective-permute-done((f32[136,128]{1,0:T(8,128)S(1)}, f32[136,128]{1,0:T(8,128)S(1)}, u32[]{:S(2)}, u32[]{:S(2)}) %collective-permute-start.6) | collective-permute-done | bytes 69664 | tf_op jit(solution)/shard_map/ppermute | solution.py:479
  40.2 2.4 %collective-permute-done.7.wind_west.from_west_0 = f32[136,128]{1,0:T(8,128)S(1)} collective-permute-done((f32[136,128]{1,0:T(8,128)S(1)}, f32[136,128]{1,0:T(8,128)S(1)}, u32[]{:S(2)}, u32[]{:S(2)}) %collective-permute-start.7) | collective-permute-done | bytes 69664 | tf_op jit(solution)/shard_map/ppermute | solution.py:479
  42.5 4.8 %shard_map.107 = (f32[544,256]{1,0:T(8,128)S(1)}, f32[272,128]{1,0:T(8,128)S(1)}, f32[272,128]{1,0:T(8,128)S(1)}) custom-call(f32[544,256]{1,0:T(8,128)S(1)} %get-tuple-element.16.field.hour_0, f32[272,256]{1,0:T(8,128)S(1)} %get-tuple-element.19.winds, f32[8,256]{1,0:T(8,128)S(1)} %get-tuple-element.20.regimes, f32[4,136,136]{2,1,0:T(8,128)S(1)} %copy-done, ...), custom_call_target="tpu_custom_call" | custom-call | tf_op jit(solution)/shard_map/pallas_call | solution.py:513
  47.4 0.5 collective-permute-start.11
  48.0 2.2 %shard_map.108.sums = f32[8,64]{1,0:T(8,128)S(1)} custom-call(f32[4,4,12,128]{3,2,1,0:T(8,128)S(1)} %copy.23.others, f32[544,256]{1,0:T(8,128)S(1)} %get-tuple-element.16.field.hour_0, f32[544,256]{1,0:T(8,128)S(1)} %get-tuple-element.25.hour_1.field), custom_call_target="tpu_custom_call" | custom-call | tf_op jit(solution)/shard_map/pallas_call | solution.py:519
  50.2 2.5 %collective-permute-done.11.from_west = f32[272,128]{1,0:T(8,128)S(1)} collective-permute-done((f32[272,128]{1,0:T(8,128)S(1)}, f32[272,128]{1,0:T(8,128)S(1)}, u32[]{:S(2)}, u32[]{:S(2)}) %collective-permute-start.11) | collective-permute-done | bytes 139296 | tf_op jit(solution)/shard_map/ppermute | solution.py:479
  52.7 4.4 %shard_map.109 = f32[16,72,128]{2,1,0:T(8,128)S(1)} custom-call(f32[544,256]{1,0:T(8,128)S(1)} %get-tuple-element.25.hour_1.field, f32[272,256]{1,0:T(8,128)S(1)} %get-tuple-element.19.winds, f32[136,128]{1,0:T(8,128)S(1)} %collective-permute-done.6.wind_east.from_east_0, f32[136,128]{1,0:T(8,128)S(1)} %collective-permute-done.7.wind_west.from_west_0, ...), custom_call_target="tpu_custom_call" | custom-call | tf_op jit(solution)/shard_map/pallas_call | solution.py:522
  57.1 19.9 %all_to_all.10.recv = f32[16,72,128]{2,1,0:T(8,128)S(1)} all-to-all(f32[16,72,128]{2,1,0:T(8,128)S(1)} %shard_map.109), channel_id=1, replica_groups=mesh['lat'=4,'lev'=4,'lon'=2] {'lat','lev'}, dimensions={0} | all-to-all | bytes 1179648 | tf_op jit(solution)/shard_map/all_to_all | solution.py:476
  76.9 1.8 %shard_map.110 = (f32[4,34,4,256]{3,2,1,0:T(4,128)}, f32[2,4,1,4]{3,2,1,0:T(1,128)}) custom-call(f32[16,72,128]{2,1,0:T(8,128)S(1)} %all_to_all.10.recv), custom_call_target="tpu_custom_call" | custom-call | tf_op jit(solution)/shard_map/pallas_call | solution.py:527
  (41 shorter events, 0.7 us)
Async XLA Ops:
  4.3 7.5 %copy-start.1 = (f32[16,40,128]{2,1,0:T(8,128)S(1)}, f32[16,40,128]{2,1,0:T(8,128)}, u32[]{:S(2)}) copy-start(f32[16,40,128]{2,1,0:T(8,128)} %get-tuple-element.17) | copy-start | bytes 983044
  4.3 24.6 %all-to-all-start = ((f32[16,72,128]{2,1,0:T(8,128)}), f32[16,72,128]{2,1,0:T(8,128)S(1)}, u32[]{:S(2)}, u32[]{:S(2)}) async-start(f32[16,72,128]{2,1,0:T(8,128)} %get-tuple-element.15), calls=%async_computation | async-start | bytes 1179648 | tf_op jit(solution)/shard_map/all_to_all | solution.py:476
  11.9 0.7 copy-start.2
  12.7 2.1 %collective-permute-start = (f32[148,128]{1,0:T(8,128)S(1)}, f32[148,128]{1,0:T(8,128)S(1)}, u32[]{:S(2)}, u32[]{:S(2)}) collective-permute-start(f32[148,128]{1,0:T(8,128)S(1)} %get-tuple-element.41), channel_id=1, source_target_pairs={{0,8},{8,0},{16,24},{24,16},{1,9},{9,1},{17,25},{25,17},{2,10},{10... | collective-permute-start | bytes 227336 | tf_op jit(solution)/shard_map/ppermute | solution.py:434
  13.1 9.0 %collective-permute-start.1 = (f32[148,128]{1,0:T(8,128)S(1)}, f32[148,128]{1,0:T(8,128)S(1)}, u32[]{:S(2)}, u32[]{:S(2)}) collective-permute-start(f32[148,128]{1,0:T(8,128)S(1)} %get-tuple-element.42), channel_id=1, source_target_pairs={{0,16},{8,24},{16,0},{24,8},{1,17},{9,25},{17,1},{25,9},{2,18},{10... | collective-permute-start | bytes 227336 | tf_op jit(solution)/shard_map/ppermute | solution.py:434
  14.8 8.5 %collective-permute-start.2 = (f32[148,128]{1,0:T(8,128)S(1)}, f32[148,128]{1,0:T(8,128)S(1)}, u32[]{:S(2)}, u32[]{:S(2)}) collective-permute-start(f32[148,128]{1,0:T(8,128)S(1)} %get-tuple-element.43), channel_id=1, source_target_pairs={{0,24},{8,16},{16,8},{24,0},{1,25},{9,17},{17,9},{25,1},{2,26},{10... | collective-permute-start | bytes 227336 | tf_op jit(solution)/shard_map/ppermute | solution.py:434
  23.6 5.3 %copy-start = (f32[4,136,136]{2,1,0:T(8,128)S(1)}, f32[4,136,136]{2,1,0:T(8,128)}, u32[]{:S(2)}) copy-start(f32[4,136,136]{2,1,0:T(8,128)} %kz.3) | copy-start | bytes 887812
  23.7 8.4 %collective-permute-start.3 = (f32[184,128]{1,0:T(8,128)S(1)}, f32[184,128]{1,0:T(8,128)S(1)}, u32[]{:S(2)}, u32[]{:S(2)}) collective-permute-start(f32[184,128]{1,0:T(8,128)S(1)} %get-tuple-element.37), channel_id=1, source_target_pairs={{0,2},{2,0},{4,6},{6,4},{1,3},{3,1},{5,7},{7,5},{8,10},{10,8},{12,... | collective-permute-start | bytes 282632 | tf_op jit(solution)/shard_map/ppermute | solution.py:434
  23.9 12.1 %collective-permute-start.4 = (f32[184,128]{1,0:T(8,128)S(1)}, f32[184,128]{1,0:T(8,128)S(1)}, u32[]{:S(2)}, u32[]{:S(2)}) collective-permute-start(f32[184,128]{1,0:T(8,128)S(1)} %get-tuple-element.38), channel_id=1, source_target_pairs={{0,4},{2,6},{4,0},{6,2},{1,5},{3,7},{5,1},{7,3},{8,12},{10,14},{12... | collective-permute-start | bytes 282632 | tf_op jit(solution)/shard_map/ppermute | solution.py:434
  28.4 7.6 %collective-permute-start.5 = (f32[184,128]{1,0:T(8,128)S(1)}, f32[184,128]{1,0:T(8,128)S(1)}, u32[]{:S(2)}, u32[]{:S(2)}) collective-permute-start(f32[184,128]{1,0:T(8,128)S(1)} %get-tuple-element.39), channel_id=1, source_target_pairs={{0,6},{2,4},{4,2},{6,0},{1,7},{3,5},{5,3},{7,1},{8,14},{10,12},{12... | collective-permute-start | bytes 282632 | tf_op jit(solution)/shard_map/ppermute | solution.py:434
  30.5 12.0 %collective-permute-start.8 = (f32[272,128]{1,0:T(8,128)S(1)}, f32[272,128]{1,0:T(8,128)S(1)}, u32[]{:S(2)}, u32[]{:S(2)}) collective-permute-start(f32[272,128]{1,0:T(8,128)S(1)} %get-tuple-element.23), channel_id=1, source_target_pairs={{0,1},{8,0},{2,8},{10,2},{4,10},{12,4},{6,12},{14,6},{22,14},{30,2... | collective-permute-start | bytes 417800 | tf_op jit(solution)/shard_map/ppermute | solution.py:479
  32.1 10.4 %collective-permute-start.9 = (f32[272,128]{1,0:T(8,128)S(1)}, f32[272,128]{1,0:T(8,128)S(1)}, u32[]{:S(2)}, u32[]{:S(2)}) collective-permute-start(f32[272,128]{1,0:T(8,128)S(1)} %get-tuple-element.24), channel_id=1, source_target_pairs={{0,8},{8,2},{2,10},{10,4},{4,12},{12,6},{6,14},{14,22},{22,30},{30... | collective-permute-start | bytes 417800 | tf_op jit(solution)/shard_map/ppermute | solution.py:479
  36.7 3.5 %collective-permute-start.6 = (f32[136,128]{1,0:T(8,128)S(1)}, f32[136,128]{1,0:T(8,128)S(1)}, u32[]{:S(2)}, u32[]{:S(2)}) collective-permute-start(f32[136,128]{1,0:T(8,128)S(1)} %get-tuple-element.21), channel_id=1, source_target_pairs={{0,1},{8,0},{2,8},{10,2},{4,10},{12,4},{6,12},{14,6},{22,14},{30,2... | collective-permute-start | bytes 208904 | tf_op jit(solution)/shard_map/ppermute | solution.py:479
  38.2 4.3 %collective-permute-start.7 = (f32[136,128]{1,0:T(8,128)S(1)}, f32[136,128]{1,0:T(8,128)S(1)}, u32[]{:S(2)}, u32[]{:S(2)}) collective-permute-start(f32[136,128]{1,0:T(8,128)S(1)} %get-tuple-element.22), channel_id=1, source_target_pairs={{0,8},{8,2},{2,10},{10,4},{4,12},{12,6},{6,14},{14,22},{22,30},{30... | collective-permute-start | bytes 208904 | tf_op jit(solution)/shard_map/ppermute | solution.py:479
  47.3 2.9 %collective-permute-start.10 = (f32[272,128]{1,0:T(8,128)S(1)}, f32[272,128]{1,0:T(8,128)S(1)}, u32[]{:S(2)}, u32[]{:S(2)}) collective-permute-start(f32[272,128]{1,0:T(8,128)S(1)} %get-tuple-element.26), channel_id=1, source_target_pairs={{0,1},{8,0},{2,8},{10,2},{4,10},{12,4},{6,12},{14,6},{22,14},{30,2... | collective-permute-start | bytes 417800 | tf_op jit(solution)/shard_map/ppermute | solution.py:479
  47.4 5.3 %collective-permute-start.11 = (f32[272,128]{1,0:T(8,128)S(1)}, f32[272,128]{1,0:T(8,128)S(1)}, u32[]{:S(2)}, u32[]{:S(2)}) collective-permute-start(f32[272,128]{1,0:T(8,128)S(1)} %get-tuple-element.27), channel_id=1, source_target_pairs={{0,8},{8,2},{2,10},{10,4},{4,12},{12,6},{6,14},{14,22},{22,30},{30... | collective-permute-start | bytes 417800 | tf_op jit(solution)/shard_map/ppermute | solution.py:479

commit v4 on v3

--- a/solution.py
+++ b/solution.py
@@ -13,7 +13,6 @@
 SPO = 4
 LANES = 128
 GRAIN = 16
-ENTRY_ROWS = 12
 F32 = jnp.float32
 BF16 = jnp.bfloat16
 AXES = ("lat", "lev")
@@ -101,9 +100,9 @@
 
 
 def pack_kernel(place, *refs):
-    count = (len(refs) - 4) // 2
-    given, outs = refs[:count], refs[count : count + 3]
-    held, sems = refs[count + 3 : -1], refs[-1]
+    count = (len(refs) - 3) // 2
+    given, outs = refs[:count], refs[count : count + 2]
+    held, sems = refs[count + 2 : -1], refs[-1]
     place = owners(place)
     copies = [
         pltpu.make_async_copy(a, b, sems.at[i]) for i, (a, b) in enumerate(zip(given, held))
@@ -111,7 +110,7 @@
     for copy in copies:
         copy.start()
     adj, east, north, regime, cell, owner, station, weight = held
-    fields, winds, entries = outs
+    fields, winds = outs
     levels = adj.shape[1]
     rows = adj.shape[2]
 
@@ -133,11 +132,11 @@
     place_pieces(srcs, fields, 2 * levels, 1)
     cells = cell[0].astype(F32)
     stations = (owner[...] * SPO + station[0]).astype(F32)
-    for k in range(4):
-        part = slice(k * LANES, (k + 1) * LANES)
-        entries[k : k + 1, :] = cells[:, part]
-        entries[4 + k : 5 + k, :] = stations[:, part]
-        entries[8 + k : 9 + k, :] = weight[0][:, part]
+    for g in range(fields.shape[0]):
+        k = g // (fields.shape[0] // 4)
+        for at, value in enumerate((cells, stations, weight[0])):
+            row = 2 * levels + 1 + at
+            fields[g, row : row + 1, :] = value[:, k * LANES : (k + 1) * LANES]
 
 
 def solve_columns(high, low, kz_high, kz_low, regime, levels):
@@ -199,9 +198,13 @@
     )
 
 
-def unpack_winds_kernel(n_lev, others, winds, first, last, field):
+def unpack_winds_kernel(n_lev, *refs):
+    pieces, (winds, first, last, field, others) = refs[:n_lev], refs[n_lev + 1 :]
     total = winds.shape[0] // 2
     levels = total // n_lev
+    for m in range(n_lev):
+        for k in range(others.shape[1]):
+            others[m, k] = pieces[m][k * levels : (k + 1) * levels, :]
     own_lat, own_lev = lax.axis_index("lat"), lax.axis_index("lev")
     for z in range(n_lev):
         for half in range(2):
@@ -319,13 +322,14 @@
     )
 
 
-def footprint_kernel(n_lev, entry_row, others, hour_0, hour_1, sums):
+def footprint_kernel(n_lev, quarters, hour_0, hour_1, sums):
     own_lat, own_lev = lax.axis_index("lat"), lax.axis_index("lev")
     chip, core = own_lat // 2, own_lat % 2
     step = jnp.where(chip % 2 == 0, own_lev, n_lev - 1 - own_lev)
     chunk = (chip * n_lev + step) * 2 + core
     odd = lax.axis_index("lon") % 2 == 1
-    first_lon = jnp.where(odd, others.shape[0] * others.shape[1] - 1 - chunk, chunk) * GRAIN
+    group = quarters.shape[1] // 3
+    first_lon = jnp.where(odd, group - 1 - chunk, chunk) * GRAIN
     total = hour_0.shape[0] // 4
     matrix = transpose_matrix()
     low = jnp.concatenate(
@@ -338,17 +342,16 @@
     cell_ids = lax.broadcasted_iota(jnp.int32, (GRAIN, 512), 0)
     level_ids = lax.broadcasted_iota(jnp.int32, (FOOT_LEVELS, 512), 0)
     station_ids = lax.broadcasted_iota(jnp.int32, (64, 512), 0)
-    for row in range(others.shape[0] * others.shape[1]):
-        z, a = (row % n_lev) ^ own_lev, (row // n_lev) ^ own_lat
+    for row in range(group):
 
         def entries(at):
             return jnp.concatenate(
-                [others[z, a, at + k : at + k + 1, :] for k in range(4)], axis=1
+                [quarters[k, 3 * row + at : 3 * row + at + 1, :] for k in range(4)], axis=1
             )
 
-        code = entries(entry_row).astype(jnp.int32)
-        station = entries(entry_row + 4).astype(jnp.int32)
-        weight = entries(entry_row + 8)
+        code = entries(0).astype(jnp.int32)
+        station = entries(1).astype(jnp.int32)
+        weight = entries(2)
         cells = ((code & 255) - first_lon == cell_ids).astype(F32).astype(BF16)
         picked = mm(parts[:, row * GRAIN : (row + 1) * GRAIN], cells)
         picked = (picked[:count] + picked[count : 2 * count]) + picked[2 * count :]
@@ -424,33 +427,27 @@
             stations[h, t, :, :] = line[:, at : at + 4]
 
 
-def gather_others(sizes, winds, entries):
+def swaps(x, axis, count, piece):
+    return [piece(x, 0)] + [
+        lax.ppermute(piece(x, k), axis, [(i, i ^ k) for i in range(count)])
+        for k in range(1, count)
+    ]
+
+
+def gather_winds(sizes, winds):
     n_lat, n_lev, _ = sizes
     own_lat, own_lev = lax.axis_index("lat"), lax.axis_index("lev")
     levels = winds.shape[1]
-    pieces = winds.reshape(n_lat, n_lev * levels, LANES)
-
-    def swap(x, axis, count, k):
-        return lax.ppermute(x, axis, [(i, i ^ k) for i in range(count)])
-
-    def for_lat(k):
-        piece = lax.dynamic_index_in_dim(pieces, own_lat ^ k, 0, keepdims=False)
-        return jnp.concatenate([piece, entries], axis=0)
-
-    here = jnp.stack([for_lat(0)] + [swap(for_lat(k), "lat", n_lat, k) for k in range(1, n_lat)])
-    pieces = here[:, : n_lev * levels].reshape(n_lat, n_lev, levels, LANES)
-    entries = here[:, n_lev * levels :].reshape(-1, LANES)
-
-    def for_lev(k):
-        piece = lax.dynamic_index_in_dim(pieces, own_lev ^ k, 1, keepdims=False)
-        return jnp.concatenate([piece.reshape(-1, LANES), entries], axis=0)
-
-    both = jnp.stack([for_lev(0)] + [swap(for_lev(k), "lev", n_lev, k) for k in range(1, n_lev)])
-    split = n_lat * levels
-    return (
-        both[:, :split].reshape(n_lev, n_lat, levels, LANES),
-        both[:, split:].reshape(n_lev, n_lat, -1, LANES),
-    )
+
+    def for_lat(x, k):
+        return lax.dynamic_index_in_dim(x, own_lat ^ k, 0, keepdims=False)
+
+    def for_lev(x, k):
+        return lax.dynamic_index_in_dim(x, own_lev ^ k, 1, keepdims=False).reshape(-1, LANES)
+
+    here = swaps(winds.reshape(n_lat, n_lev * levels, LANES), "lat", n_lat, for_lat)
+    here = jnp.stack(here).reshape(n_lat, n_lev, levels, LANES)
+    return swaps(here, "lev", n_lev, for_lev)
 
 
 def call(kernel, outs, scratch=()):
@@ -480,24 +477,26 @@
 
     out_rows = 2 * levels + 1
     out_rows += -out_rows % 8
+    in_rows = 2 * levels + 4
+    in_rows += -in_rows % 8
     wind_rows = levels + -levels % 8
     given = (
         adjoint, wind_east, wind_north, kz_regime, fp_cell, fp_owner.reshape(1, -1), fp_station, fp_weight
     )
-    fields, winds, entries = pl.pallas_call(
+    fields, winds = pl.pallas_call(
         functools.partial(pack_kernel, place),
         in_specs=[pl.BlockSpec(memory_space=pltpu.HBM)] * len(given),
         out_shape=[
             jax.ShapeDtypeStruct(shape, F32)
             for shape in (
-                (group, out_rows, LANES), (group, wind_rows, LANES), (ENTRY_ROWS, LANES)
+                (group, in_rows, LANES), (group, wind_rows, LANES)
             )
         ],
         scratch_shapes=[pltpu.VMEM(x.shape, x.dtype) for x in given]
         + [pltpu.SemaphoreType.DMA((len(given),))],
     )(*given)
     recv = exchange(fields)
-    winds, entries = gather_others(sizes, winds[:, :levels], entries)
+    winds = gather_winds(sizes, winds[:, :levels])
     solved_0, regimes, first, last = call(
         functools.partial(unpack_solve_kernel, n_lev),
         [(4 * total, 256), (8, 256), (2 * total, LANES), (2 * total, LANES)],
@@ -507,16 +506,18 @@
     winds, first, last = call(
         functools.partial(unpack_winds_kernel, n_lev),
         [(2 * total, 256), (total, LANES), (total, LANES)],
-        [(2 * total, 256)],
-    )(winds)
+        [(2 * total, 256), (n_lev, n_lat, levels, LANES)],
+    )(*winds, regimes)
     wind_rims = rims(first, last)
+    entries = recv[:, 2 * levels + 1 : 2 * levels + 4].reshape(-1, LANES)
+    entries = jnp.stack(swaps(entries, "lat", n_lat, lambda x, k: x))
     solved_1, first, last = call(
         functools.partial(transport_solve_kernel, lat_count),
         [(4 * total, 256), (2 * total, LANES), (2 * total, LANES)],
         [(6, total, 384), (2, 4 * total, 384), (4 * total, 256)],
     )(solved_0, winds, regimes, kz_inverse, *wind_rims, east_0, west_0)
     east_1, west_1 = rims(first, last)
-    (sums,) = call(functools.partial(footprint_kernel, n_lev, 0), [(8, 64)])(
+    (sums,) = call(functools.partial(footprint_kernel, n_lev), [(8, 64)])(
         entries, solved_0, solved_1
     )
     (back,) = call(
@@ -661,6 +662,7 @@
         and n_lat * n_lev == 16
         and levels * n_lev == kz_shape[1]
         and kz_shape[1] % 8 == 0
+        and levels % 2 == 0
         and entries == 512
     )
 

time: 79.1 us -> 78.5 us (level)
  starting transfers between devices: 18.1 us -> 19.3 us
  waiting for transfers between devices: 19.8 us -> 18.8 us
  local copies, waits for them, and re-layouts: 1.13 us -> 0.2 us
    ppermute x6 -> x9, waiting for transfers between devices: 12.5 us -> 9.46 us  [swaps(): lax.ppermute(piece(x, k), axis, [(i, i ^ k) for i in range(count)])]
    all_to_all x1, waiting for transfers between devices: 0.47 us -> 3.2 us  [exchange(): return lax.all_to_all(x, AXES, split_axis=0, concat_axis=0, tiled=True)]
    ppermute x6 -> x9, starting transfers between devices: 6.88 us -> 7.3 us  [swaps(): lax.ppermute(piece(x, k), axis, [(i, i ^ k) for i in range(count)])]
  transfers between devices with their start and end apart: 13 -> 16, of which waited for: 7 -> 6; matrix products, arithmetic and copies ran while one was open for 1% -> 1% of each run, Pallas kernels for 5% -> 12%
where the time goes in v4:
time: 78.5 us; the launch traced here: 78.2 us
  blocking collectives  19.9 us (25%)
  starting transfers between devices  19.3 us (25%)
  Pallas kernels  18.9 us (24%)
  waiting for transfers between devices  18.8 us (24%)
  between operations  0.9 us (1%)
    all_to_all x1, blocking collectives, exchange(): return lax.all_to_all(x, AXES, split_axis=0, concat_axis=0, tiled=True)  19.9 us
    ppermute x9, waiting for transfers between devices, swaps(): lax.ppermute(piece(x, k), axis, [(i, i ^ k) for i in range(count)])  9.46 us
    all_to_all x1, starting transfers between devices, exchange(): return lax.all_to_all(x, AXES, split_axis=0, concat_axis=0, tiled=True)  7.5 us
    ppermute x9, starting transfers between devices, swaps(): lax.ppermute(piece(x, k), axis, [(i, i ^ k) for i in range(count)])  7.3 us
    pallas_call x1, Pallas kernels, regrouped(): call(functools.partial(transport_solve_kernel, lat_count), [(4 * total, 2...  4.75 us
    ppermute x3, waiting for transfers between devices, rims(): lax.ppermute(last, RING, to_east)  4.61 us
    pallas_call x1, Pallas kernels, regrouped(): call(functools.partial(transport_pack_kernel, lat_count, n_lev), [(group,...  4.36 us
    ppermute x3, starting transfers between devices, rims(): lax.ppermute(first, RING, to_west)  3.73 us
  transfers between devices with their start and end apart: 16, of which 6 were waited for; matrix products, arithmetic and copies ran while one was open for 1% of the time, Pallas kernels for 12%

profile of v4, /device:TPU:0, one launch (start us, length us, event | category | flops | bytes accessed | tf_op | source)
XLA Modules:
  0.0 78.2 jit_solution(13912759647590436416)
XLA Ops:
  0.6 3.7 %shard_map.104 = (f32[16,72,128]{2,1,0:T(8,128)}, f32[16,40,128]{2,1,0:T(8,128)}) custom-call(f32[4,34,4,256]{3,2,1,0:T(4,128)} %refs_0_.1, f32[34,4,256]{2,1,0:T(4,128)} %refs_1_.1, f32[34,4,256]{2,1,0:T(4,128)} %refs_2_.1, s32[2,4,256]{2,1,0:T(4,128)} %refs_3_.1, s32[1,1,512]{2,1,0:T(1,128)} %refs_4_.1, s32[1,512]{1,0:T(1,128)} %bitcast.31, ...), custom_call_target="tpu_custom_call" | custom-call | tf_op jit(solution)/shard_map/pallas_call | solution.py:486
  4.4 7.5 %all-to-all-start = ((f32[16,72,128]{2,1,0:T(8,128)}), f32[16,72,128]{2,1,0:T(8,128)S(1)}, u32[]{:S(2)}, u32[]{:S(2)}) async-start(f32[16,72,128]{2,1,0:T(8,128)} %get-tuple-element.14), calls=%async_computation | async-start | bytes 1179648 | tf_op jit(solution)/shard_map/all_to_all | solution.py:473
  12.0 1.7 %collective-permute-start.2 = (f32[136,128]{1,0:T(8,128)S(1)}, f32[136,128]{1,0:T(8,128)S(1)}, u32[]{:S(2)}, u32[]{:S(2)}) collective-permute-start(f32[136,128]{1,0:T(8,128)S(1)} %get-tuple-element.31), channel_id=1, source_target_pairs={{0,24},{8,16},{16,8},{24,0},{1,25},{9,17},{17,9},{25,1},{2,26},{10... | collective-permute-start | bytes 208904 | tf_op jit(solution)/shard_map/ppermute | solution.py:432
  13.7 0.4 collective-permute-start.1
  14.1 5.9 %collective-permute-done.2 = f32[136,128]{1,0:T(8,128)S(1)} collective-permute-done((f32[136,128]{1,0:T(8,128)S(1)}, f32[136,128]{1,0:T(8,128)S(1)}, u32[]{:S(2)}, u32[]{:S(2)}) %collective-permute-start.2) | collective-permute-done | bytes 69664 | tf_op jit(solution)/shard_map/ppermute | solution.py:432
  20.0 3.5 %collective-permute-done.1 = f32[136,128]{1,0:T(8,128)S(1)} collective-permute-done((f32[136,128]{1,0:T(8,128)S(1)}, f32[136,128]{1,0:T(8,128)S(1)}, u32[]{:S(2)}, u32[]{:S(2)}) %collective-permute-start.1) | collective-permute-done | bytes 69664 | tf_op jit(solution)/shard_map/ppermute | solution.py:432
  23.5 0.3 pad_maximum_fusion
  23.9 4.1 %collective-permute-start.5 = (f32[136,128]{1,0:T(8,128)S(1)}, f32[136,128]{1,0:T(8,128)S(1)}, u32[]{:S(2)}, u32[]{:S(2)}) collective-permute-start(f32[136,128]{1,0:T(8,128)S(1)} %reshape.42), channel_id=1, source_target_pairs={{0,6},{2,4},{4,2},{6,0},{1,7},{3,5},{5,3},{7,1},{8,14},{10,12},{12... | collective-permute-start | bytes 208904 | tf_op jit(solution)/shard_map/ppermute | solution.py:432
  28.1 0.6 collective-permute-start.3
  28.7 3.2 %all-to-all-done.recv = f32[16,72,128]{2,1,0:T(8,128)S(1)} async-done(((f32[16,72,128]{2,1,0:T(8,128)}), f32[16,72,128]{2,1,0:T(8,128)S(1)}, u32[]{:S(2)}, u32[]{:S(2)}) %all-to-all-start) | async-done | bytes 589856 | tf_op jit(solution)/shard_map/all_to_all | solution.py:473
  31.9 1.6 %shard_map.105 = (f32[544,256]{1,0:T(8,128)S(1)}, f32[8,256]{1,0:T(8,128)S(1)}, f32[272,128]{1,0:T(8,128)S(1)}, f32[272,128]{1,0:T(8,128)S(1)}) custom-call(f32[16,72,128]{2,1,0:T(8,128)S(1)} %all-to-all-done.recv, f32[4,136,136]{2,1,0:T(8,128)S(1)} %copy-done), custom_call_target="tpu_custom_call" | custom-call | tf_op jit(solution)/shard_map/pallas_call | solution.py:500
  33.6 1.6 %collective-permute-start.8 = (f32[272,128]{1,0:T(8,128)S(1)}, f32[272,128]{1,0:T(8,128)S(1)}, u32[]{:S(2)}, u32[]{:S(2)}) collective-permute-start(f32[272,128]{1,0:T(8,128)S(1)} %get-tuple-element.21), channel_id=1, source_target_pairs={{0,1},{8,0},{2,8},{10,2},{4,10},{12,4},{6,12},{14,6},{22,14},{30,2... | collective-permute-start | bytes 417800 | tf_op jit(solution)/shard_map/ppermute | solution.py:476
  35.2 0.4 shard_map.106
  35.6 2.1 %collective-permute-start.6 = (f32[136,128]{1,0:T(8,128)S(1)}, f32[136,128]{1,0:T(8,128)S(1)}, u32[]{:S(2)}, u32[]{:S(2)}) collective-permute-start(f32[136,128]{1,0:T(8,128)S(1)} %get-tuple-element.19), channel_id=1, source_target_pairs={{0,1},{8,0},{2,8},{10,2},{4,10},{12,4},{6,12},{14,6},{22,14},{30,2... | collective-permute-start | bytes 208904 | tf_op jit(solution)/shard_map/ppermute | solution.py:476
  37.7 0.4 collective-permute-start.14
  38.1 1.5 %collective-permute-done.6.wind_east.from_east_0 = f32[136,128]{1,0:T(8,128)S(1)} collective-permute-done((f32[136,128]{1,0:T(8,128)S(1)}, f32[136,128]{1,0:T(8,128)S(1)}, u32[]{:S(2)}, u32[]{:S(2)}) %collective-permute-start.6) | collective-permute-done | bytes 69664 | tf_op jit(solution)/shard_map/ppermute | solution.py:476
  39.6 2.4 %collective-permute-done.7.wind_west.from_west_0 = f32[136,128]{1,0:T(8,128)S(1)} collective-permute-done((f32[136,128]{1,0:T(8,128)S(1)}, f32[136,128]{1,0:T(8,128)S(1)}, u32[]{:S(2)}, u32[]{:S(2)}) %collective-permute-start.7) | collective-permute-done | bytes 69664 | tf_op jit(solution)/shard_map/ppermute | solution.py:476
  42.0 4.8 %shard_map.107 = (f32[544,256]{1,0:T(8,128)S(1)}, f32[272,128]{1,0:T(8,128)S(1)}, f32[272,128]{1,0:T(8,128)S(1)}) custom-call(f32[544,256]{1,0:T(8,128)S(1)} %get-tuple-element.15.field.hour_0, f32[272,256]{1,0:T(8,128)S(1)} %get-tuple-element.18.winds, f32[8,256]{1,0:T(8,128)S(1)} %get-tuple-element.17.refs_4_.regimes, f32[4,136,136]{2,1,0:T(8,128)S(1)} %copy-done, ...), custom_call_target="tpu_custom_call" | custom-call | tf_op jit(solution)/shard_map/pallas_call | solution.py:514
  46.9 0.7 collective-permute-start.11
  47.7 2.2 %shard_map.108.sums = f32[8,64]{1,0:T(8,128)S(1)} custom-call(f32[4,48,128]{2,1,0:T(8,128)S(1)} %pad_maximum_fusion.1.quarters, f32[544,256]{1,0:T(8,128)S(1)} %get-tuple-element.15.field.hour_0, f32[544,256]{1,0:T(8,128)S(1)} %get-tuple-element.23.hour_1.field), custom_call_target="tpu_custom_call" | custom-call | tf_op jit(solution)/shard_map/pallas_call | solution.py:520
  49.9 2.2 %collective-permute-done.11.from_west = f32[272,128]{1,0:T(8,128)S(1)} collective-permute-done((f32[272,128]{1,0:T(8,128)S(1)}, f32[272,128]{1,0:T(8,128)S(1)}, u32[]{:S(2)}, u32[]{:S(2)}) %collective-permute-start.11) | collective-permute-done | bytes 139296 | tf_op jit(solution)/shard_map/ppermute | solution.py:476
  52.2 4.4 %shard_map.109 = f32[16,72,128]{2,1,0:T(8,128)S(1)} custom-call(f32[544,256]{1,0:T(8,128)S(1)} %get-tuple-element.23.hour_1.field, f32[272,256]{1,0:T(8,128)S(1)} %get-tuple-element.18.winds, f32[136,128]{1,0:T(8,128)S(1)} %collective-permute-done.6.wind_east.from_east_0, f32[136,128]{1,0:T(8,128)S(1)} %collective-permute-done.7.wind_west.from_west_0, ...), custom_call_target="tpu_custom_call" | custom-call | tf_op jit(solution)/shard_map/pallas_call | solution.py:523
  56.5 19.9 %all_to_all.10.recv = f32[16,72,128]{2,1,0:T(8,128)S(1)} all-to-all(f32[16,72,128]{2,1,0:T(8,128)S(1)} %shard_map.109), channel_id=1, replica_groups=mesh['lat'=4,'lev'=4,'lon'=2] {'lat','lev'}, dimensions={0} | all-to-all | bytes 1179648 | tf_op jit(solution)/shard_map/all_to_all | solution.py:473
  76.4 1.8 %shard_map.110 = (f32[4,34,4,256]{3,2,1,0:T(4,128)}, f32[2,4,1,4]{3,2,1,0:T(1,128)}) custom-call(f32[16,72,128]{2,1,0:T(8,128)S(1)} %all_to_all.10.recv), custom_call_target="tpu_custom_call" | custom-call | tf_op jit(solution)/shard_map/pallas_call | solution.py:528
  (36 shorter events, 0.4 us)
Async XLA Ops:
  4.3 7.5 %copy-start.1 = (f32[16,40,128]{2,1,0:T(8,128)S(1)}, f32[16,40,128]{2,1,0:T(8,128)}, u32[]{:S(2)}) copy-start(f32[16,40,128]{2,1,0:T(8,128)} %get-tuple-element.16) | copy-start | bytes 983044
  4.4 27.6 %all-to-all-start = ((f32[16,72,128]{2,1,0:T(8,128)}), f32[16,72,128]{2,1,0:T(8,128)S(1)}, u32[]{:S(2)}, u32[]{:S(2)}) async-start(f32[16,72,128]{2,1,0:T(8,128)} %get-tuple-element.14), calls=%async_computation | async-start | bytes 1179648 | tf_op jit(solution)/shard_map/all_to_all | solution.py:473
  12.0 8.0 %collective-permute-start.2 = (f32[136,128]{1,0:T(8,128)S(1)}, f32[136,128]{1,0:T(8,128)S(1)}, u32[]{:S(2)}, u32[]{:S(2)}) collective-permute-start(f32[136,128]{1,0:T(8,128)S(1)} %get-tuple-element.31), channel_id=1, source_target_pairs={{0,24},{8,16},{16,8},{24,0},{1,25},{9,17},{17,9},{25,1},{2,26},{10... | collective-permute-start | bytes 208904 | tf_op jit(solution)/shard_map/ppermute | solution.py:432
  13.7 9.8 %collective-permute-start.1 = (f32[136,128]{1,0:T(8,128)S(1)}, f32[136,128]{1,0:T(8,128)S(1)}, u32[]{:S(2)}, u32[]{:S(2)}) collective-permute-start(f32[136,128]{1,0:T(8,128)S(1)} %get-tuple-element.32), channel_id=1, source_target_pairs={{0,16},{8,24},{16,0},{24,8},{1,17},{9,25},{17,1},{25,9},{2,18},{10... | collective-permute-start | bytes 208904 | tf_op jit(solution)/shard_map/ppermute | solution.py:432
  14.1 9.4 %collective-permute-start = (f32[136,128]{1,0:T(8,128)S(1)}, f32[136,128]{1,0:T(8,128)S(1)}, u32[]{:S(2)}, u32[]{:S(2)}) collective-permute-start(f32[136,128]{1,0:T(8,128)S(1)} %get-tuple-element.33), channel_id=1, source_target_pairs={{0,8},{8,0},{16,24},{24,16},{1,9},{9,1},{17,25},{25,17},{2,10},{10... | collective-permute-start | bytes 208904 | tf_op jit(solution)/shard_map/ppermute | solution.py:432
  23.8 8.1 %copy-start = (f32[4,136,136]{2,1,0:T(8,128)S(1)}, f32[4,136,136]{2,1,0:T(8,128)}, u32[]{:S(2)}) copy-start(f32[4,136,136]{2,1,0:T(8,128)} %kz.3) | copy-start | bytes 887812
  23.9 11.3 %collective-permute-start.5 = (f32[136,128]{1,0:T(8,128)S(1)}, f32[136,128]{1,0:T(8,128)S(1)}, u32[]{:S(2)}, u32[]{:S(2)}) collective-permute-start(f32[136,128]{1,0:T(8,128)S(1)} %reshape.42), channel_id=1, source_target_pairs={{0,6},{2,4},{4,2},{6,0},{1,7},{3,5},{5,3},{7,1},{8,14},{10,12},{12... | collective-permute-start | bytes 208904 | tf_op jit(solution)/shard_map/ppermute | solution.py:432
  28.0 7.2 %collective-permute-start.4 = (f32[136,128]{1,0:T(8,128)S(1)}, f32[136,128]{1,0:T(8,128)S(1)}, u32[]{:S(2)}, u32[]{:S(2)}) collective-permute-start(f32[136,128]{1,0:T(8,128)S(1)} %reshape.41), channel_id=1, source_target_pairs={{0,4},{2,6},{4,0},{6,2},{1,5},{3,7},{5,1},{7,3},{8,12},{10,14},{12... | collective-permute-start | bytes 208904 | tf_op jit(solution)/shard_map/ppermute | solution.py:432
  28.1 7.1 %collective-permute-start.3 = (f32[136,128]{1,0:T(8,128)S(1)}, f32[136,128]{1,0:T(8,128)S(1)}, u32[]{:S(2)}, u32[]{:S(2)}) collective-permute-start(f32[136,128]{1,0:T(8,128)S(1)} %reshape.40), channel_id=1, source_target_pairs={{0,2},{2,0},{4,6},{6,4},{1,3},{3,1},{5,7},{7,5},{8,10},{10,8},{12,... | collective-permute-start | bytes 208904 | tf_op jit(solution)/shard_map/ppermute | solution.py:432
  33.6 8.5 %collective-permute-start.8 = (f32[272,128]{1,0:T(8,128)S(1)}, f32[272,128]{1,0:T(8,128)S(1)}, u32[]{:S(2)}, u32[]{:S(2)}) collective-permute-start(f32[272,128]{1,0:T(8,128)S(1)} %get-tuple-element.21), channel_id=1, source_target_pairs={{0,1},{8,0},{2,8},{10,2},{4,10},{12,4},{6,12},{14,6},{22,14},{30,2... | collective-permute-start | bytes 417800 | tf_op jit(solution)/shard_map/ppermute | solution.py:476
  35.1 6.9 %collective-permute-start.9 = (f32[272,128]{1,0:T(8,128)S(1)}, f32[272,128]{1,0:T(8,128)S(1)}, u32[]{:S(2)}, u32[]{:S(2)}) collective-permute-start(f32[272,128]{1,0:T(8,128)S(1)} %get-tuple-element.22), channel_id=1, source_target_pairs={{0,8},{8,2},{2,10},{10,4},{4,12},{12,6},{6,14},{14,22},{22,30},{30... | collective-permute-start | bytes 417800 | tf_op jit(solution)/shard_map/ppermute | solution.py:476
  35.6 4.0 %collective-permute-start.6 = (f32[136,128]{1,0:T(8,128)S(1)}, f32[136,128]{1,0:T(8,128)S(1)}, u32[]{:S(2)}, u32[]{:S(2)}) collective-permute-start(f32[136,128]{1,0:T(8,128)S(1)} %get-tuple-element.19), channel_id=1, source_target_pairs={{0,1},{8,0},{2,8},{10,2},{4,10},{12,4},{6,12},{14,6},{22,14},{30,2... | collective-permute-start | bytes 208904 | tf_op jit(solution)/shard_map/ppermute | solution.py:476
  37.7 4.3 %collective-permute-start.7 = (f32[136,128]{1,0:T(8,128)S(1)}, f32[136,128]{1,0:T(8,128)S(1)}, u32[]{:S(2)}, u32[]{:S(2)}) collective-permute-start(f32[136,128]{1,0:T(8,128)S(1)} %get-tuple-element.20), channel_id=1, source_target_pairs={{0,8},{8,2},{2,10},{10,4},{4,12},{12,6},{6,14},{14,22},{22,30},{30... | collective-permute-start | bytes 208904 | tf_op jit(solution)/shard_map/ppermute | solution.py:476
  37.7 9.9 %collective-permute-start.14 = (f32[48,128]{1,0:T(8,128)S(1)}, f32[48,128]{1,0:T(8,128)S(1)}, u32[]{:S(2)}, u32[]{:S(2)}) collective-permute-start(f32[48,128]{1,0:T(8,128)S(1)} %reshape.43), channel_id=1, source_target_pairs={{0,24},{8,16},{16,8},{24,0},{1,25},{9,17},{17,9},{25,1},{2,26},{10... | collective-permute-start | bytes 73736 | tf_op jit(solution)/shard_map/ppermute | solution.py:432
  39.6 8.0 %collective-permute-start.13 = (f32[48,128]{1,0:T(8,128)S(1)}, f32[48,128]{1,0:T(8,128)S(1)}, u32[]{:S(2)}, u32[]{:S(2)}) collective-permute-start(f32[48,128]{1,0:T(8,128)S(1)} %reshape.43), channel_id=1, source_target_pairs={{0,16},{8,24},{16,0},{24,8},{1,17},{9,25},{17,1},{25,9},{2,18},{10... | collective-permute-start | bytes 73736 | tf_op jit(solution)/shard_map/ppermute | solution.py:432
  42.0 5.6 %collective-permute-start.12 = (f32[48,128]{1,0:T(8,128)S(1)}, f32[48,128]{1,0:T(8,128)S(1)}, u32[]{:S(2)}, u32[]{:S(2)}) collective-permute-start(f32[48,128]{1,0:T(8,128)S(1)} %reshape.43), channel_id=1, source_target_pairs={{0,8},{8,0},{16,24},{24,16},{1,9},{9,1},{17,25},{25,17},{2,10},{10... | collective-permute-start | bytes 73736 | tf_op jit(solution)/shard_map/ppermute | solution.py:432
  46.8 3.1 %collective-permute-start.10 = (f32[272,128]{1,0:T(8,128)S(1)}, f32[272,128]{1,0:T(8,128)S(1)}, u32[]{:S(2)}, u32[]{:S(2)}) collective-permute-start(f32[272,128]{1,0:T(8,128)S(1)} %get-tuple-element.24), channel_id=1, source_target_pairs={{0,1},{8,0},{2,8},{10,2},{4,10},{12,4},{6,12},{14,6},{22,14},{30,2... | collective-permute-start | bytes 417800 | tf_op jit(solution)/shard_map/ppermute | solution.py:476
  46.9 5.3 %collective-permute-start.11 = (f32[272,128]{1,0:T(8,128)S(1)}, f32[272,128]{1,0:T(8,128)S(1)}, u32[]{:S(2)}, u32[]{:S(2)}) collective-permute-start(f32[272,128]{1,0:T(8,128)S(1)} %get-tuple-element.25), channel_id=1, source_target_pairs={{0,8},{8,2},{2,10},{10,4},{4,12},{12,6},{6,14},{14,22},{22,30},{30... | collective-permute-start | bytes 417800 | tf_op jit(solution)/shard_map/ppermute | solution.py:476

commit v5 on v4

--- a/solution.py
+++ b/solution.py
@@ -107,7 +107,11 @@
     copies = [
         pltpu.make_async_copy(a, b, sems.at[i]) for i, (a, b) in enumerate(zip(given, held))
     ]
-    for copy in copies:
+    halves = [
+        pltpu.make_async_copy(given[0].at[part], held[0].at[part], sems.at[at])
+        for part, at in ((pl.ds(0, 2), 0), (pl.ds(2, 2), count))
+    ]
+    for copy in halves + copies[1:]:
         copy.start()
     adj, east, north, regime, cell, owner, station, weight = held
     fields, winds = outs
@@ -120,8 +124,8 @@
             for j, piece in enumerate(swap_grains([s[:, lanes] for s in srcs])):
                 out[place[half * 8 + j], first : first + count, :] = piece
 
-    copies[0].wait()
     for pair in range(2):
+        halves[pair].wait()
         srcs = [adj[2 * pair + k, :, r, :] for k in range(2) for r in range(rows)]
         place_pieces(srcs, fields, pair * levels, levels)
     for copy in copies[1:]:
@@ -365,13 +369,15 @@
     sums[...] = jnp.sum(acc.reshape(count // FOOT_LEVELS, FOOT_LEVELS, 64), axis=1)
 
 
+def face_kernel(lat_count, winds, wind_east, wind_west, _, faces):
+    face_weights(lat_count, winds, wind_east, wind_west, winds.shape[0] // 2, faces)
+
+
 def transport_pack_kernel(
-    lat_count, n_lev, field, winds, from_east_0, from_west_0, from_east, from_west, sums, out,
-    faces, buffers, moved,
+    lat_count, n_lev, field, faces, from_east, from_west, sums, out, buffers, moved
 ):
-    total = winds.shape[0] // 2
+    total = faces.shape[1]
     levels = total // n_lev
-    face_weights(lat_count, winds, from_east_0, from_west_0, total, faces)
     transport(lat_count, field, from_east, from_west, faces, total, buffers, moved)
     matrix = transpose_matrix()
     for pair in range(2):
@@ -493,8 +499,9 @@
             )
         ],
         scratch_shapes=[pltpu.VMEM(x.shape, x.dtype) for x in given]
-        + [pltpu.SemaphoreType.DMA((len(given),))],
-    )(*given)
+        + [pltpu.SemaphoreType.DMA((len(given) + 1,))],
+        compiler_params=pltpu.CompilerParams(vmem_limit_bytes=48 * 1024 * 1024),
+    )(*[pltpu.with_memory_space_constraint(x, pltpu.HBM) for x in given])
     recv = exchange(fields)
     winds = gather_winds(sizes, winds[:, :levels])
     solved_0, regimes, first, last = call(
@@ -520,11 +527,14 @@
     (sums,) = call(functools.partial(footprint_kernel, n_lev), [(8, 64)])(
         entries, solved_0, solved_1
     )
+    (faces,) = call(functools.partial(face_kernel, lat_count), [(6, total, 384)])(
+        winds, *wind_rims, first
+    )
     (back,) = call(
         functools.partial(transport_pack_kernel, lat_count, n_lev),
         [(group, out_rows, LANES)],
-        [(6, total, 384), (2, 4 * total, 384), (4 * total, 256)],
-    )(solved_1, winds, *wind_rims, east_1, west_1, sums)
+        [(2, 4 * total, 384), (4 * total, 256)],
+    )(solved_1, faces, east_1, west_1, sums)
     final, stations = call(
         functools.partial(unpack_kernel, place), [adjoint.shape, (HOURS, 4, 1, SPO)]
     )(exchange(back))

time: 78.5 us -> 77.8 us (level)
  waiting for transfers between devices: 18.8 us -> 17.1 us
  starting transfers between devices: 19.3 us -> 20.4 us
    ppermute x3, waiting for transfers between devices: 4.61 us -> 2.88 us  [rims(): lax.ppermute(last, RING, to_east)]
    ppermute x3, starting transfers between devices: 3.73 us -> 5.17 us  [rims(): lax.ppermute(first, RING, to_west)]
where the time goes in v5:
time: 77.8 us; the launch traced here: 77.6 us
  starting transfers between devices  20.4 us (26%)
  blocking collectives  19.9 us (26%)
  Pallas kernels  18.9 us (24%)
  waiting for transfers between devices  17.1 us (22%)
  between operations  0.88 us (1%)
    all_to_all x1, blocking collectives, exchange(): return lax.all_to_all(x, AXES, split_axis=0, concat_axis=0, tiled=True)  19.9 us
    ppermute x9, waiting for transfers between devices, swaps(): lax.ppermute(piece(x, k), axis, [(i, i ^ k) for i in range(count)])  9.45 us
    all_to_all x1, starting transfers between devices, exchange(): return lax.all_to_all(x, AXES, split_axis=0, concat_axis=0, tiled=True)  7.37 us
    ppermute x9, starting transfers between devices, swaps(): lax.ppermute(piece(x, k), axis, [(i, i ^ k) for i in range(count)])  7.3 us
    ppermute x3, starting transfers between devices, rims(): lax.ppermute(first, RING, to_west)  5.17 us
    pallas_call x1, Pallas kernels, regrouped(): call(functools.partial(transport_solve_kernel, lat_count), [(4 * total, 2...  4.75 us
    pallas_call x1, Pallas kernels, regrouped(): call(functools.partial(transport_pack_kernel, lat_count, n_lev), [(group,...  4.21 us
    pallas_call x1, Pallas kernels, regrouped(): pl.pallas_call(functools.partial(pack_kernel, place), in_specs=[pl.BlockS...  3.62 us
  transfers between devices with their start and end apart: 16, of which 6 were waited for; matrix products, arithmetic and copies ran while one was open for 1% of the time, Pallas kernels for 12%

profile of v5, /device:TPU:0, one launch (start us, length us, event | category | flops | bytes accessed | tf_op | source)
XLA Modules:
  0.0 77.6 jit_solution(1378452375348792580)
XLA Ops:
  0.6 3.6 %shard_map.104 = (f32[16,72,128]{2,1,0:T(8,128)}, f32[16,40,128]{2,1,0:T(8,128)S(1)}) custom-call(f32[4,34,4,256]{3,2,1,0:T(4,128)} %refs_0_.1, f32[34,4,256]{2,1,0:T(4,128)} %refs_1_.1, f32[34,4,256]{2,1,0:T(4,128)} %refs_2_.1, s32[2,4,256]{2,1,0:T(4,128)} %refs_3_.1, s32[1,1,512]{2,1,0:T(1,128)} %refs_4_.1, s32[1,512]{1,0:T(1,128)} %bitcast.31, ...), custom_call_target="tpu_custom_call" | custom-call | tf_op jit(solution)/shard_map/pallas_call | solution.py:492
  4.3 7.4 %all-to-all-start = ((f32[16,72,128]{2,1,0:T(8,128)}), f32[16,72,128]{2,1,0:T(8,128)S(1)}, u32[]{:S(2)}, u32[]{:S(2)}) async-start(f32[16,72,128]{2,1,0:T(8,128)} %get-tuple-element.14), calls=%async_computation | async-start | bytes 1179648 | tf_op jit(solution)/shard_map/all_to_all | solution.py:479
  11.7 1.7 %collective-permute-start.2 = (f32[136,128]{1,0:T(8,128)S(1)}, f32[136,128]{1,0:T(8,128)S(1)}, u32[]{:S(2)}, u32[]{:S(2)}) collective-permute-start(f32[136,128]{1,0:T(8,128)S(1)} %get-tuple-element.31), channel_id=1, source_target_pairs={{0,24},{8,16},{16,8},{24,0},{1,25},{9,17},{17,9},{25,1},{2,26},{10... | collective-permute-start | bytes 208904 | tf_op jit(solution)/shard_map/ppermute | solution.py:438
  13.5 0.4 collective-permute-start.1
  13.8 5.9 %collective-permute-done.2 = f32[136,128]{1,0:T(8,128)S(1)} collective-permute-done((f32[136,128]{1,0:T(8,128)S(1)}, f32[136,128]{1,0:T(8,128)S(1)}, u32[]{:S(2)}, u32[]{:S(2)}) %collective-permute-start.2) | collective-permute-done | bytes 69664 | tf_op jit(solution)/shard_map/ppermute | solution.py:438
  19.7 3.5 %collective-permute-done.1 = f32[136,128]{1,0:T(8,128)S(1)} collective-permute-done((f32[136,128]{1,0:T(8,128)S(1)}, f32[136,128]{1,0:T(8,128)S(1)}, u32[]{:S(2)}, u32[]{:S(2)}) %collective-permute-start.1) | collective-permute-done | bytes 69664 | tf_op jit(solution)/shard_map/ppermute | solution.py:438
  23.6 4.1 %collective-permute-start.5 = (f32[136,128]{1,0:T(8,128)S(1)}, f32[136,128]{1,0:T(8,128)S(1)}, u32[]{:S(2)}, u32[]{:S(2)}) collective-permute-start(f32[136,128]{1,0:T(8,128)S(1)} %reshape.42), channel_id=1, source_target_pairs={{0,6},{2,4},{4,2},{6,0},{1,7},{3,5},{5,3},{7,1},{8,14},{10,12},{12... | collective-permute-start | bytes 208904 | tf_op jit(solution)/shard_map/ppermute | solution.py:438
  27.9 0.6 collective-permute-start.3
  28.5 3.2 %all-to-all-done.recv = f32[16,72,128]{2,1,0:T(8,128)S(1)} async-done(((f32[16,72,128]{2,1,0:T(8,128)}), f32[16,72,128]{2,1,0:T(8,128)S(1)}, u32[]{:S(2)}, u32[]{:S(2)}) %all-to-all-start) | async-done | bytes 589856 | tf_op jit(solution)/shard_map/all_to_all | solution.py:479
  31.7 1.6 %shard_map.105 = (f32[544,256]{1,0:T(8,128)S(1)}, f32[8,256]{1,0:T(8,128)S(1)}, f32[272,128]{1,0:T(8,128)S(1)}, f32[272,128]{1,0:T(8,128)S(1)}) custom-call(f32[16,72,128]{2,1,0:T(8,128)S(1)} %all-to-all-done.recv, f32[4,136,136]{2,1,0:T(8,128)S(1)} %copy-done), custom_call_target="tpu_custom_call" | custom-call | tf_op jit(solution)/shard_map/pallas_call | solution.py:507
  33.3 1.6 %collective-permute-start.8 = (f32[272,128]{1,0:T(8,128)S(1)}, f32[272,128]{1,0:T(8,128)S(1)}, u32[]{:S(2)}, u32[]{:S(2)}) collective-permute-start(f32[272,128]{1,0:T(8,128)S(1)} %get-tuple-element.21), channel_id=1, source_target_pairs={{0,1},{8,0},{2,8},{10,2},{4,10},{12,4},{6,12},{14,6},{22,14},{30,2... | collective-permute-start | bytes 417800 | tf_op jit(solution)/shard_map/ppermute | solution.py:482
  35.0 0.4 shard_map.106
  35.4 2.1 %collective-permute-start.6 = (f32[136,128]{1,0:T(8,128)S(1)}, f32[136,128]{1,0:T(8,128)S(1)}, u32[]{:S(2)}, u32[]{:S(2)}) collective-permute-start(f32[136,128]{1,0:T(8,128)S(1)} %get-tuple-element.19), channel_id=1, source_target_pairs={{0,1},{8,0},{2,8},{10,2},{4,10},{12,4},{6,12},{14,6},{22,14},{30,2... | collective-permute-start | bytes 208904 | tf_op jit(solution)/shard_map/ppermute | solution.py:482
  37.5 0.4 collective-permute-start.14
  37.9 1.5 %collective-permute-done.6.wind_east = f32[136,128]{1,0:T(8,128)S(1)} collective-permute-done((f32[136,128]{1,0:T(8,128)S(1)}, f32[136,128]{1,0:T(8,128)S(1)}, u32[]{:S(2)}, u32[]{:S(2)}) %collective-permute-start.6) | collective-permute-done | bytes 69664 | tf_op jit(solution)/shard_map/ppermute | solution.py:482
  39.4 2.4 %collective-permute-done.7.wind_west = f32[136,128]{1,0:T(8,128)S(1)} collective-permute-done((f32[136,128]{1,0:T(8,128)S(1)}, f32[136,128]{1,0:T(8,128)S(1)}, u32[]{:S(2)}, u32[]{:S(2)}) %collective-permute-start.7) | collective-permute-done | bytes 69664 | tf_op jit(solution)/shard_map/ppermute | solution.py:482
  41.8 4.8 %shard_map.107 = (f32[544,256]{1,0:T(8,128)S(1)}, f32[272,128]{1,0:T(8,128)S(1)}, f32[272,128]{1,0:T(8,128)S(1)}) custom-call(f32[544,256]{1,0:T(8,128)S(1)} %get-tuple-element.15.field.hour_0, f32[272,256]{1,0:T(8,128)S(1)} %get-tuple-element.18.winds, f32[8,256]{1,0:T(8,128)S(1)} %get-tuple-element.17.refs_4_.regimes, f32[4,136,136]{2,1,0:T(8,128)S(1)} %copy-done, ...), custom_call_target="tpu_custom_call" | custom-call | tf_op jit(solution)/shard_map/pallas_call | solution.py:521
  46.6 0.6 collective-permute-start.11
  47.1 1.5 %collective-permute-start.10 = (f32[272,128]{1,0:T(8,128)S(1)}, f32[272,128]{1,0:T(8,128)S(1)}, u32[]{:S(2)}, u32[]{:S(2)}) collective-permute-start(f32[272,128]{1,0:T(8,128)S(1)} %get-tuple-element.24._), channel_id=1, source_target_pairs={{0,1},{8,0},{2,8},{10,2},{4,10},{12,4},{6,12},{14,6},{22,14},{30,2... | collective-permute-start | bytes 417800 | tf_op jit(solution)/shard_map/ppermute | solution.py:482
  48.7 2.2 %shard_map.109.sums = f32[8,64]{1,0:T(8,128)S(1)} custom-call(f32[4,48,128]{2,1,0:T(8,128)S(1)} %pad_maximum_fusion.1.quarters, f32[544,256]{1,0:T(8,128)S(1)} %get-tuple-element.15.field.hour_0, f32[544,256]{1,0:T(8,128)S(1)} %get-tuple-element.23.hour_1.field), custom_call_target="tpu_custom_call" | custom-call | tf_op jit(solution)/shard_map/pallas_call | solution.py:527
  51.2 0.5 collective-permute-done.11.from_west
  51.7 4.2 %shard_map.110 = f32[16,72,128]{2,1,0:T(8,128)S(1)} custom-call(f32[544,256]{1,0:T(8,128)S(1)} %get-tuple-element.23.hour_1.field, f32[6,136,384]{2,1,0:T(8,128)S(1)} %shard_map.108.faces, f32[272,128]{1,0:T(8,128)S(1)} %collective-permute-done.10.from_east, f32[272,128]{1,0:T(8,128)S(1)} %collective-permute-done.11.from_west, f32[8,64]{1,0:T(8,128)S(1)} %shard_map.109.sums), custom_call_target="tpu_custom_call" | custom-call | tf_op jit(solution)/shard_map/pallas_call | solution.py:533
  55.9 19.9 %all_to_all.10.recv = f32[16,72,128]{2,1,0:T(8,128)S(1)} all-to-all(f32[16,72,128]{2,1,0:T(8,128)S(1)} %shard_map.110), channel_id=1, replica_groups=mesh['lat'=4,'lev'=4,'lon'=2] {'lat','lev'}, dimensions={0} | all-to-all | bytes 1179648 | tf_op jit(solution)/shard_map/all_to_all | solution.py:479
  75.8 1.8 %shard_map.111 = (f32[4,34,4,256]{3,2,1,0:T(4,128)}, f32[2,4,1,4]{3,2,1,0:T(1,128)}) custom-call(f32[16,72,128]{2,1,0:T(8,128)S(1)} %all_to_all.10.recv), custom_call_target="tpu_custom_call" | custom-call | tf_op jit(solution)/shard_map/pallas_call | solution.py:538
  (35 shorter events, 0.8 us)
Async XLA Ops:
  4.3 27.5 %all-to-all-start = ((f32[16,72,128]{2,1,0:T(8,128)}), f32[16,72,128]{2,1,0:T(8,128)S(1)}, u32[]{:S(2)}, u32[]{:S(2)}) async-start(f32[16,72,128]{2,1,0:T(8,128)} %get-tuple-element.14), calls=%async_computation | async-start | bytes 1179648 | tf_op jit(solution)/shard_map/all_to_all | solution.py:479
  11.7 20.0 %copy-start = (f32[4,136,136]{2,1,0:T(8,128)S(1)}, f32[4,136,136]{2,1,0:T(8,128)}, u32[]{:S(2)}) copy-start(f32[4,136,136]{2,1,0:T(8,128)} %kz.3) | copy-start | bytes 887812
  11.7 8.0 %collective-permute-start.2 = (f32[136,128]{1,0:T(8,128)S(1)}, f32[136,128]{1,0:T(8,128)S(1)}, u32[]{:S(2)}, u32[]{:S(2)}) collective-permute-start(f32[136,128]{1,0:T(8,128)S(1)} %get-tuple-element.31), channel_id=1, source_target_pairs={{0,24},{8,16},{16,8},{24,0},{1,25},{9,17},{17,9},{25,1},{2,26},{10... | collective-permute-start | bytes 208904 | tf_op jit(solution)/shard_map/ppermute | solution.py:438
  13.5 9.8 %collective-permute-start.1 = (f32[136,128]{1,0:T(8,128)S(1)}, f32[136,128]{1,0:T(8,128)S(1)}, u32[]{:S(2)}, u32[]{:S(2)}) collective-permute-start(f32[136,128]{1,0:T(8,128)S(1)} %get-tuple-element.32), channel_id=1, source_target_pairs={{0,16},{8,24},{16,0},{24,8},{1,17},{9,25},{17,1},{25,9},{2,18},{10... | collective-permute-start | bytes 208904 | tf_op jit(solution)/shard_map/ppermute | solution.py:438
  13.8 9.4 %collective-permute-start = (f32[136,128]{1,0:T(8,128)S(1)}, f32[136,128]{1,0:T(8,128)S(1)}, u32[]{:S(2)}, u32[]{:S(2)}) collective-permute-start(f32[136,128]{1,0:T(8,128)S(1)} %get-tuple-element.33), channel_id=1, source_target_pairs={{0,8},{8,0},{16,24},{24,16},{1,9},{9,1},{17,25},{25,17},{2,10},{10... | collective-permute-start | bytes 208904 | tf_op jit(solution)/shard_map/ppermute | solution.py:438
  23.6 11.3 %collective-permute-start.5 = (f32[136,128]{1,0:T(8,128)S(1)}, f32[136,128]{1,0:T(8,128)S(1)}, u32[]{:S(2)}, u32[]{:S(2)}) collective-permute-start(f32[136,128]{1,0:T(8,128)S(1)} %reshape.42), channel_id=1, source_target_pairs={{0,6},{2,4},{4,2},{6,0},{1,7},{3,5},{5,3},{7,1},{8,14},{10,12},{12... | collective-permute-start | bytes 208904 | tf_op jit(solution)/shard_map/ppermute | solution.py:438
  27.8 7.2 %collective-permute-start.4 = (f32[136,128]{1,0:T(8,128)S(1)}, f32[136,128]{1,0:T(8,128)S(1)}, u32[]{:S(2)}, u32[]{:S(2)}) collective-permute-start(f32[136,128]{1,0:T(8,128)S(1)} %reshape.41), channel_id=1, source_target_pairs={{0,4},{2,6},{4,0},{6,2},{1,5},{3,7},{5,1},{7,3},{8,12},{10,14},{12... | collective-permute-start | bytes 208904 | tf_op jit(solution)/shard_map/ppermute | solution.py:438
  27.9 7.1 %collective-permute-start.3 = (f32[136,128]{1,0:T(8,128)S(1)}, f32[136,128]{1,0:T(8,128)S(1)}, u32[]{:S(2)}, u32[]{:S(2)}) collective-permute-start(f32[136,128]{1,0:T(8,128)S(1)} %reshape.40), channel_id=1, source_target_pairs={{0,2},{2,0},{4,6},{6,4},{1,3},{3,1},{5,7},{7,5},{8,10},{10,8},{12,... | collective-permute-start | bytes 208904 | tf_op jit(solution)/shard_map/ppermute | solution.py:438
  33.3 8.5 %collective-permute-start.8 = (f32[272,128]{1,0:T(8,128)S(1)}, f32[272,128]{1,0:T(8,128)S(1)}, u32[]{:S(2)}, u32[]{:S(2)}) collective-permute-start(f32[272,128]{1,0:T(8,128)S(1)} %get-tuple-element.21), channel_id=1, source_target_pairs={{0,1},{8,0},{2,8},{10,2},{4,10},{12,4},{6,12},{14,6},{22,14},{30,2... | collective-permute-start | bytes 417800 | tf_op jit(solution)/shard_map/ppermute | solution.py:482
  34.9 6.9 %collective-permute-start.9 = (f32[272,128]{1,0:T(8,128)S(1)}, f32[272,128]{1,0:T(8,128)S(1)}, u32[]{:S(2)}, u32[]{:S(2)}) collective-permute-start(f32[272,128]{1,0:T(8,128)S(1)} %get-tuple-element.22), channel_id=1, source_target_pairs={{0,8},{8,2},{2,10},{10,4},{4,12},{12,6},{6,14},{14,22},{22,30},{30... | collective-permute-start | bytes 417800 | tf_op jit(solution)/shard_map/ppermute | solution.py:482
  35.4 4.0 %collective-permute-start.6 = (f32[136,128]{1,0:T(8,128)S(1)}, f32[136,128]{1,0:T(8,128)S(1)}, u32[]{:S(2)}, u32[]{:S(2)}) collective-permute-start(f32[136,128]{1,0:T(8,128)S(1)} %get-tuple-element.19), channel_id=1, source_target_pairs={{0,1},{8,0},{2,8},{10,2},{4,10},{12,4},{6,12},{14,6},{22,14},{30,2... | collective-permute-start | bytes 208904 | tf_op jit(solution)/shard_map/ppermute | solution.py:482
  37.5 4.3 %collective-permute-start.7 = (f32[136,128]{1,0:T(8,128)S(1)}, f32[136,128]{1,0:T(8,128)S(1)}, u32[]{:S(2)}, u32[]{:S(2)}) collective-permute-start(f32[136,128]{1,0:T(8,128)S(1)} %get-tuple-element.20), channel_id=1, source_target_pairs={{0,8},{8,2},{2,10},{10,4},{4,12},{12,6},{6,14},{14,22},{22,30},{30... | collective-permute-start | bytes 208904 | tf_op jit(solution)/shard_map/ppermute | solution.py:482
  37.5 11.2 %collective-permute-start.14 = (f32[48,128]{1,0:T(8,128)S(1)}, f32[48,128]{1,0:T(8,128)S(1)}, u32[]{:S(2)}, u32[]{:S(2)}) collective-permute-start(f32[48,128]{1,0:T(8,128)S(1)} %reshape.43), channel_id=1, source_target_pairs={{0,24},{8,16},{16,8},{24,0},{1,25},{9,17},{17,9},{25,1},{2,26},{10... | collective-permute-start | bytes 73736 | tf_op jit(solution)/shard_map/ppermute | solution.py:438
  39.4 9.3 %collective-permute-start.13 = (f32[48,128]{1,0:T(8,128)S(1)}, f32[48,128]{1,0:T(8,128)S(1)}, u32[]{:S(2)}, u32[]{:S(2)}) collective-permute-start(f32[48,128]{1,0:T(8,128)S(1)} %reshape.43), channel_id=1, source_target_pairs={{0,16},{8,24},{16,0},{24,8},{1,17},{9,25},{17,1},{25,9},{2,18},{10... | collective-permute-start | bytes 73736 | tf_op jit(solution)/shard_map/ppermute | solution.py:438
  41.8 6.9 %collective-permute-start.12 = (f32[48,128]{1,0:T(8,128)S(1)}, f32[48,128]{1,0:T(8,128)S(1)}, u32[]{:S(2)}, u32[]{:S(2)}) collective-permute-start(f32[48,128]{1,0:T(8,128)S(1)} %reshape.43), channel_id=1, source_target_pairs={{0,8},{8,0},{16,24},{24,16},{1,9},{9,1},{17,25},{25,17},{2,10},{10... | collective-permute-start | bytes 73736 | tf_op jit(solution)/shard_map/ppermute | solution.py:438
  46.6 5.1 %collective-permute-start.11 = (f32[272,128]{1,0:T(8,128)S(1)}, f32[272,128]{1,0:T(8,128)S(1)}, u32[]{:S(2)}, u32[]{:S(2)}) collective-permute-start(f32[272,128]{1,0:T(8,128)S(1)} %get-tuple-element.25), channel_id=1, source_target_pairs={{0,8},{8,2},{2,10},{10,4},{4,12},{12,6},{6,14},{14,22},{22,30},{30... | collective-permute-start | bytes 417800 | tf_op jit(solution)/shard_map/ppermute | solution.py:482
  47.1 4.6 %collective-permute-start.10 = (f32[272,128]{1,0:T(8,128)S(1)}, f32[272,128]{1,0:T(8,128)S(1)}, u32[]{:S(2)}, u32[]{:S(2)}) collective-permute-start(f32[272,128]{1,0:T(8,128)S(1)} %get-tuple-element.24._), channel_id=1, source_target_pairs={{0,1},{8,0},{2,8},{10,2},{4,10},{12,4},{6,12},{14,6},{22,14},{30,2... | collective-permute-start | bytes 417800 | tf_op jit(solution)/shard_map/ppermute | solution.py:482

commit v6 on v5

--- a/solution.py
+++ b/solution.py
@@ -72,10 +72,11 @@
     )
 
 
-def transpose_matrix():
-    i = lax.broadcasted_iota(jnp.int32, (256, 256), 0)
-    j = lax.broadcasted_iota(jnp.int32, (256, 256), 1)
-    return ((i // 16 == j % 16) & (i % 16 == j // 16)).astype(F32).astype(BF16)
+def lane_matrix(back):
+    major = lax.broadcasted_iota(jnp.int32, (256, 256), 1 if back else 0)
+    work = lax.broadcasted_iota(jnp.int32, (256, 256), 0 if back else 1)
+    lon = (work % LANES) // GRAIN * 2 + work // LANES
+    return ((major // GRAIN == work % GRAIN) & (major % GRAIN == lon)).astype(F32).astype(BF16)
 
 
 def split_two(x):
@@ -157,10 +158,18 @@
 
 
 def rim_messages(top, bottom, first, last, rows):
-    half = LANES // 2
-    low = lane_ids(top.shape[0]) < half
-    first[rows, :] = jnp.where(low, top[:, :LANES], pltpu.roll(bottom[:, :LANES], half, 1))
-    last[rows, :] = jnp.where(low, pltpu.roll(top[:, LANES:], half, 1), bottom[:, LANES:])
+    pair = lane_ids(top.shape[0]) // (2 * GRAIN)
+    blocks = [top[:, :LANES], top[:, LANES:], bottom[:, :LANES], bottom[:, LANES:]]
+
+    def gathered(offset):
+        out = blocks[3] if offset == 3 else turned(blocks[3], (3 - offset) * 2 * GRAIN)
+        for k in range(3):
+            shift = (k - offset) * 2 * GRAIN
+            out = jnp.where(pair == k, turned(blocks[k], shift) if shift else blocks[k], out)
+        return out
+
+    first[rows, :] = gathered(0)
+    last[rows, :] = gathered(3)
 
 
 def unpack_solve_kernel(n_lev, recv, kz, solved, regimes, first, last, field):
@@ -186,7 +195,7 @@
         ]
         for k, value in enumerate(swap_halves(a, b)):
             field[base + k : base + k + 1, lanes] = value
-    matrix = transpose_matrix()
+    matrix = lane_matrix(False)
     regime = mm(field[base : base + 8, :].astype(BF16), matrix)
     regimes[...] = regime
     kz_high, kz_low = mixing(kz)
@@ -219,17 +228,21 @@
             for k, value in enumerate(swap_halves(a, b)):
                 base = k * total + z * levels
                 field[base : base + levels, lanes] = value
-    winds[...] = move_lanes(field[...], transpose_matrix())
+    winds[...] = move_lanes(field[...], lane_matrix(False))
     rim_messages(winds[0:total, :], winds[total:, :], first, last, slice(0, total))
 
 
 def rim_lanes(from_east, from_west, rows, upper):
     half = LANES // 2
     east, west = from_east[rows, :], from_west[rows, :]
-    low = lane_ids(east.shape[0]) < half
+    lane = lane_ids(east.shape[0])
     if upper:
-        return jnp.where(low, pltpu.roll(east, half, 1), west)
-    return jnp.where(low, east, pltpu.roll(west, half, 1))
+        both = jnp.where(lane < half, pltpu.roll(east, half, 1), west)
+    else:
+        both = jnp.where(lane < half, east, pltpu.roll(west, half, 1))
+    place = lane // GRAIN % 4
+    both = jnp.where(place == 1, turned(both, -GRAIN), jnp.where(place == 2, turned(both, GRAIN), both))
+    return both
 
 
 def columns(ref, rows):
@@ -245,14 +258,14 @@
 
 
 def stepped(blocks, shift):
-    count = len(blocks)
-    lane = lane_ids(blocks[0].shape[0])
-    moved = [turned(x, shift) for x in blocks]
+    even, odd, rim = blocks
+    lane = lane_ids(even.shape[0])
+    outer = turned(rim, shift)
     if shift > 0:
-        return [jnp.where(lane < shift, moved[i - 1], moved[i]) for i in range(count)]
-    return [
-        jnp.where(lane >= LANES + shift, moved[(i + 1) % count], moved[i]) for i in range(count)
-    ]
+        inner, edge = turned(odd, shift), lane < shift
+        return [jnp.where(edge, outer, inner), even, jnp.where(edge, inner, outer)]
+    inner, edge = turned(even, shift), lane >= LANES + shift
+    return [odd, jnp.where(edge, outer, inner), jnp.where(edge, inner, outer)]
 
 
 def face_weights(lat_count, winds, from_east, from_west, total, faces):
@@ -278,13 +291,36 @@
         faces[5, :, lanes] = before
 
 
-def transport(lat_count, field, east_rows, west_rows, faces, total, buffers, result):
+def first_sweep_kernel(lat_count, field, winds, swept):
+    total = winds.shape[0] // 2
+    lat = lane_ids(total) % lat_count
+    for i, north in enumerate(pair_columns(winds, slice(total, 2 * total))):
+        lanes = slice(i * LANES, (i + 1) * LANES)
+        north = jnp.where(lat == lat_count - 1, 0.0, north)
+        after = jnp.maximum(north, 0.0)
+        before = -jnp.minimum(jnp.where(lat == 0, 0.0, turned(north, 1)), 0.0)
+        stay = 1.0 - after - before
+        for t in range(4):
+            own = slice(t * total, (t + 1) * total)
+            f = field[own, lanes]
+            swept[own, lanes] = stay * f + after * turned(f, -1) + before * turned(f, 1)
+
+
+def transport(lat_count, field, east_rows, west_rows, faces, total, buffers, result, begun=False):
     for t in range(4):
         own = slice(t * total, (t + 1) * total)
         rim = slice((t % 2) * total, (t % 2 + 1) * total)
-        buffers[0, own, 0:256] = field[own, :]
-        buffers[0, own, 256:384] = rim_lanes(east_rows, west_rows, rim, t >= 2)
-    for step in range(2 * NSUB):
+        rim = rim_lanes(east_rows, west_rows, rim, t >= 2)
+        if begun:
+            lanes = slice(256, 384)
+            rim = (
+                faces[0, :, lanes] * rim
+                + faces[1, :, lanes] * turned(rim, -1)
+                + faces[2, :, lanes] * turned(rim, 1)
+            )
+        buffers[int(begun), own, 0:256] = field[own, :]
+        buffers[int(begun), own, 256:384] = rim
+    for step in range(int(begun), 2 * NSUB):
         last = step == 2 * NSUB - 1
         for t in range(4):
             own = slice(t * total, (t + 1) * total)
@@ -314,7 +350,7 @@
 ):
     total = kz.shape[1]
     face_weights(lat_count, winds, wind_east, wind_west, total, faces)
-    transport(lat_count, field, from_east, from_west, faces, total, buffers, moved)
+    transport(lat_count, field, from_east, from_west, faces, total, buffers, moved, True)
     kz_high, kz_low = mixing(kz)
     for t in range(4):
         high, low = split_two(moved[t * total : (t + 1) * total, :])
@@ -335,7 +371,7 @@
     group = quarters.shape[1] // 3
     first_lon = jnp.where(odd, group - 1 - chunk, chunk) * GRAIN
     total = hour_0.shape[0] // 4
-    matrix = transpose_matrix()
+    matrix = lane_matrix(True)
     low = jnp.concatenate(
         [h[t * total : t * total + FOOT_LEVELS, :] for h in (hour_0, hour_1) for t in range(4)],
         axis=0,
@@ -379,7 +415,7 @@
     total = faces.shape[1]
     levels = total // n_lev
     transport(lat_count, field, from_east, from_west, faces, total, buffers, moved)
-    matrix = transpose_matrix()
+    matrix = lane_matrix(True)
     for pair in range(2):
         for k in range(2):
             rows = slice((2 * pair + k) * total, (2 * pair + k + 1) * total)
@@ -516,13 +552,16 @@
         [(2 * total, 256), (n_lev, n_lat, levels, LANES)],
     )(*winds, regimes)
     wind_rims = rims(first, last)
+    (swept,) = call(functools.partial(first_sweep_kernel, lat_count), [(4 * total, 256)])(
+        solved_0, winds
+    )
     entries = recv[:, 2 * levels + 1 : 2 * levels + 4].reshape(-1, LANES)
     entries = jnp.stack(swaps(entries, "lat", n_lat, lambda x, k: x))
     solved_1, first, last = call(
         functools.partial(transport_solve_kernel, lat_count),
         [(4 * total, 256), (2 * total, LANES), (2 * total, LANES)],
         [(6, total, 384), (2, 4 * total, 384), (4 * total, 256)],
-    )(solved_0, winds, regimes, kz_inverse, *wind_rims, east_0, west_0)
+    )(swept, winds, regimes, kz_inverse, *wind_rims, east_0, west_0)
     east_1, west_1 = rims(first, last)
     (sums,) = call(functools.partial(footprint_kernel, n_lev), [(8, 64)])(
         entries, solved_0, solved_1

time: 77.8 us -> 77.7 us (level)
  waiting for transfers between devices: 17.1 us -> 16.2 us
  transfers between devices with their start and end apart: 16 -> 16, of which waited for: 6 -> 6; matrix products, arithmetic and copies ran while one was open for 1% -> 1% of each run, Pallas kernels for 12% -> 13%
where the time goes in v6:
time: 77.7 us; the launch traced here: 77.4 us
  starting transfers between devices  20.7 us (27%)
  blocking collectives  19.9 us (26%)
  Pallas kernels  19.2 us (25%)
  waiting for transfers between devices  16.2 us (21%)
  between operations  0.89 us (1%)
    all_to_all x1, blocking collectives, exchange(): return lax.all_to_all(x, AXES, split_axis=0, concat_axis=0, tiled=True)  19.9 us
    ppermute x9, waiting for transfers between devices, swaps(): lax.ppermute(piece(x, k), axis, [(i, i ^ k) for i in range(count)])  9.45 us
    ppermute x9, starting transfers between devices, swaps(): lax.ppermute(piece(x, k), axis, [(i, i ^ k) for i in range(count)])  7.61 us
    all_to_all x1, starting transfers between devices, exchange(): return lax.all_to_all(x, AXES, split_axis=0, concat_axis=0, tiled=True)  7.37 us
    ppermute x3, starting transfers between devices, rims(): lax.ppermute(first, RING, to_west)  5.17 us
    pallas_call x1, Pallas kernels, regrouped(): call(functools.partial(transport_solve_kernel, lat_count), [(4 * total, 2...  4.78 us
    pallas_call x1, Pallas kernels, regrouped(): call(functools.partial(transport_pack_kernel, lat_count, n_lev), [(group,...  3.93 us
    pallas_call x1, Pallas kernels, regrouped(): pl.pallas_call(functools.partial(pack_kernel, place), in_specs=[pl.BlockS...  3.62 us
  transfers between devices with their start and end apart: 16, of which 6 were waited for; matrix products, arithmetic and copies ran while one was open for 1% of the time, Pallas kernels for 13%

profile of v6, /device:TPU:0, one launch (start us, length us, event | category | flops | bytes accessed | tf_op | source)
XLA Modules:
  0.0 77.4 jit_solution(7757137606842682696)
XLA Ops:
  0.6 3.6 %shard_map.104 = (f32[16,72,128]{2,1,0:T(8,128)}, f32[16,40,128]{2,1,0:T(8,128)S(1)}) custom-call(f32[4,34,4,256]{3,2,1,0:T(4,128)} %refs_0_.1, f32[34,4,256]{2,1,0:T(4,128)} %refs_1_.1, f32[34,4,256]{2,1,0:T(4,128)} %refs_2_.1, s32[2,4,256]{2,1,0:T(4,128)} %refs_3_.1, s32[1,1,512]{2,1,0:T(1,128)} %refs_4_.1, s32[1,512]{1,0:T(1,128)} %bitcast.31, ...), custom_call_target="tpu_custom_call" | custom-call | tf_op jit(solution)/shard_map/pallas_call | solution.py:528
  4.3 7.4 %all-to-all-start = ((f32[16,72,128]{2,1,0:T(8,128)}), f32[16,72,128]{2,1,0:T(8,128)S(1)}, u32[]{:S(2)}, u32[]{:S(2)}) async-start(f32[16,72,128]{2,1,0:T(8,128)} %get-tuple-element.14), calls=%async_computation | async-start | bytes 1179648 | tf_op jit(solution)/shard_map/all_to_all | solution.py:515
  11.7 1.7 %collective-permute-start.2 = (f32[136,128]{1,0:T(8,128)S(1)}, f32[136,128]{1,0:T(8,128)S(1)}, u32[]{:S(2)}, u32[]{:S(2)}) collective-permute-start(f32[136,128]{1,0:T(8,128)S(1)} %get-tuple-element.31), channel_id=1, source_target_pairs={{0,24},{8,16},{16,8},{24,0},{1,25},{9,17},{17,9},{25,1},{2,26},{10... | collective-permute-start | bytes 208904 | tf_op jit(solution)/shard_map/ppermute | solution.py:474
  13.5 0.4 collective-permute-start.1
  13.8 5.9 %collective-permute-done.2 = f32[136,128]{1,0:T(8,128)S(1)} collective-permute-done((f32[136,128]{1,0:T(8,128)S(1)}, f32[136,128]{1,0:T(8,128)S(1)}, u32[]{:S(2)}, u32[]{:S(2)}) %collective-permute-start.2) | collective-permute-done | bytes 69664 | tf_op jit(solution)/shard_map/ppermute | solution.py:474
  19.7 3.5 %collective-permute-done.1 = f32[136,128]{1,0:T(8,128)S(1)} collective-permute-done((f32[136,128]{1,0:T(8,128)S(1)}, f32[136,128]{1,0:T(8,128)S(1)}, u32[]{:S(2)}, u32[]{:S(2)}) %collective-permute-start.1) | collective-permute-done | bytes 69664 | tf_op jit(solution)/shard_map/ppermute | solution.py:474
  23.6 4.1 %collective-permute-start.5 = (f32[136,128]{1,0:T(8,128)S(1)}, f32[136,128]{1,0:T(8,128)S(1)}, u32[]{:S(2)}, u32[]{:S(2)}) collective-permute-start(f32[136,128]{1,0:T(8,128)S(1)} %reshape.42), channel_id=1, source_target_pairs={{0,6},{2,4},{4,2},{6,0},{1,7},{3,5},{5,3},{7,1},{8,14},{10,12},{12... | collective-permute-start | bytes 208904 | tf_op jit(solution)/shard_map/ppermute | solution.py:474
  27.9 0.6 collective-permute-start.3
  28.5 3.2 %all-to-all-done.recv = f32[16,72,128]{2,1,0:T(8,128)S(1)} async-done(((f32[16,72,128]{2,1,0:T(8,128)}), f32[16,72,128]{2,1,0:T(8,128)S(1)}, u32[]{:S(2)}, u32[]{:S(2)}) %all-to-all-start) | async-done | bytes 589856 | tf_op jit(solution)/shard_map/all_to_all | solution.py:515
  31.7 1.6 %shard_map.105 = (f32[544,256]{1,0:T(8,128)S(1)}, f32[8,256]{1,0:T(8,128)S(1)}, f32[272,128]{1,0:T(8,128)S(1)}, f32[272,128]{1,0:T(8,128)S(1)}) custom-call(f32[16,72,128]{2,1,0:T(8,128)S(1)} %all-to-all-done.recv, f32[4,136,136]{2,1,0:T(8,128)S(1)} %copy-done), custom_call_target="tpu_custom_call" | custom-call | tf_op jit(solution)/shard_map/pallas_call | solution.py:543
  33.4 1.6 %collective-permute-start.8 = (f32[272,128]{1,0:T(8,128)S(1)}, f32[272,128]{1,0:T(8,128)S(1)}, u32[]{:S(2)}, u32[]{:S(2)}) collective-permute-start(f32[272,128]{1,0:T(8,128)S(1)} %get-tuple-element.21), channel_id=1, source_target_pairs={{0,1},{8,0},{2,8},{10,2},{4,10},{12,4},{6,12},{14,6},{22,14},{30,2... | collective-permute-start | bytes 417800 | tf_op jit(solution)/shard_map/ppermute | solution.py:518
  35.0 0.5 shard_map.106
  35.5 2.1 %collective-permute-start.6 = (f32[136,128]{1,0:T(8,128)S(1)}, f32[136,128]{1,0:T(8,128)S(1)}, u32[]{:S(2)}, u32[]{:S(2)}) collective-permute-start(f32[136,128]{1,0:T(8,128)S(1)} %get-tuple-element.19), channel_id=1, source_target_pairs={{0,1},{8,0},{2,8},{10,2},{4,10},{12,4},{6,12},{14,6},{22,14},{30,2... | collective-permute-start | bytes 208904 | tf_op jit(solution)/shard_map/ppermute | solution.py:518
  37.6 0.4 collective-permute-start.14
  38.0 0.4 shard_map.107.field
  38.4 1.1 %collective-permute-done.6.wind_east = f32[136,128]{1,0:T(8,128)S(1)} collective-permute-done((f32[136,128]{1,0:T(8,128)S(1)}, f32[136,128]{1,0:T(8,128)S(1)}, u32[]{:S(2)}, u32[]{:S(2)}) %collective-permute-start.6) | collective-permute-done | bytes 69664 | tf_op jit(solution)/shard_map/ppermute | solution.py:518
  39.8 2.1 %collective-permute-done.7.wind_west = f32[136,128]{1,0:T(8,128)S(1)} collective-permute-done((f32[136,128]{1,0:T(8,128)S(1)}, f32[136,128]{1,0:T(8,128)S(1)}, u32[]{:S(2)}, u32[]{:S(2)}) %collective-permute-start.7) | collective-permute-done | bytes 69664 | tf_op jit(solution)/shard_map/ppermute | solution.py:518
  41.9 4.8 %shard_map.108 = (f32[544,256]{1,0:T(8,128)S(1)}, f32[272,128]{1,0:T(8,128)S(1)}, f32[272,128]{1,0:T(8,128)S(1)}) custom-call(f32[544,256]{1,0:T(8,128)S(1)} %shard_map.107.field, f32[272,256]{1,0:T(8,128)S(1)} %get-tuple-element.18.winds, f32[8,256]{1,0:T(8,128)S(1)} %get-tuple-element.17.refs_4_.regimes, f32[4,136,136]{2,1,0:T(8,128)S(1)} %copy-done, ...), custom_call_target="tpu_custom_call" | custom-call | tf_op jit(solution)/shard_map/pallas_call | solution.py:560
  46.6 0.6 collective-permute-start.11
  47.2 1.5 %collective-permute-start.10 = (f32[272,128]{1,0:T(8,128)S(1)}, f32[272,128]{1,0:T(8,128)S(1)}, u32[]{:S(2)}, u32[]{:S(2)}) collective-permute-start(f32[272,128]{1,0:T(8,128)S(1)} %get-tuple-element.24._), channel_id=1, source_target_pairs={{0,1},{8,0},{2,8},{10,2},{4,10},{12,4},{6,12},{14,6},{22,14},{30,2... | collective-permute-start | bytes 417800 | tf_op jit(solution)/shard_map/ppermute | solution.py:518
  48.8 2.2 %shard_map.110.sums = f32[8,64]{1,0:T(8,128)S(1)} custom-call(f32[4,48,128]{2,1,0:T(8,128)S(1)} %pad_maximum_fusion.1.quarters, f32[544,256]{1,0:T(8,128)S(1)} %get-tuple-element.15.field.hour_0, f32[544,256]{1,0:T(8,128)S(1)} %get-tuple-element.23.hour_1.field), custom_call_target="tpu_custom_call" | custom-call | tf_op jit(solution)/shard_map/pallas_call | solution.py:566
  51.8 3.9 %shard_map.111 = f32[16,72,128]{2,1,0:T(8,128)S(1)} custom-call(f32[544,256]{1,0:T(8,128)S(1)} %get-tuple-element.23.hour_1.field, f32[6,136,384]{2,1,0:T(8,128)S(1)} %shard_map.109.faces, f32[272,128]{1,0:T(8,128)S(1)} %collective-permute-done.10.from_east, f32[272,128]{1,0:T(8,128)S(1)} %collective-permute-done.11.from_west, f32[8,64]{1,0:T(8,128)S(1)} %shard_map.110.sums), custom_call_target="tpu_custom_call" | custom-call | tf_op jit(solution)/shard_map/pallas_call | solution.py:572
  55.7 19.9 %all_to_all.10.recv = f32[16,72,128]{2,1,0:T(8,128)S(1)} all-to-all(f32[16,72,128]{2,1,0:T(8,128)S(1)} %shard_map.111), channel_id=1, replica_groups=mesh['lat'=4,'lev'=4,'lon'=2] {'lat','lev'}, dimensions={0} | all-to-all | bytes 1179648 | tf_op jit(solution)/shard_map/all_to_all | solution.py:515
  75.6 1.8 %shard_map.112 = (f32[4,34,4,256]{3,2,1,0:T(4,128)}, f32[2,4,1,4]{3,2,1,0:T(1,128)}) custom-call(f32[16,72,128]{2,1,0:T(8,128)S(1)} %all_to_all.10.recv), custom_call_target="tpu_custom_call" | custom-call | tf_op jit(solution)/shard_map/pallas_call | solution.py:577
  (36 shorter events, 1.6 us)
Async XLA Ops:
  4.3 27.5 %all-to-all-start = ((f32[16,72,128]{2,1,0:T(8,128)}), f32[16,72,128]{2,1,0:T(8,128)S(1)}, u32[]{:S(2)}, u32[]{:S(2)}) async-start(f32[16,72,128]{2,1,0:T(8,128)} %get-tuple-element.14), calls=%async_computation | async-start | bytes 1179648 | tf_op jit(solution)/shard_map/all_to_all | solution.py:515
  11.7 20.0 %copy-start = (f32[4,136,136]{2,1,0:T(8,128)S(1)}, f32[4,136,136]{2,1,0:T(8,128)}, u32[]{:S(2)}) copy-start(f32[4,136,136]{2,1,0:T(8,128)} %kz.3) | copy-start | bytes 887812
  11.7 8.0 %collective-permute-start.2 = (f32[136,128]{1,0:T(8,128)S(1)}, f32[136,128]{1,0:T(8,128)S(1)}, u32[]{:S(2)}, u32[]{:S(2)}) collective-permute-start(f32[136,128]{1,0:T(8,128)S(1)} %get-tuple-element.31), channel_id=1, source_target_pairs={{0,24},{8,16},{16,8},{24,0},{1,25},{9,17},{17,9},{25,1},{2,26},{10... | collective-permute-start | bytes 208904 | tf_op jit(solution)/shard_map/ppermute | solution.py:474
  13.5 9.8 %collective-permute-start.1 = (f32[136,128]{1,0:T(8,128)S(1)}, f32[136,128]{1,0:T(8,128)S(1)}, u32[]{:S(2)}, u32[]{:S(2)}) collective-permute-start(f32[136,128]{1,0:T(8,128)S(1)} %get-tuple-element.32), channel_id=1, source_target_pairs={{0,16},{8,24},{16,0},{24,8},{1,17},{9,25},{17,1},{25,9},{2,18},{10... | collective-permute-start | bytes 208904 | tf_op jit(solution)/shard_map/ppermute | solution.py:474
  13.8 9.4 %collective-permute-start = (f32[136,128]{1,0:T(8,128)S(1)}, f32[136,128]{1,0:T(8,128)S(1)}, u32[]{:S(2)}, u32[]{:S(2)}) collective-permute-start(f32[136,128]{1,0:T(8,128)S(1)} %get-tuple-element.33), channel_id=1, source_target_pairs={{0,8},{8,0},{16,24},{24,16},{1,9},{9,1},{17,25},{25,17},{2,10},{10... | collective-permute-start | bytes 208904 | tf_op jit(solution)/shard_map/ppermute | solution.py:474
  23.6 11.4 %collective-permute-start.5 = (f32[136,128]{1,0:T(8,128)S(1)}, f32[136,128]{1,0:T(8,128)S(1)}, u32[]{:S(2)}, u32[]{:S(2)}) collective-permute-start(f32[136,128]{1,0:T(8,128)S(1)} %reshape.42), channel_id=1, source_target_pairs={{0,6},{2,4},{4,2},{6,0},{1,7},{3,5},{5,3},{7,1},{8,14},{10,12},{12... | collective-permute-start | bytes 208904 | tf_op jit(solution)/shard_map/ppermute | solution.py:474
  27.8 7.2 %collective-permute-start.4 = (f32[136,128]{1,0:T(8,128)S(1)}, f32[136,128]{1,0:T(8,128)S(1)}, u32[]{:S(2)}, u32[]{:S(2)}) collective-permute-start(f32[136,128]{1,0:T(8,128)S(1)} %reshape.41), channel_id=1, source_target_pairs={{0,4},{2,6},{4,0},{6,2},{1,5},{3,7},{5,1},{7,3},{8,12},{10,14},{12... | collective-permute-start | bytes 208904 | tf_op jit(solution)/shard_map/ppermute | solution.py:474
  27.9 7.1 %collective-permute-start.3 = (f32[136,128]{1,0:T(8,128)S(1)}, f32[136,128]{1,0:T(8,128)S(1)}, u32[]{:S(2)}, u32[]{:S(2)}) collective-permute-start(f32[136,128]{1,0:T(8,128)S(1)} %reshape.40), channel_id=1, source_target_pairs={{0,2},{2,0},{4,6},{6,4},{1,3},{3,1},{5,7},{7,5},{8,10},{10,8},{12,... | collective-permute-start | bytes 208904 | tf_op jit(solution)/shard_map/ppermute | solution.py:474
  33.4 8.5 %collective-permute-start.8 = (f32[272,128]{1,0:T(8,128)S(1)}, f32[272,128]{1,0:T(8,128)S(1)}, u32[]{:S(2)}, u32[]{:S(2)}) collective-permute-start(f32[272,128]{1,0:T(8,128)S(1)} %get-tuple-element.21), channel_id=1, source_target_pairs={{0,1},{8,0},{2,8},{10,2},{4,10},{12,4},{6,12},{14,6},{22,14},{30,2... | collective-permute-start | bytes 417800 | tf_op jit(solution)/shard_map/ppermute | solution.py:518
  34.9 6.9 %collective-permute-start.9 = (f32[272,128]{1,0:T(8,128)S(1)}, f32[272,128]{1,0:T(8,128)S(1)}, u32[]{:S(2)}, u32[]{:S(2)}) collective-permute-start(f32[272,128]{1,0:T(8,128)S(1)} %get-tuple-element.22), channel_id=1, source_target_pairs={{0,8},{8,2},{2,10},{10,4},{4,12},{12,6},{6,14},{14,22},{22,30},{30... | collective-permute-start | bytes 417800 | tf_op jit(solution)/shard_map/ppermute | solution.py:518
  35.5 4.0 %collective-permute-start.6 = (f32[136,128]{1,0:T(8,128)S(1)}, f32[136,128]{1,0:T(8,128)S(1)}, u32[]{:S(2)}, u32[]{:S(2)}) collective-permute-start(f32[136,128]{1,0:T(8,128)S(1)} %get-tuple-element.19), channel_id=1, source_target_pairs={{0,1},{8,0},{2,8},{10,2},{4,10},{12,4},{6,12},{14,6},{22,14},{30,2... | collective-permute-start | bytes 208904 | tf_op jit(solution)/shard_map/ppermute | solution.py:518
  37.5 4.3 %collective-permute-start.7 = (f32[136,128]{1,0:T(8,128)S(1)}, f32[136,128]{1,0:T(8,128)S(1)}, u32[]{:S(2)}, u32[]{:S(2)}) collective-permute-start(f32[136,128]{1,0:T(8,128)S(1)} %get-tuple-element.20), channel_id=1, source_target_pairs={{0,8},{8,2},{2,10},{10,4},{4,12},{12,6},{6,14},{14,22},{22,30},{30... | collective-permute-start | bytes 208904 | tf_op jit(solution)/shard_map/ppermute | solution.py:518
  37.6 11.2 %collective-permute-start.14 = (f32[48,128]{1,0:T(8,128)S(1)}, f32[48,128]{1,0:T(8,128)S(1)}, u32[]{:S(2)}, u32[]{:S(2)}) collective-permute-start(f32[48,128]{1,0:T(8,128)S(1)} %reshape.43), channel_id=1, source_target_pairs={{0,24},{8,16},{16,8},{24,0},{1,25},{9,17},{17,9},{25,1},{2,26},{10... | collective-permute-start | bytes 73736 | tf_op jit(solution)/shard_map/ppermute | solution.py:474
  39.5 9.3 %collective-permute-start.13 = (f32[48,128]{1,0:T(8,128)S(1)}, f32[48,128]{1,0:T(8,128)S(1)}, u32[]{:S(2)}, u32[]{:S(2)}) collective-permute-start(f32[48,128]{1,0:T(8,128)S(1)} %reshape.43), channel_id=1, source_target_pairs={{0,16},{8,24},{16,0},{24,8},{1,17},{9,25},{17,1},{25,9},{2,18},{10... | collective-permute-start | bytes 73736 | tf_op jit(solution)/shard_map/ppermute | solution.py:474
  41.9 6.9 %collective-permute-start.12 = (f32[48,128]{1,0:T(8,128)S(1)}, f32[48,128]{1,0:T(8,128)S(1)}, u32[]{:S(2)}, u32[]{:S(2)}) collective-permute-start(f32[48,128]{1,0:T(8,128)S(1)} %reshape.43), channel_id=1, source_target_pairs={{0,8},{8,0},{16,24},{24,16},{1,9},{9,1},{17,25},{25,17},{2,10},{10... | collective-permute-start | bytes 73736 | tf_op jit(solution)/shard_map/ppermute | solution.py:474
  46.6 5.1 %collective-permute-start.11 = (f32[272,128]{1,0:T(8,128)S(1)}, f32[272,128]{1,0:T(8,128)S(1)}, u32[]{:S(2)}, u32[]{:S(2)}) collective-permute-start(f32[272,128]{1,0:T(8,128)S(1)} %get-tuple-element.25), channel_id=1, source_target_pairs={{0,8},{8,2},{2,10},{10,4},{4,12},{12,6},{6,14},{14,22},{22,30},{30... | collective-permute-start | bytes 417800 | tf_op jit(solution)/shard_map/ppermute | solution.py:518
  47.2 4.6 %collective-permute-start.10 = (f32[272,128]{1,0:T(8,128)S(1)}, f32[272,128]{1,0:T(8,128)S(1)}, u32[]{:S(2)}, u32[]{:S(2)}) collective-permute-start(f32[272,128]{1,0:T(8,128)S(1)} %get-tuple-element.24._), channel_id=1, source_target_pairs={{0,1},{8,0},{2,8},{10,2},{4,10},{12,4},{6,12},{14,6},{22,14},{30,2... | collective-permute-start | bytes 417800 | tf_op jit(solution)/shard_map/ppermute | solution.py:518

commit v7 on v6

--- a/solution.py
+++ b/solution.py
@@ -100,41 +100,52 @@
     return (mm(high, matrix) + mm(middle, matrix)) + mm(low, matrix)
 
 
-def pack_kernel(place, *refs):
-    count = (len(refs) - 3) // 2
-    given, outs = refs[:count], refs[count : count + 2]
-    held, sems = refs[count + 2 : -1], refs[-1]
-    place = owners(place)
-    copies = [
+def fetch(given, held, sems):
+    return [
         pltpu.make_async_copy(a, b, sems.at[i]) for i, (a, b) in enumerate(zip(given, held))
     ]
+
+
+def place_pieces(place, srcs, out, first, count):
+    for half in range(2):
+        lanes = slice(half * LANES, (half + 1) * LANES)
+        for j, piece in enumerate(swap_grains([s[:, lanes] for s in srcs])):
+            out[place[half * 8 + j], first : first + count, :] = piece
+
+
+def pack_winds_kernel(place, *refs):
+    given, winds, held, sems = refs[:2], refs[3], refs[4:6], refs[6]
+    copies = fetch(given, held, sems)
+    for copy in copies:
+        copy.start()
+    place = owners(place)
+    levels, rows = held[0].shape[:2]
+    for copy in copies:
+        copy.wait()
+    place_pieces(place, [w[:, r, :] for w in held for r in range(rows)], winds, 0, levels)
+
+
+def pack_fields_kernel(place, *refs):
+    count = (len(refs) - 2) // 2
+    given, fields, held, sems = refs[:count], refs[count], refs[count + 1 : -1], refs[-1]
     halves = [
         pltpu.make_async_copy(given[0].at[part], held[0].at[part], sems.at[at])
         for part, at in ((pl.ds(0, 2), 0), (pl.ds(2, 2), count))
     ]
-    for copy in halves + copies[1:]:
+    copies = fetch(given, held, sems)[1:]
+    for copy in halves + copies:
         copy.start()
-    adj, east, north, regime, cell, owner, station, weight = held
-    fields, winds = outs
-    levels = adj.shape[1]
-    rows = adj.shape[2]
-
-    def place_pieces(srcs, out, first, count):
-        for half in range(2):
-            lanes = slice(half * LANES, (half + 1) * LANES)
-            for j, piece in enumerate(swap_grains([s[:, lanes] for s in srcs])):
-                out[place[half * 8 + j], first : first + count, :] = piece
-
+    adj, regime, cell, owner, station, weight = held
+    place = owners(place)
+    levels, rows = adj.shape[1:3]
     for pair in range(2):
         halves[pair].wait()
         srcs = [adj[2 * pair + k, :, r, :] for k in range(2) for r in range(rows)]
-        place_pieces(srcs, fields, pair * levels, levels)
-    for copy in copies[1:]:
+        place_pieces(place, srcs, fields, pair * levels, levels)
+    for copy in copies:
         copy.wait()
-    srcs = [w[:, r, :] for w in (east, north) for r in range(rows)]
-    place_pieces(srcs, winds, 0, levels)
     srcs = [regime[h, r : r + 1, :].astype(F32) for h in range(HOURS) for r in range(rows)]
-    place_pieces(srcs, fields, 2 * levels, 1)
+    place_pieces(place, srcs, fields, 2 * levels, 1)
     cells = cell[0].astype(F32)
     stations = (owner[...] * SPO + station[0]).astype(F32)
     for g in range(fields.shape[0]):
@@ -522,22 +533,27 @@
     in_rows = 2 * levels + 4
     in_rows += -in_rows % 8
     wind_rows = levels + -levels % 8
-    given = (
-        adjoint, wind_east, wind_north, kz_regime, fp_cell, fp_owner.reshape(1, -1), fp_station, fp_weight
-    )
-    fields, winds = pl.pallas_call(
-        functools.partial(pack_kernel, place),
-        in_specs=[pl.BlockSpec(memory_space=pltpu.HBM)] * len(given),
-        out_shape=[
-            jax.ShapeDtypeStruct(shape, F32)
-            for shape in (
-                (group, in_rows, LANES), (group, wind_rows, LANES)
-            )
-        ],
-        scratch_shapes=[pltpu.VMEM(x.shape, x.dtype) for x in given]
-        + [pltpu.SemaphoreType.DMA((len(given) + 1,))],
-        compiler_params=pltpu.CompilerParams(vmem_limit_bytes=48 * 1024 * 1024),
-    )(*[pltpu.with_memory_space_constraint(x, pltpu.HBM) for x in given])
+
+    def pack(kernel, given, after, shape):
+        given = [pltpu.with_memory_space_constraint(x, pltpu.HBM) for x in given]
+        return pl.pallas_call(
+            functools.partial(kernel, place),
+            in_specs=[pl.BlockSpec(memory_space=pltpu.HBM)] * (len(given) + len(after)),
+            out_shape=jax.ShapeDtypeStruct(shape, F32),
+            scratch_shapes=[pltpu.VMEM(x.shape, x.dtype) for x in given]
+            + [pltpu.SemaphoreType.DMA((len(given) + 1,))],
+            compiler_params=pltpu.CompilerParams(vmem_limit_bytes=48 * 1024 * 1024),
+        )(*given, *after)
+
+    fields = pack(
+        pack_fields_kernel,
+        (adjoint, kz_regime, fp_cell, fp_owner.reshape(1, -1), fp_station, fp_weight),
+        (),
+        (group, in_rows, LANES),
+    )
+    winds = pack(
+        pack_winds_kernel, (wind_east, wind_north), (fields,), (group, wind_rows, LANES)
+    )
     recv = exchange(fields)
     winds = gather_winds(sizes, winds[:, :levels])
     solved_0, regimes, first, last = call(

time: 77.7 us -> 77.2 us (level)
  waiting for transfers between devices: 16.2 us -> 14.6 us
  Pallas kernels: 19.2 us -> 20.3 us
    ppermute x9, waiting for transfers between devices: 9.45 us -> 7.89 us  [swaps(): lax.ppermute(piece(x, k), axis, [(i, i ^ k) for i in range(count)])]
    pallas_call x1 -> x2, Pallas kernels: 3.62 us -> 4.74 us  [pack(): pl.pallas_call(functools.partial(kernel, place), in_specs=[pl.BlockSpec(m...]
  transfers between devices with their start and end apart: 16 -> 16, of which waited for: 6 -> 6; matrix products, arithmetic and copies ran while one was open for 1% -> 1% of each run, Pallas kernels for 13% -> 15%
where the time goes in v7:
time: 77.2 us; the launch traced here: 76.9 us
  starting transfers between devices  20.7 us (27%)
  Pallas kernels  20.3 us (26%)
  blocking collectives  19.9 us (26%)
  waiting for transfers between devices  14.6 us (19%)
  between operations  0.9 us (1%)
    all_to_all x1, blocking collectives, exchange(): return lax.all_to_all(x, AXES, split_axis=0, concat_axis=0, tiled=True)  19.9 us
    ppermute x9, waiting for transfers between devices, swaps(): lax.ppermute(piece(x, k), axis, [(i, i ^ k) for i in range(count)])  7.89 us
    ppermute x9, starting transfers between devices, swaps(): lax.ppermute(piece(x, k), axis, [(i, i ^ k) for i in range(count)])  7.61 us
    all_to_all x1, starting transfers between devices, exchange(): return lax.all_to_all(x, AXES, split_axis=0, concat_axis=0, tiled=True)  7.37 us
    ppermute x3, starting transfers between devices, rims(): lax.ppermute(first, RING, to_west)  5.18 us
    pallas_call x1, Pallas kernels, regrouped(): call(functools.partial(transport_solve_kernel, lat_count), [(4 * total, 2...  4.77 us
    pallas_call x2, Pallas kernels, pack(): pl.pallas_call(functools.partial(kernel, place), in_specs=[pl.BlockSpec(m...  4.74 us
    pallas_call x1, Pallas kernels, regrouped(): call(functools.partial(transport_pack_kernel, lat_count, n_lev), [(group,...  3.93 us
  transfers between devices with their start and end apart: 16, of which 6 were waited for; matrix products, arithmetic and copies ran while one was open for 1% of the time, Pallas kernels for 15%

profile of v7, /device:TPU:0, one launch (start us, length us, event | category | flops | bytes accessed | tf_op | source)
XLA Modules:
  0.0 76.9 jit_solution(7145334007712956632)
XLA Ops:
  0.6 3.2 %shard_map.104.refs_2_ = f32[16,72,128]{2,1,0:T(8,128)} custom-call(f32[4,34,4,256]{3,2,1,0:T(4,128)} %refs_0_.2, s32[2,4,256]{2,1,0:T(4,128)} %refs_1_.2, s32[1,1,512]{2,1,0:T(1,128)} %refs_2_.1, s32[1,512]{1,0:T(1,128)} %bitcast.31, s32[1,1,512]{2,1,0:T(1,128)} %refs_4_.1, f32[1,1,512]{2,1,0:T(1,128)} %refs_5_.1), custom_call_target="tpu_custom_call" | custom-call | tf_op jit(solution)/shard_map/pallas_call | solution.py:539
  3.8 7.4 %all-to-all-start = ((f32[16,72,128]{2,1,0:T(8,128)}), f32[16,72,128]{2,1,0:T(8,128)S(1)}, u32[]{:S(2)}, u32[]{:S(2)}) async-start(f32[16,72,128]{2,1,0:T(8,128)} %shard_map.104.refs_2_), calls=%async_computation | async-start | bytes 1179648 | tf_op jit(solution)/shard_map/all_to_all | solution.py:526
  11.2 1.6 %shard_map.106 = f32[16,40,128]{2,1,0:T(8,128)S(1)} custom-call(f32[34,4,256]{2,1,0:T(4,128)} %refs_0_.3, f32[34,4,256]{2,1,0:T(4,128)} %refs_1_.3, f32[16,72,128]{2,1,0:T(8,128)} %shard_map.104.refs_2_), custom_call_target="tpu_custom_call" | custom-call | tf_op jit(solution)/shard_map/pallas_call | solution.py:539
  12.9 1.7 %collective-permute-start.2 = (f32[136,128]{1,0:T(8,128)S(1)}, f32[136,128]{1,0:T(8,128)S(1)}, u32[]{:S(2)}, u32[]{:S(2)}) collective-permute-start(f32[136,128]{1,0:T(8,128)S(1)} %get-tuple-element.27), channel_id=1, source_target_pairs={{0,24},{8,16},{16,8},{24,0},{1,25},{9,17},{17,9},{25,1},{2,26},{10... | collective-permute-start | bytes 208904 | tf_op jit(solution)/shard_map/ppermute | solution.py:485
  15.0 4.3 %collective-permute-done.2 = f32[136,128]{1,0:T(8,128)S(1)} collective-permute-done((f32[136,128]{1,0:T(8,128)S(1)}, f32[136,128]{1,0:T(8,128)S(1)}, u32[]{:S(2)}, u32[]{:S(2)}) %collective-permute-start.2) | collective-permute-done | bytes 69664 | tf_op jit(solution)/shard_map/ppermute | solution.py:485
  19.3 3.5 %collective-permute-done.1 = f32[136,128]{1,0:T(8,128)S(1)} collective-permute-done((f32[136,128]{1,0:T(8,128)S(1)}, f32[136,128]{1,0:T(8,128)S(1)}, u32[]{:S(2)}, u32[]{:S(2)}) %collective-permute-start.1) | collective-permute-done | bytes 69664 | tf_op jit(solution)/shard_map/ppermute | solution.py:485
  23.2 4.1 %collective-permute-start.5 = (f32[136,128]{1,0:T(8,128)S(1)}, f32[136,128]{1,0:T(8,128)S(1)}, u32[]{:S(2)}, u32[]{:S(2)}) collective-permute-start(f32[136,128]{1,0:T(8,128)S(1)} %reshape.42), channel_id=1, source_target_pairs={{0,6},{2,4},{4,2},{6,0},{1,7},{3,5},{5,3},{7,1},{8,14},{10,12},{12... | collective-permute-start | bytes 208904 | tf_op jit(solution)/shard_map/ppermute | solution.py:485
  27.4 0.6 collective-permute-start.3
  28.1 3.2 %all-to-all-done.recv = f32[16,72,128]{2,1,0:T(8,128)S(1)} async-done(((f32[16,72,128]{2,1,0:T(8,128)}), f32[16,72,128]{2,1,0:T(8,128)S(1)}, u32[]{:S(2)}, u32[]{:S(2)}) %all-to-all-start) | async-done | bytes 589856 | tf_op jit(solution)/shard_map/all_to_all | solution.py:526
  31.3 1.6 %shard_map.105 = (f32[544,256]{1,0:T(8,128)S(1)}, f32[8,256]{1,0:T(8,128)S(1)}, f32[272,128]{1,0:T(8,128)S(1)}, f32[272,128]{1,0:T(8,128)S(1)}) custom-call(f32[16,72,128]{2,1,0:T(8,128)S(1)} %all-to-all-done.recv, f32[4,136,136]{2,1,0:T(8,128)S(1)} %copy-done), custom_call_target="tpu_custom_call" | custom-call | tf_op jit(solution)/shard_map/pallas_call | solution.py:559
  32.9 1.6 %collective-permute-start.8 = (f32[272,128]{1,0:T(8,128)S(1)}, f32[272,128]{1,0:T(8,128)S(1)}, u32[]{:S(2)}, u32[]{:S(2)}) collective-permute-start(f32[272,128]{1,0:T(8,128)S(1)} %get-tuple-element.17), channel_id=1, source_target_pairs={{0,1},{8,0},{2,8},{10,2},{4,10},{12,4},{6,12},{14,6},{22,14},{30,2... | collective-permute-start | bytes 417800 | tf_op jit(solution)/shard_map/ppermute | solution.py:529
  34.6 0.5 shard_map.107
  35.0 2.1 %collective-permute-start.6 = (f32[136,128]{1,0:T(8,128)S(1)}, f32[136,128]{1,0:T(8,128)S(1)}, u32[]{:S(2)}, u32[]{:S(2)}) collective-permute-start(f32[136,128]{1,0:T(8,128)S(1)} %get-tuple-element.15), channel_id=1, source_target_pairs={{0,1},{8,0},{2,8},{10,2},{4,10},{12,4},{6,12},{14,6},{22,14},{30,2... | collective-permute-start | bytes 208904 | tf_op jit(solution)/shard_map/ppermute | solution.py:529
  37.1 0.4 collective-permute-start.14
  37.5 0.4 shard_map.108.field
  37.9 1.1 %collective-permute-done.6.wind_east = f32[136,128]{1,0:T(8,128)S(1)} collective-permute-done((f32[136,128]{1,0:T(8,128)S(1)}, f32[136,128]{1,0:T(8,128)S(1)}, u32[]{:S(2)}, u32[]{:S(2)}) %collective-permute-start.6) | collective-permute-done | bytes 69664 | tf_op jit(solution)/shard_map/ppermute | solution.py:529
  39.4 2.0 %collective-permute-done.7.wind_west = f32[136,128]{1,0:T(8,128)S(1)} collective-permute-done((f32[136,128]{1,0:T(8,128)S(1)}, f32[136,128]{1,0:T(8,128)S(1)}, u32[]{:S(2)}, u32[]{:S(2)}) %collective-permute-start.7) | collective-permute-done | bytes 69664 | tf_op jit(solution)/shard_map/ppermute | solution.py:529
  41.4 4.8 %shard_map.109 = (f32[544,256]{1,0:T(8,128)S(1)}, f32[272,128]{1,0:T(8,128)S(1)}, f32[272,128]{1,0:T(8,128)S(1)}) custom-call(f32[544,256]{1,0:T(8,128)S(1)} %shard_map.108.field, f32[272,256]{1,0:T(8,128)S(1)} %get-tuple-element.14.winds, f32[8,256]{1,0:T(8,128)S(1)} %get-tuple-element.13.refs_4_.regimes, f32[4,136,136]{2,1,0:T(8,128)S(1)} %copy-done, ...), custom_call_target="tpu_custom_call" | custom-call | tf_op jit(solution)/shard_map/pallas_call | solution.py:576
  46.2 0.6 collective-permute-start.11
  46.8 1.5 %collective-permute-start.10 = (f32[272,128]{1,0:T(8,128)S(1)}, f32[272,128]{1,0:T(8,128)S(1)}, u32[]{:S(2)}, u32[]{:S(2)}) collective-permute-start(f32[272,128]{1,0:T(8,128)S(1)} %get-tuple-element.20._), channel_id=1, source_target_pairs={{0,1},{8,0},{2,8},{10,2},{4,10},{12,4},{6,12},{14,6},{22,14},{30,2... | collective-permute-start | bytes 417800 | tf_op jit(solution)/shard_map/ppermute | solution.py:529
  48.4 2.2 %shard_map.111.sums = f32[8,64]{1,0:T(8,128)S(1)} custom-call(f32[4,48,128]{2,1,0:T(8,128)S(1)} %pad_maximum_fusion.1.quarters, f32[544,256]{1,0:T(8,128)S(1)} %get-tuple-element.12.field.hour_0, f32[544,256]{1,0:T(8,128)S(1)} %get-tuple-element.19.hour_1.field), custom_call_target="tpu_custom_call" | custom-call | tf_op jit(solution)/shard_map/pallas_call | solution.py:582
  51.3 3.9 %shard_map.112 = f32[16,72,128]{2,1,0:T(8,128)S(1)} custom-call(f32[544,256]{1,0:T(8,128)S(1)} %get-tuple-element.19.hour_1.field, f32[6,136,384]{2,1,0:T(8,128)S(1)} %shard_map.110.faces, f32[272,128]{1,0:T(8,128)S(1)} %collective-permute-done.10.from_east, f32[272,128]{1,0:T(8,128)S(1)} %collective-permute-done.11.from_west, f32[8,64]{1,0:T(8,128)S(1)} %shard_map.111.sums), custom_call_target="tpu_custom_call" | custom-call | tf_op jit(solution)/shard_map/pallas_call | solution.py:588
  55.3 19.9 %all_to_all.10.recv = f32[16,72,128]{2,1,0:T(8,128)S(1)} all-to-all(f32[16,72,128]{2,1,0:T(8,128)S(1)} %shard_map.112), channel_id=1, replica_groups=mesh['lat'=4,'lev'=4,'lon'=2] {'lat','lev'}, dimensions={0} | all-to-all | bytes 1179648 | tf_op jit(solution)/shard_map/all_to_all | solution.py:526
  75.1 1.8 %shard_map.113 = (f32[4,34,4,256]{3,2,1,0:T(4,128)}, f32[2,4,1,4]{3,2,1,0:T(1,128)}) custom-call(f32[16,72,128]{2,1,0:T(8,128)S(1)} %all_to_all.10.recv), custom_call_target="tpu_custom_call" | custom-call | tf_op jit(solution)/shard_map/pallas_call | solution.py:593
  (37 shorter events, 2.0 us)
Async XLA Ops:
  3.8 27.5 %all-to-all-start = ((f32[16,72,128]{2,1,0:T(8,128)}), f32[16,72,128]{2,1,0:T(8,128)S(1)}, u32[]{:S(2)}, u32[]{:S(2)}) async-start(f32[16,72,128]{2,1,0:T(8,128)} %shard_map.104.refs_2_), calls=%async_computation | async-start | bytes 1179648 | tf_op jit(solution)/shard_map/all_to_all | solution.py:526
  12.8 18.4 %copy-start = (f32[4,136,136]{2,1,0:T(8,128)S(1)}, f32[4,136,136]{2,1,0:T(8,128)}, u32[]{:S(2)}) copy-start(f32[4,136,136]{2,1,0:T(8,128)} %kz.3) | copy-start | bytes 887812
  12.9 6.4 %collective-permute-start.2 = (f32[136,128]{1,0:T(8,128)S(1)}, f32[136,128]{1,0:T(8,128)S(1)}, u32[]{:S(2)}, u32[]{:S(2)}) collective-permute-start(f32[136,128]{1,0:T(8,128)S(1)} %get-tuple-element.27), channel_id=1, source_target_pairs={{0,24},{8,16},{16,8},{24,0},{1,25},{9,17},{17,9},{25,1},{2,26},{10... | collective-permute-start | bytes 208904 | tf_op jit(solution)/shard_map/ppermute | solution.py:485
  14.6 8.2 %collective-permute-start.1 = (f32[136,128]{1,0:T(8,128)S(1)}, f32[136,128]{1,0:T(8,128)S(1)}, u32[]{:S(2)}, u32[]{:S(2)}) collective-permute-start(f32[136,128]{1,0:T(8,128)S(1)} %get-tuple-element.28), channel_id=1, source_target_pairs={{0,16},{8,24},{16,0},{24,8},{1,17},{9,25},{17,1},{25,9},{2,18},{10... | collective-permute-start | bytes 208904 | tf_op jit(solution)/shard_map/ppermute | solution.py:485
  15.0 7.9 %collective-permute-start = (f32[136,128]{1,0:T(8,128)S(1)}, f32[136,128]{1,0:T(8,128)S(1)}, u32[]{:S(2)}, u32[]{:S(2)}) collective-permute-start(f32[136,128]{1,0:T(8,128)S(1)} %get-tuple-element.29), channel_id=1, source_target_pairs={{0,8},{8,0},{16,24},{24,16},{1,9},{9,1},{17,25},{25,17},{2,10},{10... | collective-permute-start | bytes 208904 | tf_op jit(solution)/shard_map/ppermute | solution.py:485
  23.2 11.3 %collective-permute-start.5 = (f32[136,128]{1,0:T(8,128)S(1)}, f32[136,128]{1,0:T(8,128)S(1)}, u32[]{:S(2)}, u32[]{:S(2)}) collective-permute-start(f32[136,128]{1,0:T(8,128)S(1)} %reshape.42), channel_id=1, source_target_pairs={{0,6},{2,4},{4,2},{6,0},{1,7},{3,5},{5,3},{7,1},{8,14},{10,12},{12... | collective-permute-start | bytes 208904 | tf_op jit(solution)/shard_map/ppermute | solution.py:485
  27.3 7.2 %collective-permute-start.4 = (f32[136,128]{1,0:T(8,128)S(1)}, f32[136,128]{1,0:T(8,128)S(1)}, u32[]{:S(2)}, u32[]{:S(2)}) collective-permute-start(f32[136,128]{1,0:T(8,128)S(1)} %reshape.41), channel_id=1, source_target_pairs={{0,4},{2,6},{4,0},{6,2},{1,5},{3,7},{5,1},{7,3},{8,12},{10,14},{12... | collective-permute-start | bytes 208904 | tf_op jit(solution)/shard_map/ppermute | solution.py:485
  27.4 7.1 %collective-permute-start.3 = (f32[136,128]{1,0:T(8,128)S(1)}, f32[136,128]{1,0:T(8,128)S(1)}, u32[]{:S(2)}, u32[]{:S(2)}) collective-permute-start(f32[136,128]{1,0:T(8,128)S(1)} %reshape.40), channel_id=1, source_target_pairs={{0,2},{2,0},{4,6},{6,4},{1,3},{3,1},{5,7},{7,5},{8,10},{10,8},{12,... | collective-permute-start | bytes 208904 | tf_op jit(solution)/shard_map/ppermute | solution.py:485
  32.9 8.5 %collective-permute-start.8 = (f32[272,128]{1,0:T(8,128)S(1)}, f32[272,128]{1,0:T(8,128)S(1)}, u32[]{:S(2)}, u32[]{:S(2)}) collective-permute-start(f32[272,128]{1,0:T(8,128)S(1)} %get-tuple-element.17), channel_id=1, source_target_pairs={{0,1},{8,0},{2,8},{10,2},{4,10},{12,4},{6,12},{14,6},{22,14},{30,2... | collective-permute-start | bytes 417800 | tf_op jit(solution)/shard_map/ppermute | solution.py:529
  34.5 6.9 %collective-permute-start.9 = (f32[272,128]{1,0:T(8,128)S(1)}, f32[272,128]{1,0:T(8,128)S(1)}, u32[]{:S(2)}, u32[]{:S(2)}) collective-permute-start(f32[272,128]{1,0:T(8,128)S(1)} %get-tuple-element.18), channel_id=1, source_target_pairs={{0,8},{8,2},{2,10},{10,4},{4,12},{12,6},{6,14},{14,22},{22,30},{30... | collective-permute-start | bytes 417800 | tf_op jit(solution)/shard_map/ppermute | solution.py:529
  35.0 4.0 %collective-permute-start.6 = (f32[136,128]{1,0:T(8,128)S(1)}, f32[136,128]{1,0:T(8,128)S(1)}, u32[]{:S(2)}, u32[]{:S(2)}) collective-permute-start(f32[136,128]{1,0:T(8,128)S(1)} %get-tuple-element.15), channel_id=1, source_target_pairs={{0,1},{8,0},{2,8},{10,2},{4,10},{12,4},{6,12},{14,6},{22,14},{30,2... | collective-permute-start | bytes 208904 | tf_op jit(solution)/shard_map/ppermute | solution.py:529
  37.1 4.3 %collective-permute-start.7 = (f32[136,128]{1,0:T(8,128)S(1)}, f32[136,128]{1,0:T(8,128)S(1)}, u32[]{:S(2)}, u32[]{:S(2)}) collective-permute-start(f32[136,128]{1,0:T(8,128)S(1)} %get-tuple-element.16), channel_id=1, source_target_pairs={{0,8},{8,2},{2,10},{10,4},{4,12},{12,6},{6,14},{14,22},{22,30},{30... | collective-permute-start | bytes 208904 | tf_op jit(solution)/shard_map/ppermute | solution.py:529
  37.1 11.2 %collective-permute-start.14 = (f32[48,128]{1,0:T(8,128)S(1)}, f32[48,128]{1,0:T(8,128)S(1)}, u32[]{:S(2)}, u32[]{:S(2)}) collective-permute-start(f32[48,128]{1,0:T(8,128)S(1)} %reshape.43), channel_id=1, source_target_pairs={{0,24},{8,16},{16,8},{24,0},{1,25},{9,17},{17,9},{25,1},{2,26},{10... | collective-permute-start | bytes 73736 | tf_op jit(solution)/shard_map/ppermute | solution.py:485
  39.0 9.3 %collective-permute-start.13 = (f32[48,128]{1,0:T(8,128)S(1)}, f32[48,128]{1,0:T(8,128)S(1)}, u32[]{:S(2)}, u32[]{:S(2)}) collective-permute-start(f32[48,128]{1,0:T(8,128)S(1)} %reshape.43), channel_id=1, source_target_pairs={{0,16},{8,24},{16,0},{24,8},{1,17},{9,25},{17,1},{25,9},{2,18},{10... | collective-permute-start | bytes 73736 | tf_op jit(solution)/shard_map/ppermute | solution.py:485
  41.4 6.9 %collective-permute-start.12 = (f32[48,128]{1,0:T(8,128)S(1)}, f32[48,128]{1,0:T(8,128)S(1)}, u32[]{:S(2)}, u32[]{:S(2)}) collective-permute-start(f32[48,128]{1,0:T(8,128)S(1)} %reshape.43), channel_id=1, source_target_pairs={{0,8},{8,0},{16,24},{24,16},{1,9},{9,1},{17,25},{25,17},{2,10},{10... | collective-permute-start | bytes 73736 | tf_op jit(solution)/shard_map/ppermute | solution.py:485
  46.2 5.1 %collective-permute-start.11 = (f32[272,128]{1,0:T(8,128)S(1)}, f32[272,128]{1,0:T(8,128)S(1)}, u32[]{:S(2)}, u32[]{:S(2)}) collective-permute-start(f32[272,128]{1,0:T(8,128)S(1)} %get-tuple-element.21), channel_id=1, source_target_pairs={{0,8},{8,2},{2,10},{10,4},{4,12},{12,6},{6,14},{14,22},{22,30},{30... | collective-permute-start | bytes 417800 | tf_op jit(solution)/shard_map/ppermute | solution.py:529
  46.8 4.6 %collective-permute-start.10 = (f32[272,128]{1,0:T(8,128)S(1)}, f32[272,128]{1,0:T(8,128)S(1)}, u32[]{:S(2)}, u32[]{:S(2)}) collective-permute-start(f32[272,128]{1,0:T(8,128)S(1)} %get-tuple-element.20._), channel_id=1, source_target_pairs={{0,1},{8,0},{2,8},{10,2},{4,10},{12,4},{6,12},{14,6},{22,14},{30,2... | collective-permute-start | bytes 417800 | tf_op jit(solution)/shard_map/ppermute | solution.py:529

commit v8 on v7

--- a/solution.py
+++ b/solution.py
@@ -133,15 +133,11 @@
         for part, at in ((pl.ds(0, 2), 0), (pl.ds(2, 2), count))
     ]
     copies = fetch(given, held, sems)[1:]
-    for copy in halves + copies:
+    for copy in copies + halves:
         copy.start()
     adj, regime, cell, owner, station, weight = held
     place = owners(place)
     levels, rows = adj.shape[1:3]
-    for pair in range(2):
-        halves[pair].wait()
-        srcs = [adj[2 * pair + k, :, r, :] for k in range(2) for r in range(rows)]
-        place_pieces(place, srcs, fields, pair * levels, levels)
     for copy in copies:
         copy.wait()
     srcs = [regime[h, r : r + 1, :].astype(F32) for h in range(HOURS) for r in range(rows)]
@@ -153,6 +149,10 @@
         for at, value in enumerate((cells, stations, weight[0])):
             row = 2 * levels + 1 + at
             fields[g, row : row + 1, :] = value[:, k * LANES : (k + 1) * LANES]
+    for pair in range(2):
+        halves[pair].wait()
+        srcs = [adj[2 * pair + k, :, r, :] for k in range(2) for r in range(rows)]
+        place_pieces(place, srcs, fields, pair * levels, levels)
 
 
 def solve_columns(high, low, kz_high, kz_low, regime, levels):

time: 77.2 us -> 77.1 us (level)
  no operation moved by 1% of the time
where the time goes in v8:
time: 77.1 us; the launch traced here: 76.8 us
  starting transfers between devices  20.7 us (27%)
  Pallas kernels  20.2 us (26%)
  blocking collectives  19.9 us (26%)
  waiting for transfers between devices  14.6 us (19%)
  between operations  0.9 us (1%)
    all_to_all x1, blocking collectives, exchange(): return lax.all_to_all(x, AXES, split_axis=0, concat_axis=0, tiled=True)  19.9 us
    ppermute x9, waiting for transfers between devices, swaps(): lax.ppermute(piece(x, k), axis, [(i, i ^ k) for i in range(count)])  7.89 us
    ppermute x9, starting transfers between devices, swaps(): lax.ppermute(piece(x, k), axis, [(i, i ^ k) for i in range(count)])  7.61 us
    all_to_all x1, starting transfers between devices, exchange(): return lax.all_to_all(x, AXES, split_axis=0, concat_axis=0, tiled=True)  7.37 us
    ppermute x3, starting transfers between devices, rims(): lax.ppermute(first, RING, to_west)  5.18 us
    pallas_call x1, Pallas kernels, regrouped(): call(functools.partial(transport_solve_kernel, lat_count), [(4 * total, 2...  4.77 us
    pallas_call x2, Pallas kernels, pack(): pl.pallas_call(functools.partial(kernel, place), in_specs=[pl.BlockSpec(m...  4.59 us
    pallas_call x1, Pallas kernels, regrouped(): call(functools.partial(transport_pack_kernel, lat_count, n_lev), [(group,...  3.93 us
  transfers between devices with their start and end apart: 16, of which 6 were waited for; matrix products, arithmetic and copies ran while one was open for 1% of the time, Pallas kernels for 15%

profile of v8, /device:TPU:0, one launch (start us, length us, event | category | flops | bytes accessed | tf_op | source)
XLA Modules:
  0.0 76.8 jit_solution(5028136724756519417)
XLA Ops:
  0.6 3.0 %shard_map.104.refs_2_ = f32[16,72,128]{2,1,0:T(8,128)} custom-call(f32[4,34,4,256]{3,2,1,0:T(4,128)} %refs_0_.2, s32[2,4,256]{2,1,0:T(4,128)} %refs_1_.2, s32[1,1,512]{2,1,0:T(1,128)} %refs_2_.1, s32[1,512]{1,0:T(1,128)} %bitcast.31, s32[1,1,512]{2,1,0:T(1,128)} %refs_4_.1, f32[1,1,512]{2,1,0:T(1,128)} %refs_5_.1), custom_call_target="tpu_custom_call" | custom-call | tf_op jit(solution)/shard_map/pallas_call | solution.py:539
  3.7 7.4 %all-to-all-start = ((f32[16,72,128]{2,1,0:T(8,128)}), f32[16,72,128]{2,1,0:T(8,128)S(1)}, u32[]{:S(2)}, u32[]{:S(2)}) async-start(f32[16,72,128]{2,1,0:T(8,128)} %shard_map.104.refs_2_), calls=%async_computation | async-start | bytes 1179648 | tf_op jit(solution)/shard_map/all_to_all | solution.py:526
  11.1 1.6 %shard_map.106 = f32[16,40,128]{2,1,0:T(8,128)S(1)} custom-call(f32[34,4,256]{2,1,0:T(4,128)} %refs_0_.3, f32[34,4,256]{2,1,0:T(4,128)} %refs_1_.3, f32[16,72,128]{2,1,0:T(8,128)} %shard_map.104.refs_2_), custom_call_target="tpu_custom_call" | custom-call | tf_op jit(solution)/shard_map/pallas_call | solution.py:539
  12.7 1.7 %collective-permute-start.2 = (f32[136,128]{1,0:T(8,128)S(1)}, f32[136,128]{1,0:T(8,128)S(1)}, u32[]{:S(2)}, u32[]{:S(2)}) collective-permute-start(f32[136,128]{1,0:T(8,128)S(1)} %get-tuple-element.27), channel_id=1, source_target_pairs={{0,24},{8,16},{16,8},{24,0},{1,25},{9,17},{17,9},{25,1},{2,26},{10... | collective-permute-start | bytes 208904 | tf_op jit(solution)/shard_map/ppermute | solution.py:485
  14.8 4.3 %collective-permute-done.2 = f32[136,128]{1,0:T(8,128)S(1)} collective-permute-done((f32[136,128]{1,0:T(8,128)S(1)}, f32[136,128]{1,0:T(8,128)S(1)}, u32[]{:S(2)}, u32[]{:S(2)}) %collective-permute-start.2) | collective-permute-done | bytes 69664 | tf_op jit(solution)/shard_map/ppermute | solution.py:485
  19.1 3.5 %collective-permute-done.1 = f32[136,128]{1,0:T(8,128)S(1)} collective-permute-done((f32[136,128]{1,0:T(8,128)S(1)}, f32[136,128]{1,0:T(8,128)S(1)}, u32[]{:S(2)}, u32[]{:S(2)}) %collective-permute-start.1) | collective-permute-done | bytes 69664 | tf_op jit(solution)/shard_map/ppermute | solution.py:485
  23.0 4.1 %collective-permute-start.5 = (f32[136,128]{1,0:T(8,128)S(1)}, f32[136,128]{1,0:T(8,128)S(1)}, u32[]{:S(2)}, u32[]{:S(2)}) collective-permute-start(f32[136,128]{1,0:T(8,128)S(1)} %reshape.42), channel_id=1, source_target_pairs={{0,6},{2,4},{4,2},{6,0},{1,7},{3,5},{5,3},{7,1},{8,14},{10,12},{12... | collective-permute-start | bytes 208904 | tf_op jit(solution)/shard_map/ppermute | solution.py:485
  27.3 0.6 collective-permute-start.3
  27.9 3.2 %all-to-all-done.recv = f32[16,72,128]{2,1,0:T(8,128)S(1)} async-done(((f32[16,72,128]{2,1,0:T(8,128)}), f32[16,72,128]{2,1,0:T(8,128)S(1)}, u32[]{:S(2)}, u32[]{:S(2)}) %all-to-all-start) | async-done | bytes 589856 | tf_op jit(solution)/shard_map/all_to_all | solution.py:526
  31.1 1.6 %shard_map.105 = (f32[544,256]{1,0:T(8,128)S(1)}, f32[8,256]{1,0:T(8,128)S(1)}, f32[272,128]{1,0:T(8,128)S(1)}, f32[272,128]{1,0:T(8,128)S(1)}) custom-call(f32[16,72,128]{2,1,0:T(8,128)S(1)} %all-to-all-done.recv, f32[4,136,136]{2,1,0:T(8,128)S(1)} %copy-done), custom_call_target="tpu_custom_call" | custom-call | tf_op jit(solution)/shard_map/pallas_call | solution.py:559
  32.8 1.6 %collective-permute-start.8 = (f32[272,128]{1,0:T(8,128)S(1)}, f32[272,128]{1,0:T(8,128)S(1)}, u32[]{:S(2)}, u32[]{:S(2)}) collective-permute-start(f32[272,128]{1,0:T(8,128)S(1)} %get-tuple-element.17), channel_id=1, source_target_pairs={{0,1},{8,0},{2,8},{10,2},{4,10},{12,4},{6,12},{14,6},{22,14},{30,2... | collective-permute-start | bytes 417800 | tf_op jit(solution)/shard_map/ppermute | solution.py:529
  34.4 0.5 shard_map.107
  34.9 2.1 %collective-permute-start.6 = (f32[136,128]{1,0:T(8,128)S(1)}, f32[136,128]{1,0:T(8,128)S(1)}, u32[]{:S(2)}, u32[]{:S(2)}) collective-permute-start(f32[136,128]{1,0:T(8,128)S(1)} %get-tuple-element.15), channel_id=1, source_target_pairs={{0,1},{8,0},{2,8},{10,2},{4,10},{12,4},{6,12},{14,6},{22,14},{30,2... | collective-permute-start | bytes 208904 | tf_op jit(solution)/shard_map/ppermute | solution.py:529
  37.0 0.4 collective-permute-start.14
  37.4 0.4 shard_map.108.field
  37.8 1.1 %collective-permute-done.6.wind_east = f32[136,128]{1,0:T(8,128)S(1)} collective-permute-done((f32[136,128]{1,0:T(8,128)S(1)}, f32[136,128]{1,0:T(8,128)S(1)}, u32[]{:S(2)}, u32[]{:S(2)}) %collective-permute-start.6) | collective-permute-done | bytes 69664 | tf_op jit(solution)/shard_map/ppermute | solution.py:529
  39.2 2.1 %collective-permute-done.7.wind_west = f32[136,128]{1,0:T(8,128)S(1)} collective-permute-done((f32[136,128]{1,0:T(8,128)S(1)}, f32[136,128]{1,0:T(8,128)S(1)}, u32[]{:S(2)}, u32[]{:S(2)}) %collective-permute-start.7) | collective-permute-done | bytes 69664 | tf_op jit(solution)/shard_map/ppermute | solution.py:529
  41.3 4.8 %shard_map.109 = (f32[544,256]{1,0:T(8,128)S(1)}, f32[272,128]{1,0:T(8,128)S(1)}, f32[272,128]{1,0:T(8,128)S(1)}) custom-call(f32[544,256]{1,0:T(8,128)S(1)} %shard_map.108.field, f32[272,256]{1,0:T(8,128)S(1)} %get-tuple-element.14.winds, f32[8,256]{1,0:T(8,128)S(1)} %get-tuple-element.13.refs_4_.regimes, f32[4,136,136]{2,1,0:T(8,128)S(1)} %copy-done, ...), custom_call_target="tpu_custom_call" | custom-call | tf_op jit(solution)/shard_map/pallas_call | solution.py:576
  46.1 0.6 collective-permute-start.11
  46.6 1.5 %collective-permute-start.10 = (f32[272,128]{1,0:T(8,128)S(1)}, f32[272,128]{1,0:T(8,128)S(1)}, u32[]{:S(2)}, u32[]{:S(2)}) collective-permute-start(f32[272,128]{1,0:T(8,128)S(1)} %get-tuple-element.20._), channel_id=1, source_target_pairs={{0,1},{8,0},{2,8},{10,2},{4,10},{12,4},{6,12},{14,6},{22,14},{30,2... | collective-permute-start | bytes 417800 | tf_op jit(solution)/shard_map/ppermute | solution.py:529
  48.2 2.2 %shard_map.111.sums = f32[8,64]{1,0:T(8,128)S(1)} custom-call(f32[4,48,128]{2,1,0:T(8,128)S(1)} %pad_maximum_fusion.1.quarters, f32[544,256]{1,0:T(8,128)S(1)} %get-tuple-element.12.field.hour_0, f32[544,256]{1,0:T(8,128)S(1)} %get-tuple-element.19.hour_1.field), custom_call_target="tpu_custom_call" | custom-call | tf_op jit(solution)/shard_map/pallas_call | solution.py:582
  51.2 3.9 %shard_map.112 = f32[16,72,128]{2,1,0:T(8,128)S(1)} custom-call(f32[544,256]{1,0:T(8,128)S(1)} %get-tuple-element.19.hour_1.field, f32[6,136,384]{2,1,0:T(8,128)S(1)} %shard_map.110.faces, f32[272,128]{1,0:T(8,128)S(1)} %collective-permute-done.10.from_east, f32[272,128]{1,0:T(8,128)S(1)} %collective-permute-done.11.from_west, f32[8,64]{1,0:T(8,128)S(1)} %shard_map.111.sums), custom_call_target="tpu_custom_call" | custom-call | tf_op jit(solution)/shard_map/pallas_call | solution.py:588
  55.1 19.9 %all_to_all.10.recv = f32[16,72,128]{2,1,0:T(8,128)S(1)} all-to-all(f32[16,72,128]{2,1,0:T(8,128)S(1)} %shard_map.112), channel_id=1, replica_groups=mesh['lat'=4,'lev'=4,'lon'=2] {'lat','lev'}, dimensions={0} | all-to-all | bytes 1179648 | tf_op jit(solution)/shard_map/all_to_all | solution.py:526
  75.0 1.8 %shard_map.113 = (f32[4,34,4,256]{3,2,1,0:T(4,128)}, f32[2,4,1,4]{3,2,1,0:T(1,128)}) custom-call(f32[16,72,128]{2,1,0:T(8,128)S(1)} %all_to_all.10.recv), custom_call_target="tpu_custom_call" | custom-call | tf_op jit(solution)/shard_map/pallas_call | solution.py:593
  (37 shorter events, 2.0 us)
Async XLA Ops:
  3.7 27.5 %all-to-all-start = ((f32[16,72,128]{2,1,0:T(8,128)}), f32[16,72,128]{2,1,0:T(8,128)S(1)}, u32[]{:S(2)}, u32[]{:S(2)}) async-start(f32[16,72,128]{2,1,0:T(8,128)} %shard_map.104.refs_2_), calls=%async_computation | async-start | bytes 1179648 | tf_op jit(solution)/shard_map/all_to_all | solution.py:526
  12.7 18.4 %copy-start = (f32[4,136,136]{2,1,0:T(8,128)S(1)}, f32[4,136,136]{2,1,0:T(8,128)}, u32[]{:S(2)}) copy-start(f32[4,136,136]{2,1,0:T(8,128)} %kz.3) | copy-start | bytes 887812
  12.7 6.4 %collective-permute-start.2 = (f32[136,128]{1,0:T(8,128)S(1)}, f32[136,128]{1,0:T(8,128)S(1)}, u32[]{:S(2)}, u32[]{:S(2)}) collective-permute-start(f32[136,128]{1,0:T(8,128)S(1)} %get-tuple-element.27), channel_id=1, source_target_pairs={{0,24},{8,16},{16,8},{24,0},{1,25},{9,17},{17,9},{25,1},{2,26},{10... | collective-permute-start | bytes 208904 | tf_op jit(solution)/shard_map/ppermute | solution.py:485
  14.5 8.2 %collective-permute-start.1 = (f32[136,128]{1,0:T(8,128)S(1)}, f32[136,128]{1,0:T(8,128)S(1)}, u32[]{:S(2)}, u32[]{:S(2)}) collective-permute-start(f32[136,128]{1,0:T(8,128)S(1)} %get-tuple-element.28), channel_id=1, source_target_pairs={{0,16},{8,24},{16,0},{24,8},{1,17},{9,25},{17,1},{25,9},{2,18},{10... | collective-permute-start | bytes 208904 | tf_op jit(solution)/shard_map/ppermute | solution.py:485
  14.8 7.9 %collective-permute-start = (f32[136,128]{1,0:T(8,128)S(1)}, f32[136,128]{1,0:T(8,128)S(1)}, u32[]{:S(2)}, u32[]{:S(2)}) collective-permute-start(f32[136,128]{1,0:T(8,128)S(1)} %get-tuple-element.29), channel_id=1, source_target_pairs={{0,8},{8,0},{16,24},{24,16},{1,9},{9,1},{17,25},{25,17},{2,10},{10... | collective-permute-start | bytes 208904 | tf_op jit(solution)/shard_map/ppermute | solution.py:485
  23.0 11.4 %collective-permute-start.5 = (f32[136,128]{1,0:T(8,128)S(1)}, f32[136,128]{1,0:T(8,128)S(1)}, u32[]{:S(2)}, u32[]{:S(2)}) collective-permute-start(f32[136,128]{1,0:T(8,128)S(1)} %reshape.42), channel_id=1, source_target_pairs={{0,6},{2,4},{4,2},{6,0},{1,7},{3,5},{5,3},{7,1},{8,14},{10,12},{12... | collective-permute-start | bytes 208904 | tf_op jit(solution)/shard_map/ppermute | solution.py:485
  27.2 7.2 %collective-permute-start.4 = (f32[136,128]{1,0:T(8,128)S(1)}, f32[136,128]{1,0:T(8,128)S(1)}, u32[]{:S(2)}, u32[]{:S(2)}) collective-permute-start(f32[136,128]{1,0:T(8,128)S(1)} %reshape.41), channel_id=1, source_target_pairs={{0,4},{2,6},{4,0},{6,2},{1,5},{3,7},{5,1},{7,3},{8,12},{10,14},{12... | collective-permute-start | bytes 208904 | tf_op jit(solution)/shard_map/ppermute | solution.py:485
  27.3 7.1 %collective-permute-start.3 = (f32[136,128]{1,0:T(8,128)S(1)}, f32[136,128]{1,0:T(8,128)S(1)}, u32[]{:S(2)}, u32[]{:S(2)}) collective-permute-start(f32[136,128]{1,0:T(8,128)S(1)} %reshape.40), channel_id=1, source_target_pairs={{0,2},{2,0},{4,6},{6,4},{1,3},{3,1},{5,7},{7,5},{8,10},{10,8},{12,... | collective-permute-start | bytes 208904 | tf_op jit(solution)/shard_map/ppermute | solution.py:485
  32.8 8.5 %collective-permute-start.8 = (f32[272,128]{1,0:T(8,128)S(1)}, f32[272,128]{1,0:T(8,128)S(1)}, u32[]{:S(2)}, u32[]{:S(2)}) collective-permute-start(f32[272,128]{1,0:T(8,128)S(1)} %get-tuple-element.17), channel_id=1, source_target_pairs={{0,1},{8,0},{2,8},{10,2},{4,10},{12,4},{6,12},{14,6},{22,14},{30,2... | collective-permute-start | bytes 417800 | tf_op jit(solution)/shard_map/ppermute | solution.py:529
  34.4 6.9 %collective-permute-start.9 = (f32[272,128]{1,0:T(8,128)S(1)}, f32[272,128]{1,0:T(8,128)S(1)}, u32[]{:S(2)}, u32[]{:S(2)}) collective-permute-start(f32[272,128]{1,0:T(8,128)S(1)} %get-tuple-element.18), channel_id=1, source_target_pairs={{0,8},{8,2},{2,10},{10,4},{4,12},{12,6},{6,14},{14,22},{22,30},{30... | collective-permute-start | bytes 417800 | tf_op jit(solution)/shard_map/ppermute | solution.py:529
  34.9 4.0 %collective-permute-start.6 = (f32[136,128]{1,0:T(8,128)S(1)}, f32[136,128]{1,0:T(8,128)S(1)}, u32[]{:S(2)}, u32[]{:S(2)}) collective-permute-start(f32[136,128]{1,0:T(8,128)S(1)} %get-tuple-element.15), channel_id=1, source_target_pairs={{0,1},{8,0},{2,8},{10,2},{4,10},{12,4},{6,12},{14,6},{22,14},{30,2... | collective-permute-start | bytes 208904 | tf_op jit(solution)/shard_map/ppermute | solution.py:529
  37.0 4.3 %collective-permute-start.7 = (f32[136,128]{1,0:T(8,128)S(1)}, f32[136,128]{1,0:T(8,128)S(1)}, u32[]{:S(2)}, u32[]{:S(2)}) collective-permute-start(f32[136,128]{1,0:T(8,128)S(1)} %get-tuple-element.16), channel_id=1, source_target_pairs={{0,8},{8,2},{2,10},{10,4},{4,12},{12,6},{6,14},{14,22},{22,30},{30... | collective-permute-start | bytes 208904 | tf_op jit(solution)/shard_map/ppermute | solution.py:529
  37.0 11.2 %collective-permute-start.14 = (f32[48,128]{1,0:T(8,128)S(1)}, f32[48,128]{1,0:T(8,128)S(1)}, u32[]{:S(2)}, u32[]{:S(2)}) collective-permute-start(f32[48,128]{1,0:T(8,128)S(1)} %reshape.43), channel_id=1, source_target_pairs={{0,24},{8,16},{16,8},{24,0},{1,25},{9,17},{17,9},{25,1},{2,26},{10... | collective-permute-start | bytes 73736 | tf_op jit(solution)/shard_map/ppermute | solution.py:485
  38.9 9.3 %collective-permute-start.13 = (f32[48,128]{1,0:T(8,128)S(1)}, f32[48,128]{1,0:T(8,128)S(1)}, u32[]{:S(2)}, u32[]{:S(2)}) collective-permute-start(f32[48,128]{1,0:T(8,128)S(1)} %reshape.43), channel_id=1, source_target_pairs={{0,16},{8,24},{16,0},{24,8},{1,17},{9,25},{17,1},{25,9},{2,18},{10... | collective-permute-start | bytes 73736 | tf_op jit(solution)/shard_map/ppermute | solution.py:485
  41.3 6.9 %collective-permute-start.12 = (f32[48,128]{1,0:T(8,128)S(1)}, f32[48,128]{1,0:T(8,128)S(1)}, u32[]{:S(2)}, u32[]{:S(2)}) collective-permute-start(f32[48,128]{1,0:T(8,128)S(1)} %reshape.43), channel_id=1, source_target_pairs={{0,8},{8,0},{16,24},{24,16},{1,9},{9,1},{17,25},{25,17},{2,10},{10... | collective-permute-start | bytes 73736 | tf_op jit(solution)/shard_map/ppermute | solution.py:485
  46.1 5.1 %collective-permute-start.11 = (f32[272,128]{1,0:T(8,128)S(1)}, f32[272,128]{1,0:T(8,128)S(1)}, u32[]{:S(2)}, u32[]{:S(2)}) collective-permute-start(f32[272,128]{1,0:T(8,128)S(1)} %get-tuple-element.21), channel_id=1, source_target_pairs={{0,8},{8,2},{2,10},{10,4},{4,12},{12,6},{6,14},{14,22},{22,30},{30... | collective-permute-start | bytes 417800 | tf_op jit(solution)/shard_map/ppermute | solution.py:529
  46.6 4.6 %collective-permute-start.10 = (f32[272,128]{1,0:T(8,128)S(1)}, f32[272,128]{1,0:T(8,128)S(1)}, u32[]{:S(2)}, u32[]{:S(2)}) collective-permute-start(f32[272,128]{1,0:T(8,128)S(1)} %get-tuple-element.20._), channel_id=1, source_target_pairs={{0,1},{8,0},{2,8},{10,2},{4,10},{12,4},{6,12},{14,6},{22,14},{30,2... | collective-permute-start | bytes 417800 | tf_op jit(solution)/shard_map/ppermute | solution.py:529
